TPU v7x, 256 devices: a whole 4x4x8 slice. The times are simulated.
256 devices in a mesh: ctx: 16 (over x_lo, y, core), grp: 16 (over x_hi, z).
Axes of the slice: x: 4 (x_hi: 2, x_lo: 2; x = x_hi * 2 + x_lo), y: 4, z: 8, core: 2. Of those that a mesh axis runs over, the one named last changes fastest.
Arguments:
- queries: bfloat16 [1024, 12288], P(('ctx', 'grp')), may hold values from -240 to 240
- latents: bfloat16 [16384, 512], P(('ctx', 'grp')), may hold values from -6 to 6
- key_rope: bfloat16 [16384, 64], P(('ctx', 'grp')), may hold values from -4 to 4
- key_up: bfloat16 [64, 128, 512], P('grp'), may hold values from -0.5 to 0.5
- value_up: bfloat16 [64, 512, 128], P('grp'), may hold values from -0.25 to 0.25
- pattern: int32 [8, 128], replicated, may hold values 0 or 1
- stripe: int32 [128], replicated, may hold values from 0 to 127, each once
Outputs:
- attended: bfloat16 [1024, 8192], P(('ctx', 'grp'))
All inputs are finite; a program needn't handle non-finite values.
Results may differ from a plain program's by a relative error of at most 0.011.
Values may be sent and summed in bfloat16 or wider, within the bound.
No kernel may reach another device: no remote copies, remote signals or barrier semaphores. Data moves between devices by JAX's collectives and lax.ppermute only.
A program may use at most 128 MiB of HBM per device.

v0:
```python
import math

import jax
import jax.numpy as jnp
from jax import lax
from jax.sharding import PartitionSpec as P

L = 512
QN = 128
QR = 64
VD = 128
BLOCK = 128


def query_info(query_ids, pattern):
    span_blocks = pattern.shape[0]
    block_count = pattern.shape[1]
    span_block = query_ids // BLOCK
    position_block = (span_block + block_count - span_blocks).astype(jnp.float32)
    span_hot = (span_block[:, None] == jnp.arange(span_blocks)[None, :]).astype(jnp.float32)
    pattern_rows = jnp.dot(span_hot, pattern.astype(jnp.float32), precision=lax.Precision.HIGHEST)
    return (position_block, query_ids % BLOCK, pattern_rows)


def allowed_for(info, key_count, stripe):
    position_block, query_offset, pattern_rows = info
    block_count = stripe.shape[0]
    key_ids = jnp.arange(key_count, dtype=jnp.int32)
    key_hot = ((key_ids // BLOCK)[:, None] == jnp.arange(block_count)[None, :]).astype(jnp.float32)
    key_block = jnp.dot(key_hot, stripe.astype(jnp.float32), precision=lax.Precision.HIGHEST)
    key_offset = key_ids % BLOCK
    block_hot = (key_block[:, None] == jnp.arange(block_count)[None, :].astype(jnp.float32)).astype(
        jnp.float32
    )
    pattern_hit = jnp.dot(pattern_rows, block_hot.T, precision=lax.Precision.HIGHEST) > 0.5
    lower = position_block[:, None] > key_block[None, :]
    same_block = position_block[:, None] == key_block[None, :]
    return lower & pattern_hit | same_block & (key_offset[None, :] <= query_offset[:, None])


def compute(absorbed_part, rope_part, latent_piece, rope_piece, allowed, state):
    running_max, denominator, accumulated = state
    score_scale = 1.0 / math.sqrt(QN + QR)
    scores = jnp.einsum(
        "rhc,nc->rhn", absorbed_part, latent_piece, preferred_element_type=jnp.float32
    )
    scores = scores + jnp.einsum(
        "rhe,ne->rhn", rope_part, rope_piece, preferred_element_type=jnp.float32
    )
    scores = scores * score_scale
    mask_three = allowed[:, None, :]
    masked = jnp.where(mask_three, scores, -1e30)
    new_max = jnp.maximum(running_max, jnp.max(masked, axis=2))
    weights = jnp.where(mask_three, jnp.exp(scores - new_max[:, :, None]), 0.0)
    denominator = jnp.sum(weights, axis=2)
    update = jnp.einsum(
        "rhn,nc->rhc",
        weights.astype(jnp.bfloat16),
        latent_piece,
        preferred_element_type=jnp.float32,
    )
    accumulated = update
    return (new_max, denominator, accumulated)


def over_blocks(absorbed_part, rope_part, latent_piece, rope_piece, allowed, state):
    return compute(absorbed_part, rope_part, latent_piece, rope_piece, allowed, state)


def starting(row_count, head_count):
    return (
        jnp.full((row_count, head_count), -1e30, jnp.float32),
        jnp.zeros((row_count, head_count), jnp.float32),
        jnp.zeros((row_count, head_count, L), jnp.float32),
    )


def body(queries, latents, key_rope, key_up, value_up, pattern, stripe):
    gathered = lax.all_to_all(queries, "grp", split_axis=1, concat_axis=0, tiled=True)
    row_count = gathered.shape[0]
    head_count = key_up.shape[0]
    group_latent, group_rope = (
        lax.all_gather(latents, "grp", axis=0, tiled=True),
        lax.all_gather(key_rope, "grp", axis=0, tiled=True),
    )
    query_heads = gathered.reshape(row_count, head_count, QN + QR)
    absorbed = jnp.einsum(
        "rhd,hdc->rhc", query_heads[:, :, :QN], key_up, preferred_element_type=jnp.float32
    ).astype(jnp.bfloat16)
    query_rope = query_heads[:, :, QN:]
    own_ids = lax.axis_index("ctx") * row_count + jnp.arange(row_count, dtype=jnp.int32)
    own_info = query_info(own_ids, pattern)
    latent_piece = lax.all_gather(group_latent, "ctx", axis=0, tiled=True)
    rope_piece = lax.all_gather(group_rope, "ctx", axis=0, tiled=True)
    allowed = allowed_for(own_info, latent_piece.shape[0], stripe)
    final = over_blocks(
        absorbed, query_rope, latent_piece, rope_piece, allowed, starting(row_count, head_count)
    )
    running_max, denominator, accumulated = final
    mixed = (accumulated / denominator[:, :, None]).astype(jnp.bfloat16)
    head_out = jnp.einsum(
        "rhc,hcv->rhv", mixed, value_up, preferred_element_type=jnp.float32
    ).astype(jnp.bfloat16)
    head_out = head_out.reshape(row_count, head_count * VD)
    return lax.all_to_all(head_out, "grp", split_axis=0, concat_axis=1, tiled=True)


def solution(mesh):
    in_specs = (
        P(("ctx", "grp"), None),
        P(("ctx", "grp"), None),
        P(("ctx", "grp"), None),
        P("grp", None, None),
        P("grp", None, None),
        P(),
        P(),
    )
    out_specs = P(("ctx", "grp"), None)
    return jax.shard_map(body, mesh=mesh, in_specs=in_specs, out_specs=out_specs, check_vma=False)
```

profile of v0, /device:TPU:32, one launch (start us, length us, event | category | flops | bytes accessed | tf_op | source)
XLA Modules:
  0.0 286.6 jit_solution(803648787566525795)
XLA Ops:
  6.5 0.7 all-gather.4.cloned.1.call-update
  7.3 0.0 all-gather.6.cloned.1.call-start
  7.3 83.3 %all-gather.4.cloned.1.call-done = bf16[1024,512]{1,0:T(8,128)(2,1)} async-done(((bf16[64,512]{1,0:T(8,128)(2,1)}), bf16[1024,512]{1,0:T(8,128)(2,1)}) %all-gather.4.cloned.1.call-update) | async-done | bytes 1048592 | tf_op jit(solution)/shard_map/all_gather | solution.py:83
  90.6 0.0 all-gather.6.cloned.1.call-update
  90.6 5.4 %all-to-all-start = ((bf16[4,16,768]{2,0,1:T(4,128)(2,1)}), bf16[4,16,768]{2,0,1:T(4,128)(2,1)S(1)}, u32[]{:S(2)}, u32[]{:S(2)}) async-start(bf16[4,16,768]{2,0,1:T(4,128)(2,1)} %bitcast.35), calls=%async_computation | async-start | bytes 196608 | tf_op jit(solution)/shard_map/all_to_all | solution.py:79
  96.0 0.0 all-gather.8.cloned.1.call-start
  96.1 39.5 %all_gather.14 = bf16[1024,64]{1,0:T(8,128)(2,1)S(1)} all-gather(bf16[64,64]{1,0:T(8,128)(2,1)} %param.9), channel_id=1, replica_groups=mesh['ctx'=16,'grp'=16] {'grp'}, dimensions={0}, use_global_device_ids=true | all-gather | bytes 139264 | tf_op jit(solution)/shard_map/all_gather | solution.py:84
  135.6 0.8 copy.16
  136.3 0.0 all-gather.8.cloned.1.call-update
  136.4 0.9 fusion.41
  137.3 6.5 %fusion.14 = f32[1,16384]{1,0:T(1,128)S(1)} fusion(s32[16384]{0:T(1024)S(1)} %add_select_fusion, s32[128]{0:T(128)} %param.13), kind=kOutput, calls=%fused_computation.18 | convolution fusion | flops 27263104 | bytes 131584 | tf_op jit(solution)/shard_map/dot_general | solution.py:30
  143.8 6.9 %fusion.2 = pred[64,16384]{1,0:T(8,128)(4,1)S(1)} fusion(f32[64,128]{1,0:T(8,128)S(1)} %fusion.41, f32[128]{0:T(128)S(1)} %iota_convert_fusion, f32[16384]{0:T(1024)S(1)} %bitcast.36, s32[16384]{0:T(1024)S(1)} %fusion.31, s32[64]{0:T(128)S(1)} %get-tuple-element.7, f32[64]{0:T(128)S(1)} %get-tuple-element.8), kind=kOutput, calls=%fused_computation.4 | convolution fusion | flops 1620049920 | bytes 1213440 | tf_op jit(solution)/shard_map/dot_general | solution.py:35
  150.7 0.0 all-to-all-done
  150.8 0.1 reshape.82
  151.0 33.0 %all-gather.6.cloned.1.call-done = bf16[16384,512]{1,0:T(8,128)(2,1)} async-done(((bf16[1024,512]{1,0:T(8,128)(2,1)}), bf16[16384,512]{1,0:T(8,128)(2,1)}) %all-gather.6.cloned.1.call-update) | async-done | bytes 16777232 | tf_op jit(solution)/shard_map/all_gather | solution.py:93
  184.0 11.6 %fusion.5 = f32[64,4,16384]{2,0,1:T(8,128)} fusion(bf16[16384,512]{1,0:T(8,128)(2,1)} %all-gather.6.cloned.1.call-done, bf16[4,128,512]{2,1,0:T(8,128)(2,1)S(1)} %copy-done, bf16[64,4,128]{2,1,0:T(4,128)(2,1)S(1)} %slice.8), kind=kOutput, calls=%fused_computation.7 | convolution fusion | flops 4328652800 | bytes 34144256 | tf_op jit(solution)/shard_map/rhc,nc->rhn/dot_general | solution.py:44
  195.6 27.6 %all-gather.8.cloned.1.call-done = bf16[16384,64]{0,1:T(8,128)(2,1)} async-done(((bf16[1024,64]{0,1:T(8,128)(2,1)}), bf16[16384,64]{0,1:T(8,128)(2,1)}) %all-gather.8.cloned.1.call-update) | async-done | bytes 2097168 | tf_op jit(solution)/shard_map/all_gather | solution.py:94
  223.3 12.5 %select_reduce_fusion = (f32[64,4]{0,1:T(4,128)S(1)}, f32[64,4,16384]{2,0,1:T(8,128)}) fusion(pred[64,16384]{1,0:T(8,128)(4,1)S(1)} %fusion.2, f32[64,4,16384]{2,0,1:T(8,128)} %fusion.5, bf16[16384,64]{0,1:T(8,128)(2,1)} %all-gather.8.cloned.1.call-done, bf16[64,4,64]{2,1,0:T(4,128)(2,1)S(1)} %slice.9), kind=kOutput, calls=%fused_computation.10 | convolution fusion | flops 553647872 | bytes 36733952 | tf_op jit(solution)/shard_map/rhe,ne->rhn/dot_general | solution.py:47
  235.7 9.8 %fusion.7 = f32[64,4]{0,1:T(4,128)S(1)} fusion(f32[64,4,16384]{2,0,1:T(8,128)} %get-tuple-element.6, f32[64,4]{0,1:T(4,128)S(1)} %broadcast_maximum_fusion, pred[64,16384]{1,0:T(8,128)(4,1)S(1)} %fusion.2), kind=kLoop, calls=%fused_computation.11 | loop fusion | flops 12582656 | bytes 17827840 | tf_op jit(solution)/shard_map/reduce_sum | solution.py:55
  245.5 15.1 %fusion.26 = bf16[64,4,512]{2,0,1:T(8,128)(2,1)S(1)} fusion(bf16[16384,512]{1,0:T(8,128)(2,1)} %all-gather.6.cloned.1.call-done, f32[64,4,16384]{2,0,1:T(8,128)} %get-tuple-element.6, f32[64,4]{0,1:T(4,128)S(1)} %broadcast_maximum_fusion, pred[64,16384]{1,0:T(8,128)(4,1)S(1)} %fusion.2, f32[64,4]{0,1:T(4,128)S(1)} %fusion.7), kind=kOutput, calls=%fused_computation.28 | convolution fusion | flops 4307812352 | bytes 34867200 | tf_op jit(solution)/shard_map/rhn,nc->rhc/dot_general | solution.py:56
  260.7 0.2 fusion.20
  260.9 0.1 copy.17
  261.0 18.5 %all_to_all.35 = bf16[16,4,512]{2,1,0:T(4,128)(2,1)S(1)} all-to-all(bf16[16,4,512]{2,1,0:T(4,128)(2,1)S(1)} %all_to_all.29), channel_id=1, replica_groups=mesh['ctx'=16,'grp'=16] {'grp'}, dimensions={0} | all-to-all | bytes 131072 | tf_op jit(solution)/shard_map/all_to_all | solution.py:105
  279.5 0.6 copy.28
  (14 shorter events, 0.2 us)
Async XLA Ops:
  6.5 177.5 %copy-start = (bf16[4,128,512]{2,1,0:T(8,128)(2,1)S(1)}, bf16[4,128,512]{2,1,0:T(8,128)(2,1)}, u32[]{:S(2)}) copy-start(bf16[4,128,512]{2,1,0:T(8,128)(2,1)} %param.10) | copy-start | bytes 1572868
  6.5 84.0 %all-gather.4.cloned.1.call-start = ((), (), s32[]{:S(2)}) async-start(), calls=%async_computation.2 | async-start | bytes 1114112 | tf_op jit(solution)/shard_map/all_gather | solution.py:83
  7.3 176.7 %all-gather.6.cloned.1.call-start = ((), (), s32[]{:S(2)}) async-start(), calls=%async_computation.3 | async-start | bytes 17825792 | tf_op jit(solution)/shard_map/all_gather | solution.py:93
  90.6 60.1 %all-to-all-start = ((bf16[4,16,768]{2,0,1:T(4,128)(2,1)}), bf16[4,16,768]{2,0,1:T(4,128)(2,1)S(1)}, u32[]{:S(2)}, u32[]{:S(2)}) async-start(bf16[4,16,768]{2,0,1:T(4,128)(2,1)} %bitcast.35), calls=%async_computation | async-start | bytes 196608 | tf_op jit(solution)/shard_map/all_to_all | solution.py:79
  96.0 127.3 %all-gather.8.cloned.1.call-start = ((), (), s32[]{:S(2)}) async-start(), calls=%async_computation.4 | async-start | bytes 2228224 | tf_op jit(solution)/shard_map/all_gather | solution.py:94
  245.5 15.1 %copy-start.1 = (bf16[4,512,128]{2,1,0:T(8,128)(2,1)S(1)}, bf16[4,512,128]{2,1,0:T(8,128)(2,1)}, u32[]{:S(2)}) copy-start(bf16[4,512,128]{2,1,0:T(8,128)(2,1)} %param.11) | copy-start | bytes 1572868
Sparse Core Ops, SparseCore 0:
  9.9 80.5 all-gather.3
  92.4 91.5 all-gather.5
  185.8 37.4 all-gather.7
where the time goes:
time: 288 us; the launch traced here: 287 us
  waiting for transfers between devices  145 us (50%)
  blocking collectives  58 us (20%)
  matrix products  53.7 us (19%)
  between operations  13.2 us (5%)
  other arithmetic  9.82 us (3%)
  starting transfers between devices  5.49 us (2%)
    all_gather x1, waiting for transfers between devices, body(): lax.all_gather(latents, 'grp', axis=0, tiled=True)  83.3 us
    all_gather x1, blocking collectives, body(): lax.all_gather(key_rope, 'grp', axis=0, tiled=True)  39.5 us
    all_gather x1, waiting for transfers between devices, body(): latent_piece = lax.all_gather(group_latent, 'ctx', axis=0, tiled=True)  33 us
    all_gather x1, waiting for transfers between devices, body(): rope_piece = lax.all_gather(group_rope, 'ctx', axis=0, tiled=True)  27.6 us
    all_to_all x1, blocking collectives, body(): lax.all_to_all(head_out, 'grp', split_axis=0, concat_axis=1, tiled=True)  18.5 us
    dot_general x1, matrix products, compute(): jnp.einsum('rhn,nc->rhc', weights.astype(jnp.bfloat16), latent_piece, pre...  15.1 us
    dot_general x1, matrix products, compute(): jnp.einsum('rhe,ne->rhn', rope_part, rope_piece, preferred_element_type=j...  12.5 us
    dot_general x1, matrix products, compute(): jnp.einsum('rhc,nc->rhn', absorbed_part, latent_piece, preferred_element_...  11.6 us
  transfers between devices with their start and end apart: 4, of which 3 were waited for; matrix products, arithmetic and copies ran while one was open for 9% of the time, Pallas kernels for 0%

commit v1 on v0

v1 whole, which is shorter than its diff:
```python
import functools
import math

import jax
import jax.numpy as jnp
from jax import lax
from jax.experimental import pallas as pl
from jax.experimental.pallas import tpu as pltpu
from jax.sharding import Mesh
from jax.sharding import PartitionSpec as P

L = 512
QN = 128
QR = 64
QD = QN + QR
VD = 128
BLOCK = 128
HEADS = 4
NEG = -1e30
SCALE = 1.0 / math.sqrt(QD)
LOG2E = math.log2(math.e)

AXES = ("xl", "y", "core", "xh", "z")
CHIPS = ("xl", "y", "xh", "z")
XLN, YN, CN, XHN, ZN = 2, 4, 2, 2, 8
CELLS = XLN * YN
GRP = XHN * ZN
PER = 64
TOK = 4
ROWS = CELLS * GRP * TOK
SLOTS = 2 * CN * ZN
KEYS = SLOTS * PER
EXT = HEADS * VD + 128

QT = 256
KT = 512


def attend_kernel(q_ref, lat_ref, rope_ref, w_ref, thr_ref, off_ref, o_ref, kcat, vals, sco, stats):
    h = pl.program_id(0)
    for i in range(KEYS // KT):
        rows = pl.ds(i * KT, KT)
        kv = jnp.dot(lat_ref[rows, :], w_ref[0], preferred_element_type=jnp.float32)
        kv = kv.astype(jnp.bfloat16)
        kcat[rows, 0:QN] = kv[:, 0:QN]
        vals[rows, :] = kv[:, QN:]

    @pl.when(h == 0)
    def _():
        kcat[:, QN:QD] = rope_ref[...]
        stats[...] = jnp.zeros_like(stats)

    lane = lax.broadcasted_iota(jnp.int32, (QT, 128), 1)
    off = off_ref[...]
    for t in range(ROWS // QT):
        q = q_ref[0, pl.ds(t * QT, QT), :]
        top = jnp.full((QT, 128), NEG, jnp.float32)
        for i in range(KEYS // KT):
            rows = pl.ds(i * KT, KT)
            s = lax.dot_general(
                q, kcat[rows, 0:QD], (((1,), (1,)), ((), ())), preferred_element_type=jnp.float32
            )
            parts = []
            for b in range(QT // 64):
                thr = thr_ref[pl.ds(t * (QT // 64) + b, 1), rows]
                cols = []
                for c in range(KT // 128):
                    piece = s[b * 64 : (b + 1) * 64, c * 128 : (c + 1) * 128]
                    cols.append(jnp.where(off >= thr[:, c * 128 : (c + 1) * 128], piece, NEG))
                best = functools.reduce(jnp.maximum, cols)
                parts.append(best)
                for c in range(KT // 128):
                    sco[b * 64 : (b + 1) * 64, i * KT + c * 128 : i * KT + (c + 1) * 128] = cols[c]
            top = jnp.maximum(top, jnp.concatenate(parts, axis=0))
        m = jnp.max(top, axis=1, keepdims=True)
        mc = m * (SCALE * LOG2E)
        total = jnp.zeros((QT, 128), jnp.float32)
        acc = jnp.zeros((QT, VD), jnp.float32)
        for i in range(KEYS // KT):
            p = jnp.exp2(sco[:, pl.ds(i * KT, KT)] * (SCALE * LOG2E) - mc)
            for c in range(KT // 128):
                total = total + p[:, c * 128 : (c + 1) * 128]
            acc = acc + jnp.dot(
                p.astype(jnp.bfloat16),
                vals[pl.ds(i * KT, KT), :],
                preferred_element_type=jnp.float32,
            )
        den = jnp.sum(total, axis=1, keepdims=True)
        lse = m * SCALE + jnp.log(den)
        o_ref[pl.ds(t * QT, QT), pl.ds(pl.multiple_of(h * VD, VD), VD)] = (acc / den).astype(
            jnp.bfloat16
        )
        hi = lse.astype(jnp.bfloat16).astype(jnp.float32)
        mid = (lse - hi).astype(jnp.bfloat16).astype(jnp.float32)
        low = lse - hi - mid
        old = stats[pl.ds(t * QT, QT), :]
        old = jnp.where(lane == 3 * h, hi, old)
        old = jnp.where(lane == 3 * h + 1, mid, old)
        stats[pl.ds(t * QT, QT), :] = jnp.where(lane == 3 * h + 2, low, old)

    @pl.when(h == HEADS - 1)
    def _():
        o_ref[:, HEADS * VD :] = stats[...].astype(jnp.bfloat16)


def attend(q, lat, rope, weights, thr, off):
    full = lambda shape: pl.BlockSpec(shape, lambda h: tuple(0 for _ in shape))
    return pl.pallas_call(
        attend_kernel,
        grid=(HEADS,),
        out_shape=jax.ShapeDtypeStruct((ROWS, EXT), jnp.bfloat16),
        in_specs=[
            pl.BlockSpec((1, ROWS, QD), lambda h: (h, 0, 0)),
            full((KEYS, L)),
            full((KEYS, QR)),
            pl.BlockSpec((1, L, QN + VD), lambda h: (h, 0, 0)),
            full((CELLS, KEYS)),
            full((64, 128)),
        ],
        out_specs=full((ROWS, EXT)),
        scratch_shapes=[
            pltpu.VMEM((KEYS, QN + 128), jnp.bfloat16),
            pltpu.VMEM((KEYS, VD), jnp.bfloat16),
            pltpu.VMEM((QT, KEYS), jnp.float32),
            pltpu.VMEM((ROWS, 128), jnp.float32),
        ],
        compiler_params=pltpu.CompilerParams(vmem_limit_bytes=40 * 1024 * 1024),
        cost_estimate=pl.CostEstimate(
            flops=6_500_000_000, bytes_accessed=6_000_000, transcendentals=4_200_000
        ),
        name="attend",
    )(q, lat, rope, weights, thr, off)


def combine_kernel(x_ref, o_ref):
    n = GRP * TOK
    ext = [x_ref[pl.ds(c * n, n), pl.ds(HEADS * VD, 128)].astype(jnp.float32) for c in range(CELLS)]
    for h in range(HEADS):
        lse = [
            e[:, 3 * h : 3 * h + 1] + e[:, 3 * h + 1 : 3 * h + 2] + e[:, 3 * h + 2 : 3 * h + 3]
            for e in ext
        ]
        top = functools.reduce(jnp.maximum, lse)
        part = [jnp.exp(v - top) for v in lse]
        scale = 1.0 / functools.reduce(jnp.add, part)
        acc = jnp.zeros((n, VD), jnp.float32)
        for c in range(CELLS):
            acc = acc + x_ref[pl.ds(c * n, n), pl.ds(h * VD, VD)].astype(jnp.float32) * (
                part[c] * scale
            )
        o_ref[:, pl.ds(h * VD, VD)] = acc.astype(jnp.bfloat16)


def combine(x):
    return pl.pallas_call(
        combine_kernel,
        out_shape=jax.ShapeDtypeStruct((GRP * TOK, HEADS * VD), jnp.bfloat16),
        name="combine",
    )(x)


def shift(n, k):
    return [(i, (i + k) % n) for i in range(n)]


def gather_keys(piece):
    xn = [(a * 2 + b, (1 - a) * 2 + 1 - b) for a in range(2) for b in range(2)]
    other = lax.ppermute(piece, ("xl", "xh"), xn)
    own = jnp.stack([piece, other])
    up = down = own
    chunks = [own]
    for _ in range(3):
        up = lax.ppermute(up, "z", shift(ZN, 1))
        down = lax.ppermute(down, "z", shift(ZN, -1))
        chunks += [up, down]
    last = [lax.ppermute(up[0], "z", shift(ZN, 1)), lax.ppermute(down[1], "z", shift(ZN, -1))]
    chunks.append(jnp.stack(last))
    mine = jnp.stack(chunks)
    theirs = lax.ppermute(mine, "core", shift(CN, 1))
    return jnp.concatenate([mine, theirs]).reshape(KEYS, mine.shape[-1])


def thresholds(pattern, stripe):
    xl, y, core = lax.axis_index("xl"), lax.axis_index("y"), lax.axis_index("core")
    xh, z = lax.axis_index("xh"), lax.axis_index("z")
    ids = jnp.arange(SLOTS, dtype=jnp.int32)
    swap = ids % 2
    step = (ids // 2) % ZN
    k = core ^ (ids // (2 * ZN))
    back = jnp.where(step % 2 == 1, -((step + 1) // 2), step // 2)
    zz = (z + back) % ZN
    cell = ((xl ^ swap) * YN + y) * CN + k
    grp = (xh ^ swap) * ZN + zz
    place = cell * GRP + grp
    block = place * PER // BLOCK
    base = place * PER % BLOCK
    nb = stripe.shape[0]
    every = jnp.arange(nb, dtype=jnp.int32)
    kb = jnp.sum(jnp.where(block[:, None] == every[None, :], stripe[None, :], 0), axis=1)
    hit = jnp.sum(jnp.where(kb[None, :, None] == every[None, None, :], pattern[:, None, :], 0), axis=2)
    qb = nb - CELLS + jnp.arange(CELLS, dtype=jnp.int32)[:, None]
    see = (kb[None, :] < qb) & (hit == 1)
    offset = base[:, None] + jnp.arange(PER, dtype=jnp.int32)[None, :]
    thr = jnp.where(
        see[:, :, None], 0, jnp.where((kb[None, :] == qb)[:, :, None], offset[None], 4 * BLOCK)
    )
    return thr.reshape(CELLS, KEYS).astype(jnp.float32)


def body(queries, latents, key_rope, key_up, value_up, pattern, stripe):
    keys = gather_keys(jnp.concatenate([latents, key_rope], axis=1))
    send = queries.reshape(TOK, GRP, HEADS * QD).transpose(1, 0, 2)
    send = jnp.broadcast_to(send[None], (CELLS, GRP, TOK, HEADS * QD))
    send = send.reshape(CELLS * GRP, TOK, HEADS * QD)
    got = lax.all_to_all(send, CHIPS, split_axis=0, concat_axis=0, tiled=True)
    q = got.reshape(ROWS, HEADS, QD).transpose(1, 0, 2)
    weights = jnp.concatenate([key_up.transpose(0, 2, 1), value_up], axis=2)
    thr = thresholds(pattern, stripe)
    off = (lax.axis_index("core") * 64 + jnp.arange(64, dtype=jnp.int32)).astype(jnp.float32)
    off = jnp.broadcast_to(off[:, None], (64, 128))
    part = attend(q, keys[:, :L], keys[:, L:], weights, thr, off)
    back = lax.all_to_all(
        part.reshape(CELLS * GRP, TOK, EXT), CHIPS, split_axis=0, concat_axis=0, tiled=True
    )
    out = combine(back.reshape(CELLS * GRP * TOK, EXT))
    return out.reshape(GRP, TOK, HEADS * VD).transpose(1, 0, 2).reshape(TOK, GRP * HEADS * VD)


def solution(mesh):
    fine = Mesh(mesh.devices.reshape(XLN, YN, CN, XHN, ZN), AXES)
    in_specs = (
        P(AXES, None),
        P(AXES, None),
        P(AXES, None),
        P(("xh", "z"), None, None),
        P(("xh", "z"), None, None),
        P(),
        P(),
    )
    return jax.shard_map(body, mesh=fine, in_specs=in_specs, out_specs=P(AXES, None), check_vma=False)
```

time: 288 us -> 124 us (0.43)
  waiting for transfers between devices: 145 us -> 21.3 us
  matrix products: 53.7 us -> 0 us
  starting transfers between devices: 5.49 us -> 26.8 us
  blocking collectives: 58 us -> 38.5 us
  local copies, waits for them, and re-layouts: 1.68 us -> 20.1 us
  Pallas kernels: 0 us -> 13.5 us
  between operations: 13.2 us -> 0.24 us
  other arithmetic: 9.82 us -> 2.27 us
    all_gather x3 -> x0, waiting for transfers between devices: 144 us -> none  [the longest x1 83.3 us: body(): lax.all_gather(latents, 'grp', axis=0, tiled=True)]
    dot_general x7 -> x0, matrix products: 53.7 us -> none  [the longest x1 15.1 us: compute(): jnp.einsum('rhn,nc->rhc', weights.astype(jnp.bfloat16), latent_piece, pre...]
    all_gather x1 -> x0, blocking collectives: 39.5 us -> none  [body(): lax.all_gather(key_rope, 'grp', axis=0, tiled=True)]
    ppermute x0 -> x10, waiting for transfers between devices: none -> 21.3 us  [the longest x3 20.5 us: gather_keys(): up = lax.ppermute(up, 'z', shift(ZN, 1))]
    all_to_all x1, blocking collectives: 18.5 us -> 38.5 us  [body(): lax.all_to_all(part.reshape(CELLS * GRP, TOK, EXT), CHIPS, split_axis=0,...]
    ppermute x0 -> x10, starting transfers between devices: none -> 13.6 us  [the longest x3 4.17 us: gather_keys(): down = lax.ppermute(down, 'z', shift(ZN, -1))]
    pallas_call x0 -> x2, Pallas kernels: none -> 13.5 us  [the longest x1 11.2 us: attend(): pl.pallas_call(attend_kernel, grid=(HEADS,), out_shape=jax.ShapeDtypeStru...]
    reduce_sum x1 -> x2, other arithmetic: 9.76 us -> 0.38 us  [the longest x1 0.21 us: thresholds(): jnp.sum(jnp.where(kb[None, :, None] == every[None, None, :], pattern[:, N...]
  transfers between devices with their start and end apart: 4 -> 11, of which waited for: 3 -> 4; matrix products, arithmetic and copies ran while one was open for 9% -> 10% of each run, Pallas kernels for 0% -> 0%
where the time goes in v1:
time: 124 us; the launch traced here: 123 us
  blocking collectives  38.5 us (31%)
  starting transfers between devices  26.8 us (22%)
  waiting for transfers between devices  21.3 us (17%)
  local copies, waits for them, and re-layouts  20.1 us (16%)
  Pallas kernels  13.5 us (11%)
  other arithmetic  2.27 us (2%)
    all_to_all x1, blocking collectives, body(): lax.all_to_all(part.reshape(CELLS * GRP, TOK, EXT), CHIPS, split_axis=0,...  38.5 us
    ppermute x3, waiting for transfers between devices, gather_keys(): up = lax.ppermute(up, 'z', shift(ZN, 1))  20.5 us
    all_to_all x1, starting transfers between devices, body(): got = lax.all_to_all(send, CHIPS, split_axis=0, concat_axis=0, tiled=True)  13.2 us
    pallas_call x1, Pallas kernels, attend(): pl.pallas_call(attend_kernel, grid=(HEADS,), out_shape=jax.ShapeDtypeStru...  11.2 us
    unnamed x17, local copies, waits for them, and re-layouts  6.59 us
    ppermute x3, starting transfers between devices, gather_keys(): down = lax.ppermute(down, 'z', shift(ZN, -1))  4.17 us
    ppermute x1, starting transfers between devices, gather_keys(): lax.ppermute(down[1], 'z', shift(ZN, -1))  3.31 us
    ppermute x3, starting transfers between devices, gather_keys(): up = lax.ppermute(up, 'z', shift(ZN, 1))  3.28 us
  transfers between devices with their start and end apart: 11, of which 4 were waited for; matrix products, arithmetic and copies ran while one was open for 10% of the time, Pallas kernels for 0%

profile of v1, /device:TPU:32, one launch (start us, length us, event | category | flops | bytes accessed | tf_op | source)
XLA Modules:
  0.0 122.6 jit_solution(3028450411130374403)
XLA Ops:
  0.0 0.9 constant_dynamic-update-slice_fusion.1
  1.6 2.8 %collective-permute-start = (bf16[64,576]{1,0:T(8,128)(2,1)S(1)}, bf16[64,576]{1,0:T(8,128)(2,1)S(1)}, u32[]{:S(2)}, u32[]{:S(2)}) collective-permute-start(bf16[64,576]{1,0:T(8,128)(2,1)S(1)} %constant_dynamic-update-slice_fusion), channel_id=1, source_target_pairs={{0,136},{8,128},{128,8},{136,0},{1,137},{9,129},{129,9},{137,1},{2... | collective-permute-start | bytes 221192 | tf_op jit(solution)/shard_map/ppermute | solution.py:168
  4.3 0.9 copy.23
  5.3 1.1 broadcast_in_dim.94
  6.4 13.2 %all-to-all-start = ((bf16[128,4,768]{2,1,0:T(4,128)(2,1)}), bf16[128,4,768]{2,1,0:T(4,128)(2,1)}, u32[]{:S(2)}, u32[]{:S(2)}) async-start(bf16[128,4,768]{2,1,0:T(4,128)(2,1)} %bitcast.1), calls=%async_computation | async-start | bytes 1572864 | tf_op jit(solution)/shard_map/all_to_all | solution.py:215
  19.9 1.5 %collective-permute-start.1 = (bf16[2,64,576]{2,1,0:T(8,128)(2,1)S(1)}, bf16[2,64,576]{2,1,0:T(8,128)(2,1)S(1)}, u32[]{:S(2)}, u32[]{:S(2)}) collective-permute-start(bf16[2,64,576]{2,1,0:T(8,128)(2,1)S(1)} %pad_maximum_fusion.1), channel_id=1, source_target_pairs={{0,1},{1,2},{2,3},{3,4},{4,5},{5,6},{6,7},{7,0},{8,9},{9,10},{10,1... | collective-permute-start | bytes 442376 | tf_op jit(solution)/shard_map/ppermute | solution.py:173
  22.8 17.0 %collective-permute-done.1 = bf16[2,64,576]{2,1,0:T(8,128)(2,1)S(1)} collective-permute-done((bf16[2,64,576]{2,1,0:T(8,128)(2,1)S(1)}, bf16[2,64,576]{2,1,0:T(8,128)(2,1)S(1)}, u32[]{:S(2)}, u32[]{:S(2)}) %collective-permute-start.1) | collective-permute-done | bytes 147488 | tf_op jit(solution)/shard_map/ppermute | solution.py:173
  39.8 0.9 collective-permute-start.3
  40.7 1.2 collective-permute-start.4
  43.4 1.8 %collective-permute-done.3 = bf16[2,64,576]{2,1,0:T(8,128)(2,1)S(1)} collective-permute-done((bf16[2,64,576]{2,1,0:T(8,128)(2,1)S(1)}, bf16[2,64,576]{2,1,0:T(8,128)(2,1)S(1)}, u32[]{:S(2)}, u32[]{:S(2)}) %collective-permute-start.3) | collective-permute-done | bytes 147488 | tf_op jit(solution)/shard_map/ppermute | solution.py:173
  45.2 0.8 collective-permute-start.5
  46.1 2.4 %collective-permute-start.6 = (bf16[2,64,576]{2,1,0:T(8,128)(2,1)S(1)}, bf16[2,64,576]{2,1,0:T(8,128)(2,1)S(1)}, u32[]{:S(2)}, u32[]{:S(2)}) collective-permute-start(bf16[2,64,576]{2,1,0:T(8,128)(2,1)S(1)} %collective-permute-done.4), channel_id=1, source_target_pairs={{0,7},{1,0},{2,1},{3,2},{4,3},{5,4},{6,5},{7,6},{8,15},{9,8},{10,9... | collective-permute-start | bytes 442376 | tf_op jit(solution)/shard_map/ppermute | solution.py:174
  50.0 1.8 %collective-permute-done.5 = bf16[2,64,576]{2,1,0:T(8,128)(2,1)S(1)} collective-permute-done((bf16[2,64,576]{2,1,0:T(8,128)(2,1)S(1)}, bf16[2,64,576]{2,1,0:T(8,128)(2,1)S(1)}, u32[]{:S(2)}, u32[]{:S(2)}) %collective-permute-start.5) | collective-permute-done | bytes 147488 | tf_op jit(solution)/shard_map/ppermute | solution.py:173
  51.9 3.3 %collective-permute-start.8 = (bf16[64,576]{1,0:T(8,128)(2,1)S(1)}, bf16[64,576]{1,0:T(8,128)(2,1)S(1)}, u32[]{:S(2)}, u32[]{:S(2)}) collective-permute-start(bf16[64,576]{1,0:T(8,128)(2,1)S(1)} %slice_bitcast_fusion), channel_id=1, source_target_pairs={{0,7},{1,0},{2,1},{3,2},{4,3},{5,4},{6,5},{7,6},{8,15},{9,8},{10,9... | collective-permute-start | bytes 221192 | tf_op jit(solution)/shard_map/ppermute | solution.py:176
  56.7 0.8 collective-permute-done.7
  59.8 2.7 %reshape.274 = bf16[512,4,192]{2,1,0:T(4,128)(2,1)S(1)} reshape(bf16[128,4,768]{2,1,0:T(4,128)(2,1)} %all-to-all-done) | data formatting | bytes 1572864 | tf_op jit(solution)/shard_map/reshape | solution.py:216
  62.6 2.5 %constant_dynamic-update-slice_fusion.2 = bf16[16,2,64,576]{3,2,1,0:T(8,128)(2,1)} fusion(bf16[16,2,64,576]{3,2,1,0:T(8,128)(2,1)} %get-tuple-element.8, bf16[8,2,64,576]{3,2,1,0:T(8,128)(2,1)} %collective-permute-done.9), kind=kLoop, calls=%fused_computation.27 | loop fusion | bytes 2621440 | tf_op jit(solution)/shard_map/concatenate | solution.py:180
  65.2 1.7 %slice.18.lat_ref = bf16[2048,512]{1,0:T(8,128)(2,1)S(1)} slice(bf16[2048,576]{1,0:T(8,128)(2,1)} %bitcast.17), slice={[0:2048], [0:512]} | slice | bytes 4194304 | tf_op jit(solution)/shard_map/slice | solution.py:221
  66.9 1.1 slice.19.rope_ref
  68.0 11.2 %attend.1 = bf16[512,640]{1,0:T(8,128)(2,1)S(1)} custom-call(bf16[4,512,192]{2,1,0:T(8,128)(2,1)S(1)} %bitcast.51, bf16[2048,512]{1,0:T(8,128)(2,1)S(1)} %slice.18.lat_ref, bf16[2048,64]{1,0:T(8,128)(2,1)S(1)} %slice.19.rope_ref, bf16[4,512,256]{2,1,0:T(8,128)(2,1)S(1)} %pad_maximum_fusion.w_ref, f32[8,2048]{1,0:T(8,128)S(1)} %select_convert_fusion.thr_ref, ...), custom_call_target="tpu_custom_call" | custom-call | flops 6499999744 | bytes 6000000 | tf_op jit(solution)/shard_map/attend/pallas_call | solution.py:108
  79.4 38.5 %all_to_all.10 = bf16[128,4,640]{2,1,0:T(4,128)(2,1)S(1)} all-to-all(bf16[128,4,640]{2,1,0:T(4,128)(2,1)S(1)} %reshape.276), channel_id=1, replica_groups=mesh['xl'=2,'y'=4,'core'=2,'xh'=2,'z'=8] {'xl','y','xh','z'}, dimensions={0} | all-to-all | bytes 1310720 | tf_op jit(solution)/shard_map/all_to_all | solution.py:222
  117.9 1.0 reshape.277.x_ref
  118.9 2.3 %combine.1 = bf16[64,512]{1,0:T(8,128)(2,1)} custom-call(bf16[512,640]{1,0:T(8,128)(2,1)} %reshape.277.x_ref), custom_call_target="tpu_custom_call" | custom-call | tf_op jit(solution)/shard_map/combine/pallas_call | solution.py:155
  121.1 1.5 %reshape.278 = bf16[16,4,512]{2,1,0:T(4,128)(2,1)} reshape(bf16[64,512]{1,0:T(8,128)(2,1)} %combine.1) | data formatting | bytes 131072 | tf_op jit(solution)/shard_map/reshape | solution.py:226
  (54 shorter events, 9.6 us)
Async XLA Ops:
  0.0 19.6 %copy-start.3 = (s32[128]{0:T(128)S(1)}, s32[128]{0:T(128)}, u32[]{:S(2)}) copy-start(s32[128]{0:T(128)} %param.13) | copy-start | bytes 1540
  1.6 18.2 %collective-permute-start = (bf16[64,576]{1,0:T(8,128)(2,1)S(1)}, bf16[64,576]{1,0:T(8,128)(2,1)S(1)}, u32[]{:S(2)}, u32[]{:S(2)}) collective-permute-start(bf16[64,576]{1,0:T(8,128)(2,1)S(1)} %constant_dynamic-update-slice_fusion), channel_id=1, source_target_pairs={{0,136},{8,128},{128,8},{136,0},{1,137},{9,129},{129,9},{137,1},{2... | collective-permute-start | bytes 221192 | tf_op jit(solution)/shard_map/ppermute | solution.py:168
  6.4 53.4 %all-to-all-start = ((bf16[128,4,768]{2,1,0:T(4,128)(2,1)}), bf16[128,4,768]{2,1,0:T(4,128)(2,1)}, u32[]{:S(2)}, u32[]{:S(2)}) async-start(bf16[128,4,768]{2,1,0:T(4,128)(2,1)} %bitcast.1), calls=%async_computation | async-start | bytes 1572864 | tf_op jit(solution)/shard_map/all_to_all | solution.py:215
  19.9 19.9 %collective-permute-start.1 = (bf16[2,64,576]{2,1,0:T(8,128)(2,1)S(1)}, bf16[2,64,576]{2,1,0:T(8,128)(2,1)S(1)}, u32[]{:S(2)}, u32[]{:S(2)}) collective-permute-start(bf16[2,64,576]{2,1,0:T(8,128)(2,1)S(1)} %pad_maximum_fusion.1), channel_id=1, source_target_pairs={{0,1},{1,2},{2,3},{3,4},{4,5},{5,6},{6,7},{7,0},{8,9},{9,10},{10,1... | collective-permute-start | bytes 442376 | tf_op jit(solution)/shard_map/ppermute | solution.py:173
  21.4 19.3 %collective-permute-start.2 = (bf16[2,64,576]{2,1,0:T(8,128)(2,1)S(1)}, bf16[2,64,576]{2,1,0:T(8,128)(2,1)S(1)}, u32[]{:S(2)}, u32[]{:S(2)}) collective-permute-start(bf16[2,64,576]{2,1,0:T(8,128)(2,1)S(1)} %pad_maximum_fusion.1), channel_id=1, source_target_pairs={{0,7},{1,0},{2,1},{3,2},{4,3},{5,4},{6,5},{7,6},{8,15},{9,8},{10,9... | collective-permute-start | bytes 442376 | tf_op jit(solution)/shard_map/ppermute | solution.py:174
  22.0 36.2 %copy-start.2 = (s32[8,128]{1,0:T(8,128)S(1)}, s32[8,128]{1,0:T(8,128)}, u32[]{:S(2)}) copy-start(s32[8,128]{1,0:T(8,128)} %param.12) | copy-start | bytes 12292
  22.8 36.5 %copy-start = (bf16[4,128,512]{2,1,0:T(8,128)(2,1)S(1)}, bf16[4,128,512]{2,1,0:T(8,128)(2,1)}, u32[]{:S(2)}) copy-start(bf16[4,128,512]{2,1,0:T(8,128)(2,1)} %param.10) | copy-start | bytes 1572868
  39.8 5.4 %collective-permute-start.3 = (bf16[2,64,576]{2,1,0:T(8,128)(2,1)S(1)}, bf16[2,64,576]{2,1,0:T(8,128)(2,1)S(1)}, u32[]{:S(2)}, u32[]{:S(2)}) collective-permute-start(bf16[2,64,576]{2,1,0:T(8,128)(2,1)S(1)} %collective-permute-done.1), channel_id=1, source_target_pairs={{0,1},{1,2},{2,3},{3,4},{4,5},{5,6},{6,7},{7,0},{8,9},{9,10},{10,1... | collective-permute-start | bytes 442376 | tf_op jit(solution)/shard_map/ppermute | solution.py:173
  40.7 5.4 %collective-permute-start.4 = (bf16[2,64,576]{2,1,0:T(8,128)(2,1)S(1)}, bf16[2,64,576]{2,1,0:T(8,128)(2,1)S(1)}, u32[]{:S(2)}, u32[]{:S(2)}) collective-permute-start(bf16[2,64,576]{2,1,0:T(8,128)(2,1)S(1)} %collective-permute-done.2), channel_id=1, source_target_pairs={{0,7},{1,0},{2,1},{3,2},{4,3},{5,4},{6,5},{7,6},{8,15},{9,8},{10,9... | collective-permute-start | bytes 442376 | tf_op jit(solution)/shard_map/ppermute | solution.py:174
  43.4 16.2 %copy-start.1 = (bf16[4,512,128]{2,1,0:T(8,128)(2,1)S(1)}, bf16[4,512,128]{2,1,0:T(8,128)(2,1)}, u32[]{:S(2)}) copy-start(bf16[4,512,128]{2,1,0:T(8,128)(2,1)} %param.11) | copy-start | bytes 1572868
  45.2 6.5 %collective-permute-start.5 = (bf16[2,64,576]{2,1,0:T(8,128)(2,1)S(1)}, bf16[2,64,576]{2,1,0:T(8,128)(2,1)S(1)}, u32[]{:S(2)}, u32[]{:S(2)}) collective-permute-start(bf16[2,64,576]{2,1,0:T(8,128)(2,1)S(1)} %collective-permute-done.3), channel_id=1, source_target_pairs={{0,1},{1,2},{2,3},{3,4},{4,5},{5,6},{6,7},{7,0},{8,9},{9,10},{10,1... | collective-permute-start | bytes 442376 | tf_op jit(solution)/shard_map/ppermute | solution.py:173
  46.1 5.8 %collective-permute-start.6 = (bf16[2,64,576]{2,1,0:T(8,128)(2,1)S(1)}, bf16[2,64,576]{2,1,0:T(8,128)(2,1)S(1)}, u32[]{:S(2)}, u32[]{:S(2)}) collective-permute-start(bf16[2,64,576]{2,1,0:T(8,128)(2,1)S(1)} %collective-permute-done.4), channel_id=1, source_target_pairs={{0,7},{1,0},{2,1},{3,2},{4,3},{5,4},{6,5},{7,6},{8,15},{9,8},{10,9... | collective-permute-start | bytes 442376 | tf_op jit(solution)/shard_map/ppermute | solution.py:174
  51.7 5.7 %collective-permute-start.7 = (bf16[64,576]{1,0:T(8,128)(2,1)S(1)}, bf16[64,576]{1,0:T(8,128)(2,1)S(1)}, u32[]{:S(2)}, u32[]{:S(2)}) collective-permute-start(bf16[64,576]{1,0:T(8,128)(2,1)S(1)} %slice_bitcast_fusion.1), channel_id=1, source_target_pairs={{0,1},{1,2},{2,3},{3,4},{4,5},{5,6},{6,7},{7,0},{8,9},{9,10},{10,1... | collective-permute-start | bytes 221192 | tf_op jit(solution)/shard_map/ppermute | solution.py:176
  51.9 5.6 %collective-permute-start.8 = (bf16[64,576]{1,0:T(8,128)(2,1)S(1)}, bf16[64,576]{1,0:T(8,128)(2,1)S(1)}, u32[]{:S(2)}, u32[]{:S(2)}) collective-permute-start(bf16[64,576]{1,0:T(8,128)(2,1)S(1)} %slice_bitcast_fusion), channel_id=1, source_target_pairs={{0,7},{1,0},{2,1},{3,2},{4,3},{5,4},{6,5},{7,6},{8,15},{9,8},{10,9... | collective-permute-start | bytes 221192 | tf_op jit(solution)/shard_map/ppermute | solution.py:176
  58.2 4.4 %collective-permute-start.9 = (bf16[8,2,64,576]{3,2,1,0:T(8,128)(2,1)}, bf16[8,2,64,576]{3,2,1,0:T(8,128)(2,1)}, u32[]{:S(2)}, u32[]{:S(2)}) collective-permute-start(bf16[8,2,64,576]{3,2,1,0:T(8,128)(2,1)} %get-tuple-element.7), channel_id=1, source_target_pairs={{0,16},{16,0},{1,17},{17,1},{2,18},{18,2},{3,19},{19,3},{4,20},{20... | collective-permute-start | bytes 3538952 | tf_op jit(solution)/shard_map/ppermute | solution.py:179

commit v2 on v1

v2 whole, which is shorter than its diff:
```python
import functools
import math

import jax
import jax.numpy as jnp
from jax import lax
from jax.experimental import pallas as pl
from jax.experimental.pallas import tpu as pltpu
from jax.sharding import Mesh
from jax.sharding import PartitionSpec as P

L = 512
QN = 128
QR = 64
QD = QN + QR
VD = 128
BLOCK = 128
HEADS = 4
NEG = -1e30
SCALE = 1.0 / math.sqrt(QD)
LOG2E = math.log2(math.e)

AXES = ("xl", "y", "core", "xh", "z")
CHIPS = ("xl", "y", "xh", "z")
XLN, YN, CN, XHN, ZN = 2, 4, 2, 2, 8
CELLS = XLN * YN
GRP = XHN * ZN
PER = 64
TOK = 4
ROWS = CELLS * GRP * TOK
EXT = HEADS * VD + 128

QT = 256
KT = 512

FULL = 144
HALF = 80


def chunk(swap, other, step, full):
    return [(swap, other, step, j) for j in range(2 if full else 1)]


GROUP_A = [(0, 0, 0, True)]
GROUP_A += [(0, o, s, True) for s in (1, 2) for o in (0, 1)]
GROUP_A += [(1, o, 1, True) for o in (0, 1)]
GROUP_A += [(1, o, 0, False) for o in (0, 1)]
GROUP_B = [(x, o, 3, True) for x in (0, 1) for o in (0, 1)]
GROUP_B += [(1, o, 2, True) for o in (0, 1)]
GROUP_B += [(x, o, 4, False) for x in (0, 1) for o in (0, 1)]
PIECES = [p for c in GROUP_A + GROUP_B for p in chunk(*c)]
SLOTS = len(PIECES)
KEYS = SLOTS * PER
PART = KEYS // 2


def project_kernel(count, *refs):
    chunks, (w_ref, k_ref, v_ref, lat) = refs[:count], refs[count:]
    base = 0
    for ref in chunks:
        n = 2 * PER if ref.shape[0] == FULL else PER
        lat[base : base + n, :] = ref[0:n, :]
        for r in range(n // 16):
            rope = ref[n : n + 16, r * QR : (r + 1) * QR]
            for h in range(HEADS):
                k_ref[h, base + r * 16 : base + (r + 1) * 16, QN:QD] = rope
        base += n
    for h in range(HEADS):
        for i in range(PART // KT):
            rows = slice(i * KT, (i + 1) * KT)
            kv = jnp.dot(lat[rows, :], w_ref[h], preferred_element_type=jnp.float32)
            kv = kv.astype(jnp.bfloat16)
            k_ref[h, rows, 0:QN] = kv[:, 0:QN]
            v_ref[h, rows, :] = kv[:, QN:]


def project(chunks, weights):
    return pl.pallas_call(
        functools.partial(project_kernel, len(chunks)),
        out_shape=(
            jax.ShapeDtypeStruct((HEADS, PART, QD), jnp.bfloat16),
            jax.ShapeDtypeStruct((HEADS, PART, VD), jnp.bfloat16),
        ),
        scratch_shapes=[pltpu.VMEM((PART, L), jnp.bfloat16)],
        compiler_params=pltpu.CompilerParams(vmem_limit_bytes=24 * 1024 * 1024),
        cost_estimate=pl.CostEstimate(
            flops=1_100_000_000, bytes_accessed=5_000_000, transcendentals=0
        ),
        name="project",
    )(*chunks, weights)


def attend_kernel(q_ref, ka_ref, va_ref, kb_ref, vb_ref, thr_ref, off_ref, o_ref, qs, sco, stats):
    h = pl.program_id(0)

    @pl.when(h == 0)
    def _():
        for g in range(HEADS):
            qs[g] = q_ref[:, g * QD : (g + 1) * QD]
        stats[...] = jnp.zeros_like(stats)

    keys = [(r, slice(i * KT, (i + 1) * KT)) for r in (ka_ref, kb_ref) for i in range(PART // KT)]
    vals = [(r, slice(i * KT, (i + 1) * KT)) for r in (va_ref, vb_ref) for i in range(PART // KT)]
    lane = lax.broadcasted_iota(jnp.int32, (QT, 128), 1)
    off = off_ref[...]
    for t in range(ROWS // QT):
        q = qs[h, pl.ds(t * QT, QT), :]
        top = jnp.full((QT, 128), NEG, jnp.float32)
        for i, (ref, rows) in enumerate(keys):
            s = lax.dot_general(
                q, ref[0, rows, :], (((1,), (1,)), ((), ())), preferred_element_type=jnp.float32
            )
            parts = []
            for b in range(QT // 64):
                thr = thr_ref[pl.ds(t * (QT // 64) + b, 1), pl.ds(i * KT, KT)]
                cols = []
                for c in range(KT // 128):
                    piece = s[b * 64 : (b + 1) * 64, c * 128 : (c + 1) * 128]
                    cols.append(jnp.where(off >= thr[:, c * 128 : (c + 1) * 128], piece, NEG))
                best = functools.reduce(jnp.maximum, cols)
                parts.append(best)
                for c in range(KT // 128):
                    sco[b * 64 : (b + 1) * 64, i * KT + c * 128 : i * KT + (c + 1) * 128] = cols[c]
            top = jnp.maximum(top, jnp.concatenate(parts, axis=0))
        m = jnp.max(top, axis=1, keepdims=True)
        mc = m * (SCALE * LOG2E)
        total = jnp.zeros((QT, 128), jnp.float32)
        acc = jnp.zeros((QT, VD), jnp.float32)
        for i, (ref, rows) in enumerate(vals):
            p = jnp.exp2(sco[:, pl.ds(i * KT, KT)] * (SCALE * LOG2E) - mc)
            for c in range(KT // 128):
                total = total + p[:, c * 128 : (c + 1) * 128]
            acc = acc + jnp.dot(
                p.astype(jnp.bfloat16), ref[0, rows, :], preferred_element_type=jnp.float32
            )
        den = jnp.sum(total, axis=1, keepdims=True)
        lse = m * SCALE + jnp.log(den)
        o_ref[pl.ds(t * QT, QT), pl.ds(pl.multiple_of(h * VD, VD), VD)] = (acc / den).astype(
            jnp.bfloat16
        )
        hi = lse.astype(jnp.bfloat16).astype(jnp.float32)
        mid = (lse - hi).astype(jnp.bfloat16).astype(jnp.float32)
        low = lse - hi - mid
        old = stats[pl.ds(t * QT, QT), :]
        old = jnp.where(lane == 3 * h, hi, old)
        old = jnp.where(lane == 3 * h + 1, mid, old)
        stats[pl.ds(t * QT, QT), :] = jnp.where(lane == 3 * h + 2, low, old)

    @pl.when(h == HEADS - 1)
    def _():
        o_ref[:, HEADS * VD :] = stats[...].astype(jnp.bfloat16)


def attend(q, ka, va, kb, vb, thr, off):
    full = lambda shape: pl.BlockSpec(shape, lambda h: tuple(0 for _ in shape))
    head = lambda shape: pl.BlockSpec((1, *shape), lambda h: (h, 0, 0))
    return pl.pallas_call(
        attend_kernel,
        grid=(HEADS,),
        out_shape=jax.ShapeDtypeStruct((ROWS, EXT), jnp.bfloat16),
        in_specs=[
            full((ROWS, HEADS * QD)),
            head((PART, QD)),
            head((PART, VD)),
            head((PART, QD)),
            head((PART, VD)),
            full((CELLS, KEYS)),
            full((64, 128)),
        ],
        out_specs=full((ROWS, EXT)),
        scratch_shapes=[
            pltpu.VMEM((HEADS, ROWS, QD), jnp.bfloat16),
            pltpu.VMEM((QT, KEYS), jnp.float32),
            pltpu.VMEM((ROWS, 128), jnp.float32),
        ],
        compiler_params=pltpu.CompilerParams(vmem_limit_bytes=32 * 1024 * 1024),
        cost_estimate=pl.CostEstimate(
            flops=4_000_000_000, bytes_accessed=8_000_000, transcendentals=4_200_000
        ),
        name="attend",
    )(q, ka, va, kb, vb, thr, off)


def combine_kernel(x_ref, o_ref):
    n = GRP * TOK
    ext = [x_ref[pl.ds(c * n, n), pl.ds(HEADS * VD, 128)].astype(jnp.float32) for c in range(CELLS)]
    for h in range(HEADS):
        lse = [
            e[:, 3 * h : 3 * h + 1] + e[:, 3 * h + 1 : 3 * h + 2] + e[:, 3 * h + 2 : 3 * h + 3]
            for e in ext
        ]
        top = functools.reduce(jnp.maximum, lse)
        part = [jnp.exp(v - top) for v in lse]
        scale = 1.0 / functools.reduce(jnp.add, part)
        acc = jnp.zeros((n, VD), jnp.float32)
        for c in range(CELLS):
            acc = acc + x_ref[pl.ds(c * n, n), pl.ds(h * VD, VD)].astype(jnp.float32) * (
                part[c] * scale
            )
        o_ref[:, pl.ds(h * VD, VD)] = acc.astype(jnp.bfloat16)


def combine(x):
    return pl.pallas_call(
        combine_kernel,
        out_shape=jax.ShapeDtypeStruct((GRP * TOK, HEADS * VD), jnp.bfloat16),
        name="combine",
    )(x)


def shift(n, k):
    return [(i, (i + k) % n) for i in range(n)]


def gather_keys(latents, key_rope):
    near = [(a * 2 + b, (1 - a) * 2 + 1 - b) for a in range(2) for b in range(2)]
    round_z = [(i, (i + 1) % ZN) for i in range(ZN)] + [(ZN + i, ZN + (i - 1) % ZN) for i in range(ZN)]
    to_core = lambda x: lax.ppermute(x, "core", shift(CN, 1))
    to_near = lambda x: lax.ppermute(x, ("xl", "xh"), near)
    rope = key_rope.reshape(PER // 16, 16, QR).transpose(1, 0, 2).reshape(16, PER // 16 * QR)
    piece = jnp.concatenate([latents, jnp.pad(rope, ((0, 0), (0, L - rope.shape[1])))])
    mate = to_core(piece)
    got = {}
    got[1, 0, 0] = to_near(piece)
    side = jnp.concatenate([piece[PER:, : L // 2], mate[PER:, : L // 2]], axis=1)
    now = jnp.concatenate([piece[:PER], mate[:PER], side])
    got[0, 0, 0] = now
    for s in range(1, 5):
        if s == 4:
            now = jnp.concatenate([now[:PER], now[2 * PER :]])
        now = lax.ppermute(now, ("core", "z"), round_z)
        got[0, 0, s] = now
        got[1, 0, s] = to_near(now)
    for x in range(2):
        for s in range(5):
            if (x, s) != (0, 0):
                got[x, 1, s] = to_core(got[x, 0, s])
    pick = lambda group: [got[x, o, s] for x, o, s, _ in group]
    return pick(GROUP_A), pick(GROUP_B)


def thresholds(pattern, stripe):
    xl, y, core = lax.axis_index("xl"), lax.axis_index("y"), lax.axis_index("core")
    xh, z = lax.axis_index("xh"), lax.axis_index("z")
    swap, other, step, inner = (jnp.asarray([p[i] for p in PIECES], jnp.int32) for i in range(4))
    lane = core ^ other
    k = lane ^ inner
    zz = (z + jnp.where(lane == 1, step, ZN - step)) % ZN
    cell = ((xl ^ swap) * YN + y) * CN + k
    place = cell * GRP + (xh ^ swap) * ZN + zz
    block = place * PER // BLOCK
    base = place * PER % BLOCK
    nb = stripe.shape[0]
    every = jnp.arange(nb, dtype=jnp.int32)
    kb = jnp.sum(jnp.where(block[:, None] == every[None, :], stripe[None, :], 0), axis=1)
    hit = jnp.sum(jnp.where(kb[None, :, None] == every[None, None, :], pattern[:, None, :], 0), axis=2)
    qb = nb - CELLS + jnp.arange(CELLS, dtype=jnp.int32)[:, None]
    see = (kb[None, :] < qb) & (hit == 1)
    offset = base[:, None] + jnp.arange(PER, dtype=jnp.int32)[None, :]
    thr = jnp.where(
        see[:, :, None], 0, jnp.where((kb[None, :] == qb)[:, :, None], offset[None], 4 * BLOCK)
    )
    return thr.reshape(CELLS, KEYS).astype(jnp.float32)


def body(queries, latents, key_rope, key_up, value_up, pattern, stripe):
    cells = ("xl", "y")
    groups = ("xh", "z")
    send = queries.reshape(TOK, GRP, HEADS * QD).transpose(1, 0, 2)
    mine = lax.all_to_all(send, groups, split_axis=0, concat_axis=0, tiled=True)
    mine = mine.reshape(GRP * TOK, HEADS * QD)
    send = jnp.broadcast_to(mine[None], (CELLS, *mine.shape))
    q = lax.all_to_all(send, cells, split_axis=0, concat_axis=0, tiled=True)
    q = q.reshape(ROWS, HEADS * QD)
    weights = jnp.concatenate([key_up.transpose(0, 2, 1), value_up], axis=2)
    thr = thresholds(pattern, stripe)
    off = (lax.axis_index("core") * 64 + jnp.arange(64, dtype=jnp.int32)).astype(jnp.float32)
    off = jnp.broadcast_to(off[:, None], (64, 128))
    first, second = gather_keys(latents, key_rope)
    part = attend(q, *project(first, weights), *project(second, weights), thr, off)
    back = lax.all_to_all(
        part.reshape(CELLS, GRP * TOK, EXT), cells, split_axis=0, concat_axis=0, tiled=True
    )
    out = combine(back.reshape(ROWS, EXT)).reshape(GRP, TOK, HEADS * VD)
    out = lax.all_to_all(out, groups, split_axis=0, concat_axis=0, tiled=True)
    return out.transpose(1, 0, 2).reshape(TOK, GRP * HEADS * VD)


def solution(mesh):
    fine = Mesh(mesh.devices.reshape(XLN, YN, CN, XHN, ZN), AXES)
    in_specs = (
        P(AXES, None),
        P(AXES, None),
        P(AXES, None),
        P(("xh", "z"), None, None),
        P(("xh", "z"), None, None),
        P(),
        P(),
    )
    return jax.shard_map(body, mesh=fine, in_specs=in_specs, out_specs=P(AXES, None), check_vma=False)
```

time: 124 us -> 115 us (0.927)
  waiting for transfers between devices: 21.3 us -> 9.08 us
  starting transfers between devices: 26.8 us -> 32.8 us
  local copies, waits for them, and re-layouts: 20.1 us -> 15.4 us
  other arithmetic: 2.27 us -> 6.31 us
  blocking collectives: 38.5 us -> 36.1 us
    ppermute x10 -> x19, waiting for transfers between devices: 21.3 us -> 9.07 us  [the longest x4 5.55 us: gather_keys(): now = lax.ppermute(now, ('core', 'z'), round_z)]
    ppermute x10 -> x19, starting transfers between devices: 13.6 us -> 19.5 us  [the longest x5 9.8 us: gather_keys(): to_near = lambda x: lax.ppermute(x, ('xl', 'xh'), near)]
    unnamed x17 -> x20, local copies, waits for them, and re-layouts: 6.59 us -> 11.9 us
    reshape x5 -> x3, local copies, waits for them, and re-layouts: 5.49 us -> 1.73 us  [the longest x2 0.87 us: gather_keys(): key_rope.reshape(PER // 16, 16, QR).transpose(1, 0, 2)]
    pallas_call x0 -> x2, Pallas kernels: none -> 3.45 us  [project(): pl.pallas_call(functools.partial(project_kernel, len(chunks)), out_shape=...]
    concatenate x2 -> x0, local copies, waits for them, and re-layouts: 3.24 us -> none  [the longest x1 2.51 us: gather_keys(): return jnp.concatenate([mine, theirs]).reshape(KEYS, mine.shape[-1])]
    slice x2 -> x4, local copies, waits for them, and re-layouts: 2.8 us -> 0.02 us  [the longest x1 0.01 us: gather_keys(): now = jnp.concatenate([piece[:PER], mate[:PER], side])]
    pallas_call x1, Pallas kernels: 11.2 us -> 8.52 us  [attend(): pl.pallas_call(attend_kernel, grid=(HEADS,), out_shape=jax.ShapeDtypeStru...]
  transfers between devices with their start and end apart: 11 -> 21, of which waited for: 4 -> 4; matrix products, arithmetic and copies ran while one was open for 10% -> 7% of each run, Pallas kernels for 0% -> 3%
where the time goes in v2:
time: 115 us; the launch traced here: 114 us
  blocking collectives  36.1 us (31%)
  starting transfers between devices  32.8 us (29%)
  local copies, waits for them, and re-layouts  15.4 us (13%)
  Pallas kernels  14.2 us (12%)
  waiting for transfers between devices  9.08 us (8%)
  other arithmetic  6.31 us (5%)
    all_to_all x1, blocking collectives, body(): out = lax.all_to_all(out, groups, split_axis=0, concat_axis=0, tiled=True)  19.8 us
    all_to_all x1, blocking collectives, body(): lax.all_to_all(part.reshape(CELLS, GRP * TOK, EXT), cells, split_axis=0,...  16.3 us
    unnamed x20, local copies, waits for them, and re-layouts  11.9 us
    ppermute x5, starting transfers between devices, gather_keys(): to_near = lambda x: lax.ppermute(x, ('xl', 'xh'), near)  9.8 us
    all_to_all x1, starting transfers between devices, body(): mine = lax.all_to_all(send, groups, split_axis=0, concat_axis=0, tiled=True)  8.82 us
    pallas_call x1, Pallas kernels, attend(): pl.pallas_call(attend_kernel, grid=(HEADS,), out_shape=jax.ShapeDtypeStru...  8.52 us
    ppermute x4, starting transfers between devices, gather_keys(): now = lax.ppermute(now, ('core', 'z'), round_z)  8.35 us
    ppermute x4, waiting for transfers between devices, gather_keys(): now = lax.ppermute(now, ('core', 'z'), round_z)  5.55 us
  transfers between devices with their start and end apart: 21, of which 4 were waited for; matrix products, arithmetic and copies ran while one was open for 7% of the time, Pallas kernels for 3%

profile of v2, /device:TPU:32, one launch (start us, length us, event | category | flops | bytes accessed | tf_op | source)
XLA Modules:
  0.0 114.1 jit_solution(9270201635973565230)
XLA Ops:
  1.7 2.8 %collective-permute-start.7 = (bf16[80,512]{1,0:T(8,128)(2,1)S(1)}, bf16[80,512]{1,0:T(8,128)(2,1)S(1)}, u32[]{:S(2)}, u32[]{:S(2)}) collective-permute-start(bf16[80,512]{1,0:T(8,128)(2,1)S(1)} %fusion.1), channel_id=1, source_target_pairs={{0,136},{8,128},{128,8},{136,0},{1,137},{9,129},{129,9},{137,1},{2... | collective-permute-start | bytes 245768 | tf_op jit(solution)/shard_map/ppermute | solution.py:219
  4.6 8.8 %all-to-all-start = ((bf16[16,4,768]{2,1,0:T(4,128)(2,1)}), bf16[16,4,768]{2,1,0:T(4,128)(2,1)S(1)}, u32[]{:S(2)}, u32[]{:S(2)}) async-start(bf16[16,4,768]{2,1,0:T(4,128)(2,1)} %bitcast.19), calls=%async_computation | async-start | bytes 196608 | tf_op jit(solution)/shard_map/all_to_all | solution.py:270
  15.9 1.5 %collective-permute-start.1 = (bf16[144,512]{1,0:T(8,128)(2,1)S(1)}, bf16[144,512]{1,0:T(8,128)(2,1)S(1)}, u32[]{:S(2)}, u32[]{:S(2)}) collective-permute-start(bf16[144,512]{1,0:T(8,128)(2,1)S(1)} %maximum_maximum_fusion.refs_0_), channel_id=1, source_target_pairs={{0,1},{1,2},{2,3},{3,4},{4,5},{5,6},{6,7},{7,0},{16,23},{17,16},{1... | collective-permute-start | bytes 442376 | tf_op jit(solution)/shard_map/ppermute | solution.py:231
  18.4 2.8 %collective-permute-done.1.refs_1_ = bf16[144,512]{1,0:T(8,128)(2,1)S(1)} collective-permute-done((bf16[144,512]{1,0:T(8,128)(2,1)S(1)}, bf16[144,512]{1,0:T(8,128)(2,1)S(1)}, u32[]{:S(2)}, u32[]{:S(2)}) %collective-permute-start.1) | collective-permute-done | bytes 147488 | tf_op jit(solution)/shard_map/ppermute | solution.py:231
  21.2 1.5 %collective-permute-start.3 = (bf16[144,512]{1,0:T(8,128)(2,1)S(1)}, bf16[144,512]{1,0:T(8,128)(2,1)S(1)}, u32[]{:S(2)}, u32[]{:S(2)}) collective-permute-start(bf16[144,512]{1,0:T(8,128)(2,1)S(1)} %collective-permute-done.1.refs_1_), channel_id=1, source_target_pairs={{0,1},{1,2},{2,3},{3,4},{4,5},{5,6},{6,7},{7,0},{16,23},{17,16},{1... | collective-permute-start | bytes 442376 | tf_op jit(solution)/shard_map/ppermute | solution.py:231
  24.5 4.5 %all-to-all-start.1 = ((bf16[8,64,768]{2,1,0:T(8,128)(2,1)}), bf16[8,64,768]{2,1,0:T(8,128)(2,1)S(1)}, u32[]{:S(2)}, u32[]{:S(2)}) async-start(bf16[8,64,768]{2,1,0:T(8,128)(2,1)} %broadcast_in_dim.96), calls=%async_computation.1 | async-start | bytes 1572864 | tf_op jit(solution)/shard_map/all_to_all | solution.py:273
  29.0 4.1 %collective-permute-start.5 = (bf16[144,512]{1,0:T(8,128)(2,1)S(1)}, bf16[144,512]{1,0:T(8,128)(2,1)S(1)}, u32[]{:S(2)}, u32[]{:S(2)}) collective-permute-start(bf16[144,512]{1,0:T(8,128)(2,1)S(1)} %collective-permute-done.1.refs_1_), channel_id=1, source_target_pairs={{0,136},{8,128},{128,8},{136,0},{1,137},{9,129},{129,9},{137,1},{2... | collective-permute-start | bytes 442376 | tf_op jit(solution)/shard_map/ppermute | solution.py:219
  33.1 1.7 %collective-permute-start.9 = (bf16[144,512]{1,0:T(8,128)(2,1)S(1)}, bf16[144,512]{1,0:T(8,128)(2,1)S(1)}, u32[]{:S(2)}, u32[]{:S(2)}) collective-permute-start(bf16[144,512]{1,0:T(8,128)(2,1)S(1)} %collective-permute-done.3.refs_3_), channel_id=1, source_target_pairs={{0,1},{1,2},{2,3},{3,4},{4,5},{5,6},{6,7},{7,0},{16,23},{17,16},{1... | collective-permute-start | bytes 442376 | tf_op jit(solution)/shard_map/ppermute | solution.py:231
  35.9 2.3 %collective-permute-done.9.refs_0_ = bf16[144,512]{1,0:T(8,128)(2,1)S(1)} collective-permute-done((bf16[144,512]{1,0:T(8,128)(2,1)S(1)}, bf16[144,512]{1,0:T(8,128)(2,1)S(1)}, u32[]{:S(2)}, u32[]{:S(2)}) %collective-permute-start.9) | collective-permute-done | bytes 147488 | tf_op jit(solution)/shard_map/ppermute | solution.py:231
  40.0 3.7 %collective-permute-start.15 = (bf16[80,512]{1,0:T(8,128)(2,1)}, bf16[80,512]{1,0:T(8,128)(2,1)}, u32[]{:S(2)}, u32[]{:S(2)}) collective-permute-start(bf16[80,512]{1,0:T(8,128)(2,1)} %pad_maximum_fusion.1), channel_id=1, source_target_pairs={{0,1},{1,2},{2,3},{3,4},{4,5},{5,6},{6,7},{7,0},{16,23},{17,16},{1... | collective-permute-start | bytes 245768 | tf_op jit(solution)/shard_map/ppermute | solution.py:231
  43.7 1.3 %pad_maximum_fusion.refs_9_.refs_10_ = bf16[4,512,256]{2,1,0:T(8,128)(2,1)S(1)} fusion(bf16[4,512,128]{2,1,0:T(8,128)(2,1)} %param.15, bf16[4,512,128]{2,1,0:T(8,128)(2,1)} %bitcast.17), kind=kLoop, calls=%fused_computation | loop fusion | flops 2097152 | bytes 2097152 | tf_op jit(solution)/shard_map/concatenate | solution.py:275
  46.1 1.8 %collective-permute-start.17 = (bf16[80,512]{1,0:T(8,128)(2,1)}, bf16[80,512]{1,0:T(8,128)(2,1)S(1)}, u32[]{:S(2)}, u32[]{:S(2)}) collective-permute-start(bf16[80,512]{1,0:T(8,128)(2,1)} %collective-permute-done.15.refs_6_), channel_id=1, source_target_pairs={{0,136},{8,128},{128,8},{136,0},{1,137},{9,129},{129,9},{137,1},{2... | collective-permute-start | bytes 245768 | tf_op jit(solution)/shard_map/ppermute | solution.py:219
  48.5 3.5 %collective-permute-done.17.refs_8_ = bf16[80,512]{1,0:T(8,128)(2,1)S(1)} collective-permute-done((bf16[80,512]{1,0:T(8,128)(2,1)}, bf16[80,512]{1,0:T(8,128)(2,1)S(1)}, u32[]{:S(2)}, u32[]{:S(2)}) %collective-permute-start.17) | collective-permute-done | bytes 81952 | tf_op jit(solution)/shard_map/ppermute | solution.py:219
  52.0 1.3 %project.2 = (bf16[4,1024,192]{2,1,0:T(8,128)(2,1)S(1)}, bf16[4,1024,128]{2,1,0:T(8,128)(2,1)S(1)}) custom-call(bf16[144,512]{1,0:T(8,128)(2,1)S(1)} %maximum_maximum_fusion.refs_0_, bf16[144,512]{1,0:T(8,128)(2,1)S(1)} %collective-permute-done.1.refs_1_, bf16[144,512]{1,0:T(8,128)(2,1)S(1)} %collective-permute-done.2.refs_2_, ...), custom_call_target="tpu_custom_call" | custom-call | flops 1100000000 | bytes 5000000 | tf_op jit(solution)/shard_map/project/pallas_call | solution.py:78
  53.2 1.3 %copy-done.2 = bf16[4,1024,192]{2,1,0:T(8,128)(2,1)} copy-done((bf16[4,1024,192]{2,1,0:T(8,128)(2,1)}, bf16[4,1024,192]{2,1,0:T(8,128)(2,1)S(1)}, u32[]{:S(2)}) %copy-start.2) | copy-done | bytes 1572888
  55.6 2.2 %project.3 = (bf16[4,1024,192]{2,1,0:T(8,128)(2,1)S(1)}, bf16[4,1024,128]{2,1,0:T(8,128)(2,1)S(1)}) custom-call(bf16[144,512]{1,0:T(8,128)(2,1)S(1)} %collective-permute-done.9.refs_0_, bf16[144,512]{1,0:T(8,128)(2,1)S(1)} %collective-permute-done.10.refs_1_, bf16[144,512]{1,0:T(8,128)(2,1)S(1)} %collective-permute-done.11.refs_2_, ...), custom_call_target="tpu_custom_call" | custom-call | flops 1100000000 | bytes 5000000 | tf_op jit(solution)/shard_map/project/pallas_call | solution.py:78
  57.8 1.3 %copy-done = bf16[4,1024,192]{2,1,0:T(8,128)(2,1)} copy-done((bf16[4,1024,192]{2,1,0:T(8,128)(2,1)}, bf16[4,1024,192]{2,1,0:T(8,128)(2,1)S(1)}, u32[]{:S(2)}) %copy-start) | copy-done | bytes 1572888
  60.1 1.6 %copy-done.1 = bf16[4,1024,192]{2,1,0:T(8,128)(2,1)S(1)} copy-done((bf16[4,1024,192]{2,1,0:T(8,128)(2,1)S(1)}, bf16[4,1024,192]{2,1,0:T(8,128)(2,1)}, u32[]{:S(2)}) %copy-start.1) | copy-done | bytes 1572888
  61.7 1.6 %copy-done.3 = bf16[4,1024,192]{2,1,0:T(8,128)(2,1)S(1)} copy-done((bf16[4,1024,192]{2,1,0:T(8,128)(2,1)S(1)}, bf16[4,1024,192]{2,1,0:T(8,128)(2,1)}, u32[]{:S(2)}) %copy-start.3) | copy-done | bytes 1572888
  63.3 1.2 %copy-done.5 = bf16[4,1024,128]{2,1,0:T(8,128)(2,1)S(1)} copy-done((bf16[4,1024,128]{2,1,0:T(8,128)(2,1)S(1)}, bf16[4,1024,128]{2,1,0:T(8,128)(2,1)}, u32[]{:S(2)}) %copy-start.5) | copy-done | bytes 1048600
  65.8 8.5 %attend.1 = bf16[512,640]{1,0:T(8,128)(2,1)S(1)} custom-call(bf16[512,768]{1,0:T(8,128)(2,1)S(1)} %bitcast.14, bf16[4,1024,192]{2,1,0:T(8,128)(2,1)S(1)} %copy-done.3, bf16[4,1024,128]{2,1,0:T(8,128)(2,1)S(1)} %copy-done.7, bf16[4,1024,192]{2,1,0:T(8,128)(2,1)S(1)} %copy-done.1, bf16[4,1024,128]{2,1,0:T(8,128)(2,1)S(1)} %copy-done.5, ...), custom_call_target="tpu_custom_call" | custom-call | flops 4000000000 | bytes 8000000 | tf_op jit(solution)/shard_map/attend/pallas_call | solution.py:157
  74.3 16.3 %all_to_all.20 = bf16[8,64,640]{2,1,0:T(8,128)(2,1)} all-to-all(bf16[8,64,640]{2,1,0:T(8,128)(2,1)S(1)} %bitcast.15), channel_id=1, replica_groups=mesh['xl'=2,'y'=4,'core'=2,'xh'=2,'z'=8] {'xl','y'}, dimensions={0} | all-to-all | bytes 1310720 | tf_op jit(solution)/shard_map/all_to_all | solution.py:281
  90.6 2.3 %combine.1 = bf16[64,512]{1,0:T(8,128)(2,1)} custom-call(bf16[512,640]{1,0:T(8,128)(2,1)} %bitcast.16), custom_call_target="tpu_custom_call" | custom-call | tf_op jit(solution)/shard_map/combine/pallas_call | solution.py:204
  93.7 19.8 %all_to_all.21 = bf16[16,4,512]{2,1,0:T(4,128)(2,1)S(1)} all-to-all(bf16[16,4,512]{2,1,0:T(4,128)(2,1)S(1)} %reshape.142), channel_id=1, replica_groups=mesh['xl'=2,'y'=4,'core'=2,'xh'=2,'z'=8] {'xh','z'}, dimensions={0} | all-to-all | bytes 131072 | tf_op jit(solution)/shard_map/all_to_all | solution.py:285
  (76 shorter events, 16.2 us)
Async XLA Ops:
  0.0 34.8 %copy-start.8 = (bf16[4,128,512]{2,1,0:T(8,128)(2,1)S(1)}, bf16[4,128,512]{2,1,0:T(8,128)(2,1)}, u32[]{:S(2)}) copy-start(bf16[4,128,512]{2,1,0:T(8,128)(2,1)} %param.14) | copy-start | bytes 1572868
  1.7 13.3 %collective-permute-start = (bf16[80,512]{1,0:T(8,128)(2,1)S(1)}, bf16[80,512]{1,0:T(8,128)(2,1)S(1)}, u32[]{:S(2)}, u32[]{:S(2)}) collective-permute-start(bf16[80,512]{1,0:T(8,128)(2,1)S(1)} %fusion.1), channel_id=1, source_target_pairs={{0,16},{16,0},{1,17},{17,1},{2,18},{18,2},{3,19},{19,3},{4,20},{20... | collective-permute-start | bytes 245768 | tf_op jit(solution)/shard_map/ppermute | solution.py:218
  1.7 21.7 %collective-permute-start.7 = (bf16[80,512]{1,0:T(8,128)(2,1)S(1)}, bf16[80,512]{1,0:T(8,128)(2,1)S(1)}, u32[]{:S(2)}, u32[]{:S(2)}) collective-permute-start(bf16[80,512]{1,0:T(8,128)(2,1)S(1)} %fusion.1), channel_id=1, source_target_pairs={{0,136},{8,128},{128,8},{136,0},{1,137},{9,129},{129,9},{137,1},{2... | collective-permute-start | bytes 245768 | tf_op jit(solution)/shard_map/ppermute | solution.py:219
  4.6 19.0 %all-to-all-start = ((bf16[16,4,768]{2,1,0:T(4,128)(2,1)}), bf16[16,4,768]{2,1,0:T(4,128)(2,1)S(1)}, u32[]{:S(2)}, u32[]{:S(2)}) async-start(bf16[16,4,768]{2,1,0:T(4,128)(2,1)} %bitcast.19), calls=%async_computation | async-start | bytes 196608 | tf_op jit(solution)/shard_map/all_to_all | solution.py:270
  15.9 5.2 %collective-permute-start.1 = (bf16[144,512]{1,0:T(8,128)(2,1)S(1)}, bf16[144,512]{1,0:T(8,128)(2,1)S(1)}, u32[]{:S(2)}, u32[]{:S(2)}) collective-permute-start(bf16[144,512]{1,0:T(8,128)(2,1)S(1)} %maximum_maximum_fusion.refs_0_), channel_id=1, source_target_pairs={{0,1},{1,2},{2,3},{3,4},{4,5},{5,6},{6,7},{7,0},{16,23},{17,16},{1... | collective-permute-start | bytes 442376 | tf_op jit(solution)/shard_map/ppermute | solution.py:231
  21.2 11.9 %collective-permute-start.3 = (bf16[144,512]{1,0:T(8,128)(2,1)S(1)}, bf16[144,512]{1,0:T(8,128)(2,1)S(1)}, u32[]{:S(2)}, u32[]{:S(2)}) collective-permute-start(bf16[144,512]{1,0:T(8,128)(2,1)S(1)} %collective-permute-done.1.refs_1_), channel_id=1, source_target_pairs={{0,1},{1,2},{2,3},{3,4},{4,5},{5,6},{6,7},{7,0},{16,23},{17,16},{1... | collective-permute-start | bytes 442376 | tf_op jit(solution)/shard_map/ppermute | solution.py:231
  23.5 14.8 %collective-permute-start.8 = (bf16[80,512]{1,0:T(8,128)(2,1)S(1)}, bf16[80,512]{1,0:T(8,128)(2,1)S(1)}, u32[]{:S(2)}, u32[]{:S(2)}) collective-permute-start(bf16[80,512]{1,0:T(8,128)(2,1)S(1)} %collective-permute-done.7.refs_7_), channel_id=1, source_target_pairs={{0,16},{16,0},{1,17},{17,1},{2,18},{18,2},{3,19},{19,3},{4,20},{20... | collective-permute-start | bytes 245768 | tf_op jit(solution)/shard_map/ppermute | solution.py:218
  24.5 35.6 %all-to-all-start.1 = ((bf16[8,64,768]{2,1,0:T(8,128)(2,1)}), bf16[8,64,768]{2,1,0:T(8,128)(2,1)S(1)}, u32[]{:S(2)}, u32[]{:S(2)}) async-start(bf16[8,64,768]{2,1,0:T(8,128)(2,1)} %broadcast_in_dim.96), calls=%async_computation.1 | async-start | bytes 1572864 | tf_op jit(solution)/shard_map/all_to_all | solution.py:273
  29.0 10.8 %collective-permute-start.5 = (bf16[144,512]{1,0:T(8,128)(2,1)S(1)}, bf16[144,512]{1,0:T(8,128)(2,1)S(1)}, u32[]{:S(2)}, u32[]{:S(2)}) collective-permute-start(bf16[144,512]{1,0:T(8,128)(2,1)S(1)} %collective-permute-done.1.refs_1_), channel_id=1, source_target_pairs={{0,136},{8,128},{128,8},{136,0},{1,137},{9,129},{129,9},{137,1},{2... | collective-permute-start | bytes 442376 | tf_op jit(solution)/shard_map/ppermute | solution.py:219
  33.1 7.0 %collective-permute-start.2 = (bf16[144,512]{1,0:T(8,128)(2,1)S(1)}, bf16[144,512]{1,0:T(8,128)(2,1)S(1)}, u32[]{:S(2)}, u32[]{:S(2)}) collective-permute-start(bf16[144,512]{1,0:T(8,128)(2,1)S(1)} %collective-permute-done.1.refs_1_), channel_id=1, source_target_pairs={{0,16},{16,0},{1,17},{17,1},{2,18},{18,2},{3,19},{19,3},{4,20},{20... | collective-permute-start | bytes 442376 | tf_op jit(solution)/shard_map/ppermute | solution.py:218
  33.1 5.1 %collective-permute-start.9 = (bf16[144,512]{1,0:T(8,128)(2,1)S(1)}, bf16[144,512]{1,0:T(8,128)(2,1)S(1)}, u32[]{:S(2)}, u32[]{:S(2)}) collective-permute-start(bf16[144,512]{1,0:T(8,128)(2,1)S(1)} %collective-permute-done.3.refs_3_), channel_id=1, source_target_pairs={{0,1},{1,2},{2,3},{3,4},{4,5},{5,6},{6,7},{7,0},{16,23},{17,16},{1... | collective-permute-start | bytes 442376 | tf_op jit(solution)/shard_map/ppermute | solution.py:231
  35.8 9.2 %collective-permute-start.13 = (bf16[144,512]{1,0:T(8,128)(2,1)S(1)}, bf16[144,512]{1,0:T(8,128)(2,1)S(1)}, u32[]{:S(2)}, u32[]{:S(2)}) collective-permute-start(bf16[144,512]{1,0:T(8,128)(2,1)S(1)} %collective-permute-done.3.refs_3_), channel_id=1, source_target_pairs={{0,136},{8,128},{128,8},{136,0},{1,137},{9,129},{129,9},{137,1},{2... | collective-permute-start | bytes 442376 | tf_op jit(solution)/shard_map/ppermute | solution.py:219
  38.2 6.9 %collective-permute-start.4 = (bf16[144,512]{1,0:T(8,128)(2,1)S(1)}, bf16[144,512]{1,0:T(8,128)(2,1)S(1)}, u32[]{:S(2)}, u32[]{:S(2)}) collective-permute-start(bf16[144,512]{1,0:T(8,128)(2,1)S(1)} %collective-permute-done.3.refs_3_), channel_id=1, source_target_pairs={{0,16},{16,0},{1,17},{17,1},{2,18},{18,2},{3,19},{19,3},{4,20},{20... | collective-permute-start | bytes 442376 | tf_op jit(solution)/shard_map/ppermute | solution.py:218
  38.3 9.7 %collective-permute-start.11 = (bf16[144,512]{1,0:T(8,128)(2,1)S(1)}, bf16[144,512]{1,0:T(8,128)(2,1)S(1)}, u32[]{:S(2)}, u32[]{:S(2)}) collective-permute-start(bf16[144,512]{1,0:T(8,128)(2,1)S(1)} %collective-permute-done.9.refs_0_), channel_id=1, source_target_pairs={{0,136},{8,128},{128,8},{136,0},{1,137},{9,129},{129,9},{137,1},{2... | collective-permute-start | bytes 442376 | tf_op jit(solution)/shard_map/ppermute | solution.py:219
  39.8 8.1 %collective-permute-start.6 = (bf16[144,512]{1,0:T(8,128)(2,1)S(1)}, bf16[144,512]{1,0:T(8,128)(2,1)S(1)}, u32[]{:S(2)}, u32[]{:S(2)}) collective-permute-start(bf16[144,512]{1,0:T(8,128)(2,1)S(1)} %collective-permute-done.5.refs_5_), channel_id=1, source_target_pairs={{0,16},{16,0},{1,17},{17,1},{2,18},{18,2},{3,19},{19,3},{4,20},{20... | collective-permute-start | bytes 442376 | tf_op jit(solution)/shard_map/ppermute | solution.py:218
  40.0 6.1 %collective-permute-start.15 = (bf16[80,512]{1,0:T(8,128)(2,1)}, bf16[80,512]{1,0:T(8,128)(2,1)}, u32[]{:S(2)}, u32[]{:S(2)}) collective-permute-start(bf16[80,512]{1,0:T(8,128)(2,1)} %pad_maximum_fusion.1), channel_id=1, source_target_pairs={{0,1},{1,2},{2,3},{3,4},{4,5},{5,6},{6,7},{7,0},{16,23},{17,16},{1... | collective-permute-start | bytes 245768 | tf_op jit(solution)/shard_map/ppermute | solution.py:231
  45.1 10.5 %collective-permute-start.10 = (bf16[144,512]{1,0:T(8,128)(2,1)S(1)}, bf16[144,512]{1,0:T(8,128)(2,1)S(1)}, u32[]{:S(2)}, u32[]{:S(2)}) collective-permute-start(bf16[144,512]{1,0:T(8,128)(2,1)S(1)} %collective-permute-done.9.refs_0_), channel_id=1, source_target_pairs={{0,16},{16,0},{1,17},{17,1},{2,18},{18,2},{3,19},{19,3},{4,20},{20... | collective-permute-start | bytes 442376 | tf_op jit(solution)/shard_map/ppermute | solution.py:218
  45.2 10.4 %collective-permute-start.14 = (bf16[144,512]{1,0:T(8,128)(2,1)S(1)}, bf16[144,512]{1,0:T(8,128)(2,1)S(1)}, u32[]{:S(2)}, u32[]{:S(2)}) collective-permute-start(bf16[144,512]{1,0:T(8,128)(2,1)S(1)} %collective-permute-done.13.refs_4_), channel_id=1, source_target_pairs={{0,16},{16,0},{1,17},{17,1},{2,18},{18,2},{3,19},{19,3},{4,20},{20... | collective-permute-start | bytes 442376 | tf_op jit(solution)/shard_map/ppermute | solution.py:218
  46.1 5.9 %collective-permute-start.17 = (bf16[80,512]{1,0:T(8,128)(2,1)}, bf16[80,512]{1,0:T(8,128)(2,1)S(1)}, u32[]{:S(2)}, u32[]{:S(2)}) collective-permute-start(bf16[80,512]{1,0:T(8,128)(2,1)} %collective-permute-done.15.refs_6_), channel_id=1, source_target_pairs={{0,136},{8,128},{128,8},{136,0},{1,137},{9,129},{129,9},{137,1},{2... | collective-permute-start | bytes 245768 | tf_op jit(solution)/shard_map/ppermute | solution.py:219
  48.0 7.6 %collective-permute-start.12 = (bf16[144,512]{1,0:T(8,128)(2,1)S(1)}, bf16[144,512]{1,0:T(8,128)(2,1)S(1)}, u32[]{:S(2)}, u32[]{:S(2)}) collective-permute-start(bf16[144,512]{1,0:T(8,128)(2,1)S(1)} %collective-permute-done.11.refs_2_), channel_id=1, source_target_pairs={{0,16},{16,0},{1,17},{17,1},{2,18},{18,2},{3,19},{19,3},{4,20},{20... | collective-permute-start | bytes 442376 | tf_op jit(solution)/shard_map/ppermute | solution.py:218
  48.0 7.6 %collective-permute-start.16 = (bf16[80,512]{1,0:T(8,128)(2,1)}, bf16[80,512]{1,0:T(8,128)(2,1)S(1)}, u32[]{:S(2)}, u32[]{:S(2)}) collective-permute-start(bf16[80,512]{1,0:T(8,128)(2,1)} %collective-permute-done.15.refs_6_), channel_id=1, source_target_pairs={{0,16},{16,0},{1,17},{17,1},{2,18},{18,2},{3,19},{19,3},{4,20},{20... | collective-permute-start | bytes 245768 | tf_op jit(solution)/shard_map/ppermute | solution.py:218
  52.0 3.6 %collective-permute-start.18 = (bf16[80,512]{1,0:T(8,128)(2,1)S(1)}, bf16[80,512]{1,0:T(8,128)(2,1)S(1)}, u32[]{:S(2)}, u32[]{:S(2)}) collective-permute-start(bf16[80,512]{1,0:T(8,128)(2,1)S(1)} %collective-permute-done.17.refs_8_), channel_id=1, source_target_pairs={{0,16},{16,0},{1,17},{17,1},{2,18},{18,2},{3,19},{19,3},{4,20},{20... | collective-permute-start | bytes 245768 | tf_op jit(solution)/shard_map/ppermute | solution.py:218
  60.1 1.6 %copy-start.1 = (bf16[4,1024,192]{2,1,0:T(8,128)(2,1)S(1)}, bf16[4,1024,192]{2,1,0:T(8,128)(2,1)}, u32[]{:S(2)}) copy-start(bf16[4,1024,192]{2,1,0:T(8,128)(2,1)} %copy-done) | copy-start | bytes 4718596
  61.7 1.6 %copy-start.3 = (bf16[4,1024,192]{2,1,0:T(8,128)(2,1)S(1)}, bf16[4,1024,192]{2,1,0:T(8,128)(2,1)}, u32[]{:S(2)}) copy-start(bf16[4,1024,192]{2,1,0:T(8,128)(2,1)} %copy-done.2) | copy-start | bytes 4718596
  (6 other events, 7.1 us)

commit v3 on v2

v3 whole, which is shorter than its diff:
```python
import functools
import math

import jax
import jax.numpy as jnp
from jax import lax
from jax.experimental import pallas as pl
from jax.experimental.pallas import tpu as pltpu
from jax.sharding import Mesh
from jax.sharding import PartitionSpec as P

L = 512
QN = 128
QR = 64
QD = QN + QR
VD = 128
BLOCK = 128
HEADS = 4
NEG = -1e30
SCALE = 1.0 / math.sqrt(QD)
LOG2E = math.log2(math.e)

AXES = ("xl", "y", "core", "xh", "z")
CHIPS = ("xl", "y", "xh", "z")
XLN, YN, CN, XHN, ZN = 2, 4, 2, 2, 8
CELLS = XLN * YN
GRP = XHN * ZN
PER = 64
TOK = 4
PEERS = CELLS * GRP
ROWS = PEERS * TOK
MSG = HEADS * VD
EXT = MSG + 128

VAT = 256
QT = 256
KT = 512

FULL = 144
HALF = 80


def chunk(swap, other, step, full):
    return [(swap, other, step, j) for j in range(2 if full else 1)]


GROUP_A = [(0, 0, 0, True)]
GROUP_A += [(0, o, s, True) for s in (1, 2) for o in (0, 1)]
GROUP_A += [(1, o, 1, True) for o in (0, 1)]
GROUP_A += [(1, o, 0, False) for o in (0, 1)]
GROUP_B = [(x, o, 3, True) for x in (0, 1) for o in (0, 1)]
GROUP_B += [(1, o, 2, True) for o in (0, 1)]
GROUP_B += [(x, o, 4, False) for x in (0, 1) for o in (0, 1)]
PIECES = [p for c in GROUP_A + GROUP_B for p in chunk(*c)]
SLOTS = len(PIECES)
KEYS = SLOTS * PER
PART = KEYS // 2


def unpack(chunks, lat, put_rope):
    base = 0
    for ref in chunks:
        n = 2 * PER if ref.shape[0] == FULL else PER
        lat[base : base + n, :] = ref[0:n, :]
        for r in range(n // 16):
            put_rope(base + r * 16, ref[n : n + 16, r * QR : (r + 1) * QR])
        base += n


def project_kernel(count, *refs):
    chunks, (w_ref, o_ref, lat) = refs[:count], refs[count:]

    def put_rope(row, rope):
        for h in range(HEADS):
            o_ref[h, row : row + 16, QN:QD] = rope

    unpack(chunks, lat, put_rope)
    for h in range(HEADS):
        for i in range(PART // KT):
            rows = slice(i * KT, (i + 1) * KT)
            kv = jnp.dot(lat[rows, :], w_ref[h], preferred_element_type=jnp.float32)
            kv = kv.astype(jnp.bfloat16)
            o_ref[h, rows, 0:QN] = kv[:, 0:QN]
            o_ref[h, rows, VAT:] = kv[:, QN:]


def project(chunks, weights):
    return pl.pallas_call(
        functools.partial(project_kernel, len(chunks)),
        out_shape=jax.ShapeDtypeStruct((HEADS, PART, VAT + VD), jnp.bfloat16),
        scratch_shapes=[pltpu.VMEM((PART, L), jnp.bfloat16)],
        compiler_params=pltpu.CompilerParams(vmem_limit_bytes=60 * 1024 * 1024),
        cost_estimate=pl.CostEstimate(
            flops=1_100_000_000, bytes_accessed=5_000_000, transcendentals=0
        ),
        name="project",
    )(*chunks, weights)


def attend_kernel(count, q_ref, ka_ref, *refs):
    chunks, refs = refs[:count], refs[count:]
    w_ref, thr_ref, o_ref, qs, ka, lat, side, kb, sco, stats, sems, more = refs
    h = pl.program_id(0)
    heads = [pltpu.make_async_copy(ka_ref.at[g], ka.at[g], sems.at[g]) for g in range(HEADS)]
    loads = []
    base = 0
    for j, ref in enumerate(chunks):
        n = 2 * PER if ref.shape[0] == FULL else PER
        loads.append(
            pltpu.make_async_copy(ref.at[0:n], lat.at[base : base + n], more.at[2 * j])
        )
        loads.append(pltpu.make_async_copy(ref.at[n : n + 16], side.at[j], more.at[2 * j + 1]))
        base += n

    @pl.when(h == 0)
    def _():
        for copy in [heads[0], *loads, *heads[1:]]:
            copy.start()
        for g in range(HEADS):
            qs[g] = q_ref[:, g * QD : (g + 1) * QD]
        stats[...] = jnp.zeros_like(stats)
        for copy in [heads[0], *loads]:
            copy.wait()
        row = 0
        for j, ref in enumerate(chunks):
            for r in range((2 * PER if ref.shape[0] == FULL else PER) // 16):
                kb[row : row + 16, QN:QD] = side[j, :, r * QR : (r + 1) * QR]
                row += 16

    for g in range(1, HEADS):

        @pl.when(h == g)
        def _():
            heads[g].wait()

    for i in range(PART // KT):
        rows = slice(i * KT, (i + 1) * KT)
        kv = jnp.dot(lat[rows, :], w_ref[0], preferred_element_type=jnp.float32)
        kv = kv.astype(jnp.bfloat16)
        kb[rows, 0:QN] = kv[:, 0:QN]
        kb[rows, VAT:] = kv[:, QN:]
    tiles = [(r, slice(i * KT, (i + 1) * KT)) for r in (ka.at[h], kb) for i in range(PART // KT)]
    lane = lax.broadcasted_iota(jnp.int32, (QT, 128), 1)
    off = lax.broadcasted_iota(jnp.int32, (64, 128), 0).astype(jnp.float32)
    for t in range(ROWS // QT):
        q = qs[h, pl.ds(t * QT, QT), :]
        top = jnp.full((QT, 128), NEG, jnp.float32)
        for i, (ref, rows) in enumerate(tiles):
            s = lax.dot_general(
                q, ref[rows, 0:QD], (((1,), (1,)), ((), ())), preferred_element_type=jnp.float32
            )
            parts = []
            for b in range(QT // 64):
                thr = thr_ref[pl.ds(t * (QT // 64) + b, 1), pl.ds(i * KT, KT)]
                cols = []
                for c in range(KT // 128):
                    piece = s[b * 64 : (b + 1) * 64, c * 128 : (c + 1) * 128]
                    cols.append(jnp.where(off >= thr[:, c * 128 : (c + 1) * 128], piece, NEG))
                parts.append(functools.reduce(jnp.maximum, cols))
                for c in range(KT // 128):
                    sco[t, b * 64 : (b + 1) * 64, i * KT + c * 128 : i * KT + (c + 1) * 128] = cols[c]
            top = jnp.maximum(top, jnp.concatenate(parts, axis=0))
        m = jnp.max(top, axis=1, keepdims=True)
        mc = m * (SCALE * LOG2E)
        total = jnp.zeros((QT, 128), jnp.float32)
        acc = jnp.zeros((QT, VD), jnp.float32)
        for i, (ref, rows) in enumerate(tiles):
            p = jnp.exp2(sco[t, :, pl.ds(i * KT, KT)] * (SCALE * LOG2E) - mc)
            for c in range(KT // 128):
                total = total + p[:, c * 128 : (c + 1) * 128]
            acc = acc + jnp.dot(
                p.astype(jnp.bfloat16), ref[rows, VAT:], preferred_element_type=jnp.float32
            )
        den = jnp.sum(total, axis=1, keepdims=True)
        lse = m * SCALE + jnp.log(den)
        o_ref[pl.ds(t * QT, QT), pl.ds(pl.multiple_of(h * VD, VD), VD)] = (acc / den).astype(
            jnp.bfloat16
        )
        hi = lse.astype(jnp.bfloat16).astype(jnp.float32)
        mid = (lse - hi).astype(jnp.bfloat16).astype(jnp.float32)
        low = lse - hi - mid
        old = stats[pl.ds(t * QT, QT), :]
        old = jnp.where(lane == 3 * h, hi, old)
        old = jnp.where(lane == 3 * h + 1, mid, old)
        stats[pl.ds(t * QT, QT), :] = jnp.where(lane == 3 * h + 2, low, old)

    @pl.when(h == HEADS - 1)
    def _():
        o_ref[:, MSG:] = stats[...].astype(jnp.bfloat16)


def attend(q, ka, chunks, weights, thr):
    full = lambda shape: pl.BlockSpec(shape, lambda h: tuple(0 for _ in shape))
    head = lambda shape: pl.BlockSpec((1, *shape), lambda h: (h, 0, 0))
    return pl.pallas_call(
        functools.partial(attend_kernel, len(chunks)),
        grid=(HEADS,),
        out_shape=jax.ShapeDtypeStruct((ROWS, EXT), jnp.bfloat16),
        in_specs=[
            full((ROWS, HEADS * QD)),
            pl.BlockSpec(memory_space=pltpu.HBM),
            *(pl.BlockSpec(memory_space=pltpu.HBM) for _ in chunks),
            head((L, QN + VD)),
            full((CELLS, KEYS)),
        ],
        out_specs=full((ROWS, EXT)),
        scratch_shapes=[
            pltpu.VMEM((HEADS, ROWS, QD), jnp.bfloat16),
            pltpu.VMEM((HEADS, PART, VAT + VD), jnp.bfloat16),
            pltpu.VMEM((PART, L), jnp.bfloat16),
            pltpu.VMEM((len(chunks), 16, L), jnp.bfloat16),
            pltpu.VMEM((PART, VAT + VD), jnp.bfloat16),
            pltpu.VMEM((ROWS // QT, QT, KEYS), jnp.float32),
            pltpu.VMEM((ROWS, 128), jnp.float32),
            pltpu.SemaphoreType.DMA((HEADS,)),
            pltpu.SemaphoreType.DMA((2 * len(chunks),)),
        ],
        compiler_params=pltpu.CompilerParams(vmem_limit_bytes=60 * 1024 * 1024),
        cost_estimate=pl.CostEstimate(
            flops=4_000_000_000, bytes_accessed=8_000_000, transcendentals=4_200_000
        ),
        name="attend",
    )(q, ka, *chunks, weights, thr)


def combine_kernel(x_ref, o_ref):
    n = GRP * TOK
    ext = [x_ref[pl.ds(c * n, n), MSG:].astype(jnp.float32) for c in range(CELLS)]
    for h in range(HEADS):
        j = 3 * h
        lse = [e[:, j : j + 1] + e[:, j + 1 : j + 2] + e[:, j + 2 : j + 3] for e in ext]
        top = functools.reduce(jnp.maximum, lse)
        part = [jnp.exp(v - top) for v in lse]
        scale = 1.0 / functools.reduce(jnp.add, part)
        acc = jnp.zeros((n, VD), jnp.float32)
        for c in range(CELLS):
            acc = acc + x_ref[pl.ds(c * n, n), pl.ds(h * VD, VD)].astype(jnp.float32) * (
                part[c] * scale
            )
        o_ref[:, :, pl.ds(h * VD, VD)] = acc.reshape(GRP, TOK, VD).astype(jnp.bfloat16)


def combine(x):
    return pl.pallas_call(
        combine_kernel,
        out_shape=jax.ShapeDtypeStruct((GRP, TOK, MSG), jnp.bfloat16),
        name="combine",
    )(x)


def pack_kernel(lat_ref, rope_ref, o_ref):
    o_ref[0:PER, :] = lat_ref[...]
    for r in range(L // QR):
        b = r % (PER // 16)
        o_ref[PER:HALF, r * QR : (r + 1) * QR] = rope_ref[b * 16 : (b + 1) * 16, :]


def pack(latents, key_rope):
    return pl.pallas_call(
        pack_kernel, out_shape=jax.ShapeDtypeStruct((HALF, L), jnp.bfloat16), name="pack"
    )(latents, key_rope)


def shift(n, k):
    return [(i, (i + k) % n) for i in range(n)]


def gather_keys(latents, key_rope):
    near = [(a * 2 + b, (1 - a) * 2 + 1 - b) for a in range(2) for b in range(2)]
    def round_z(x, n):
        up = [(i, (i + n) % ZN) for i in range(ZN)]
        down = [(ZN + i, ZN + (i - n) % ZN) for i in range(ZN)]
        return lax.ppermute(x, ("core", "z"), up + down)

    to_core = lambda x: lax.ppermute(x, "core", shift(CN, 1))
    to_near = lambda x: lax.ppermute(x, ("xl", "xh"), near)
    piece = pack(latents, key_rope)
    mate = to_core(piece)
    got = {}
    got[1, 0, 0] = to_near(piece)
    side = jnp.concatenate([piece[PER:, : L // 2], mate[PER:, : L // 2]], axis=1)
    now = jnp.concatenate([piece[:PER], mate[:PER], side])
    got[0, 0, 0] = now
    got[0, 0, 1] = round_z(now, 1)
    got[0, 0, 2] = now = round_z(now, 2)
    got[0, 0, 3] = round_z(now, 1)
    got[0, 0, 4] = round_z(jnp.concatenate([now[:PER], now[2 * PER :]]), 2)
    for s in range(1, 5):
        got[1, 0, s] = to_near(got[0, 0, s])
    for x in range(2):
        for s in range(5):
            if (x, s) != (0, 0):
                got[x, 1, s] = to_core(got[x, 0, s])
    pick = lambda group: [got[x, o, s] for x, o, s, _ in group]
    return pick(GROUP_A), pick(GROUP_B), now


def thresholds(pattern, stripe):
    xl, y, core = lax.axis_index("xl"), lax.axis_index("y"), lax.axis_index("core")
    xh, z = lax.axis_index("xh"), lax.axis_index("z")
    swap, other, step, inner = (jnp.asarray([p[i] for p in PIECES], jnp.int32) for i in range(4))
    lane = core ^ other
    k = lane ^ inner
    zz = (z + jnp.where(lane == 1, step, ZN - step)) % ZN
    cell = ((xl ^ swap) * YN + y) * CN + k
    place = cell * GRP + (xh ^ swap) * ZN + zz
    block = place * PER // BLOCK
    base = place * PER % BLOCK
    nb = stripe.shape[0]
    every = jnp.arange(nb, dtype=jnp.int32)
    kb = jnp.sum(jnp.where(block[:, None] == every[None, :], stripe[None, :], 0), axis=1)
    hit = jnp.sum(jnp.where(kb[None, :, None] == every[None, None, :], pattern[:, None, :], 0), axis=2)
    qb = nb - CELLS + jnp.arange(CELLS, dtype=jnp.int32)[:, None]
    see = (kb[None, :] < qb) & (hit == 1)
    offset = base[:, None] + jnp.arange(PER, dtype=jnp.int32)[None, :]
    thr = jnp.where(
        see[:, :, None], 0, jnp.where((kb[None, :] == qb)[:, :, None], offset[None], 4 * BLOCK)
    )
    return (thr - core * 64).reshape(CELLS, KEYS).astype(jnp.float32)


def body(queries, latents, key_rope, key_up, value_up, pattern, stripe):
    cells = ("xl", "y")
    groups = ("xh", "z")
    first, second, mark = gather_keys(latents, key_rope)
    send = queries.reshape(TOK, GRP, HEADS * QD).transpose(1, 0, 2)
    send, _ = lax.optimization_barrier((send, first[0]))
    mine = lax.all_to_all(send, groups, split_axis=0, concat_axis=0, tiled=True)
    mine = mine.reshape(GRP * TOK, HEADS * QD)
    send = jnp.broadcast_to(mine[None], (CELLS, *mine.shape))
    q = lax.all_to_all(send, cells, split_axis=0, concat_axis=0, tiled=True)
    q = q.reshape(ROWS, HEADS * QD)
    key_up, value_up, pattern, stripe, _ = lax.optimization_barrier(
        (key_up, value_up, pattern, stripe, mark)
    )
    weights = jnp.concatenate([key_up.transpose(0, 2, 1), value_up], axis=2)
    thr = thresholds(pattern, stripe)
    part = attend(q, project(first, weights), second, weights, thr)
    back = lax.all_to_all(
        part.reshape(CELLS, GRP * TOK, EXT), cells, split_axis=0, concat_axis=0, tiled=True
    )
    out = lax.all_to_all(combine(back.reshape(ROWS, EXT)), groups, split_axis=0, concat_axis=0, tiled=True)
    return out.transpose(1, 0, 2).reshape(TOK, GRP * MSG)


def solution(mesh):
    fine = Mesh(mesh.devices.reshape(XLN, YN, CN, XHN, ZN), AXES)
    in_specs = (
        P(AXES, None),
        P(AXES, None),
        P(AXES, None),
        P(("xh", "z"), None, None),
        P(("xh", "z"), None, None),
        P(),
        P(),
    )
    return jax.shard_map(body, mesh=fine, in_specs=in_specs, out_specs=P(AXES, None), check_vma=False)
```

time: 115 us -> 102 us (0.89)
  local copies, waits for them, and re-layouts: 15.4 us -> 5.74 us
  Pallas kernels: 14.2 us -> 22.1 us
  blocking collectives: 36.1 us -> 30.7 us
  waiting for transfers between devices: 9.08 us -> 4.77 us
  other arithmetic: 6.31 us -> 4.46 us
    unnamed x20 -> x37, local copies, waits for them, and re-layouts: 11.9 us -> 2.23 us
    pallas_call x2 -> x3, Pallas kernels: 10.8 us -> 17.5 us  [the longest x1 13.7 us: attend(): pl.pallas_call(functools.partial(attend_kernel, len(chunks)), grid=(HEADS...]
    all_to_all x1, blocking collectives: 19.8 us -> 14.2 us  [body(): lax.all_to_all(combine(back.reshape(ROWS, EXT)), groups, split_axis=0, co...]
    ppermute x4, waiting for transfers between devices: 5.55 us -> 0.01 us  [round_z(): return lax.ppermute(x, ('core', 'z'), up + down)]
    all_to_all x1, starting transfers between devices: 8.82 us -> 4.91 us  [body(): mine = lax.all_to_all(send, groups, split_axis=0, concat_axis=0, tiled=True)]
    ppermute x4, starting transfers between devices: 8.35 us -> 11.6 us  [round_z(): return lax.ppermute(x, ('core', 'z'), up + down)]
    reshape x3 -> x0, local copies, waits for them, and re-layouts: 1.73 us -> none  [the longest x2 0.87 us: gather_keys(): key_rope.reshape(PER // 16, 16, QR).transpose(1, 0, 2)]
    concatenate x2 -> x1, other arithmetic: 1.48 us -> 0.01 us  [gather_keys(): got[0, 0, 4] = round_z(jnp.concatenate([now[:PER], now[2 * PER:]]), 2)]
  transfers between devices with their start and end apart: 21 -> 21, of which waited for: 4 -> 2; matrix products, arithmetic and copies ran while one was open for 7% -> 8% of each run, Pallas kernels for 3% -> 5%
where the time goes in v3:
time: 102 us; the launch traced here: 101 us
  starting transfers between devices  33.3 us (33%)
  blocking collectives  30.7 us (30%)
  Pallas kernels  22.1 us (22%)
  local copies, waits for them, and re-layouts  5.74 us (6%)
  waiting for transfers between devices  4.77 us (5%)
  other arithmetic  4.46 us (4%)
    all_to_all x1, blocking collectives, body(): lax.all_to_all(part.reshape(CELLS, GRP * TOK, EXT), cells, split_axis=0,...  16.5 us
    all_to_all x1, blocking collectives, body(): lax.all_to_all(combine(back.reshape(ROWS, EXT)), groups, split_axis=0, co...  14.2 us
    pallas_call x1, Pallas kernels, attend(): pl.pallas_call(functools.partial(attend_kernel, len(chunks)), grid=(HEADS...  13.7 us
    ppermute x4, starting transfers between devices, round_z(): return lax.ppermute(x, ('core', 'z'), up + down)  11.6 us
    ppermute x5, starting transfers between devices, gather_keys(): to_near = lambda x: lax.ppermute(x, ('xl', 'xh'), near)  10.8 us
    all_to_all x1, starting transfers between devices, body(): mine = lax.all_to_all(send, groups, split_axis=0, concat_axis=0, tiled=True)  4.91 us
    ppermute x5, waiting for transfers between devices, gather_keys(): to_near = lambda x: lax.ppermute(x, ('xl', 'xh'), near)  4.73 us
    pallas_call x1, Pallas kernels, project(): pl.pallas_call(functools.partial(project_kernel, len(chunks)), out_shape=...  4.65 us
  transfers between devices with their start and end apart: 21, of which 2 were waited for; matrix products, arithmetic and copies ran while one was open for 8% of the time, Pallas kernels for 5%

profile of v3, /device:TPU:32, one launch (start us, length us, event | category | flops | bytes accessed | tf_op | source)
XLA Modules:
  0.0 101.5 jit_solution(5533288879914610222)
XLA Ops:
  0.0 1.5 %pack.1 = bf16[80,512]{1,0:T(8,128)(2,1)} custom-call(bf16[64,512]{1,0:T(8,128)(2,1)} %lat_ref.1, bf16[64,64]{1,0:T(8,128)(2,1)} %rope_ref.1), custom_call_target="tpu_custom_call" | custom-call | tf_op jit(solution)/shard_map/pack/pallas_call | solution.py:259
  1.5 2.8 %collective-permute-start.7 = (bf16[80,512]{1,0:T(8,128)(2,1)}, bf16[80,512]{1,0:T(8,128)(2,1)S(1)}, u32[]{:S(2)}, u32[]{:S(2)}) collective-permute-start(bf16[80,512]{1,0:T(8,128)(2,1)} %pack.1), channel_id=1, source_target_pairs={{0,136},{8,128},{128,8},{136,0},{1,137},{9,129},{129,9},{137,1},{2... | collective-permute-start | bytes 245768 | tf_op jit(solution)/shard_map/ppermute | solution.py:276
  5.8 0.8 slice.24
  6.7 3.3 %collective-permute-start.3 = (bf16[144,512]{1,0:T(8,128)(2,1)S(1)}, bf16[144,512]{1,0:T(8,128)(2,1)S(1)}, u32[]{:S(2)}, u32[]{:S(2)}) collective-permute-start(bf16[144,512]{1,0:T(8,128)(2,1)S(1)} %maximum_maximum_fusion.refs_0_), channel_id=1, source_target_pairs={{0,2},{1,3},{2,4},{3,5},{4,6},{5,7},{6,0},{7,1},{16,22},{17,23},{1... | collective-permute-start | bytes 442376 | tf_op jit(solution)/shard_map/ppermute | solution.py:273
  10.3 3.2 %collective-permute-start.1 = (bf16[144,512]{1,0:T(8,128)(2,1)S(1)}, bf16[144,512]{1,0:T(8,128)(2,1)S(1)}, u32[]{:S(2)}, u32[]{:S(2)}) collective-permute-start(bf16[144,512]{1,0:T(8,128)(2,1)S(1)} %maximum_maximum_fusion.refs_0_), channel_id=1, source_target_pairs={{0,1},{1,2},{2,3},{3,4},{4,5},{5,6},{6,7},{7,0},{16,23},{17,16},{1... | collective-permute-start | bytes 442376 | tf_op jit(solution)/shard_map/ppermute | solution.py:273
  13.5 4.9 %all-to-all-start = ((bf16[16,4,768]{2,1,0:T(4,128)(2,1)}), bf16[16,4,768]{2,1,0:T(4,128)(2,1)S(1)}, u32[]{:S(2)}, u32[]{:S(2)}) async-start(bf16[16,4,768]{2,1,0:T(4,128)(2,1)} %bitcast.15), calls=%async_computation | async-start | bytes 196608 | tf_op jit(solution)/shard_map/all_to_all | solution.py:328
  18.6 2.4 %collective-permute-start.15 = (bf16[80,512]{1,0:T(8,128)(2,1)S(1)}, bf16[80,512]{1,0:T(8,128)(2,1)}, u32[]{:S(2)}, u32[]{:S(2)}) collective-permute-start(bf16[80,512]{1,0:T(8,128)(2,1)S(1)} %pad_maximum_fusion.1), channel_id=1, source_target_pairs={{0,2},{1,3},{2,4},{3,5},{4,6},{5,7},{6,0},{7,1},{16,22},{17,23},{1... | collective-permute-start | bytes 245768 | tf_op jit(solution)/shard_map/ppermute | solution.py:273
  21.1 0.8 select_reduce_fusion.1
  22.0 2.7 %collective-permute-start.9 = (bf16[144,512]{1,0:T(8,128)(2,1)S(1)}, bf16[144,512]{1,0:T(8,128)(2,1)}, u32[]{:S(2)}, u32[]{:S(2)}) collective-permute-start(bf16[144,512]{1,0:T(8,128)(2,1)S(1)} %collective-permute-done.3.refs_3_), channel_id=1, source_target_pairs={{0,1},{1,2},{2,3},{3,4},{4,5},{5,6},{6,7},{7,0},{16,23},{17,16},{1... | collective-permute-start | bytes 442376 | tf_op jit(solution)/shard_map/ppermute | solution.py:273
  24.7 0.9 select_reduce_fusion
  25.6 2.7 %collective-permute-start.5 = (bf16[144,512]{1,0:T(8,128)(2,1)S(1)}, bf16[144,512]{1,0:T(8,128)(2,1)S(1)}, u32[]{:S(2)}, u32[]{:S(2)}) collective-permute-start(bf16[144,512]{1,0:T(8,128)(2,1)S(1)} %collective-permute-done.1.refs_1_), channel_id=1, source_target_pairs={{0,136},{8,128},{128,8},{136,0},{1,137},{9,129},{129,9},{137,1},{2... | collective-permute-start | bytes 442376 | tf_op jit(solution)/shard_map/ppermute | solution.py:276
  29.0 0.9 broadcast_in_dim.90
  29.9 4.5 %all-to-all-start.1 = ((bf16[8,64,768]{2,1,0:T(8,128)(2,1)}), bf16[8,64,768]{2,1,0:T(8,128)(2,1)S(1)}, u32[]{:S(2)}, u32[]{:S(2)}) async-start(bf16[8,64,768]{2,1,0:T(8,128)(2,1)} %broadcast_in_dim.90), calls=%async_computation.1 | async-start | bytes 1572864 | tf_op jit(solution)/shard_map/all_to_all | solution.py:331
  34.7 1.9 %collective-permute-start.13 = (bf16[144,512]{1,0:T(8,128)(2,1)S(1)}, bf16[144,512]{1,0:T(8,128)(2,1)}, u32[]{:S(2)}, u32[]{:S(2)}) collective-permute-start(bf16[144,512]{1,0:T(8,128)(2,1)S(1)} %collective-permute-done.3.refs_3_), channel_id=1, source_target_pairs={{0,136},{8,128},{128,8},{136,0},{1,137},{9,129},{129,9},{137,1},{2... | collective-permute-start | bytes 442376 | tf_op jit(solution)/shard_map/ppermute | solution.py:276
  36.8 1.2 %collective-permute-start.11 = (bf16[144,512]{1,0:T(8,128)(2,1)}, bf16[144,512]{1,0:T(8,128)(2,1)}, u32[]{:S(2)}, u32[]{:S(2)}) collective-permute-start(bf16[144,512]{1,0:T(8,128)(2,1)} %collective-permute-done.9.refs_0_), channel_id=1, source_target_pairs={{0,136},{8,128},{128,8},{136,0},{1,137},{9,129},{129,9},{137,1},{2... | collective-permute-start | bytes 442376 | tf_op jit(solution)/shard_map/ppermute | solution.py:276
  39.0 2.1 %collective-permute-start.17 = (bf16[80,512]{1,0:T(8,128)(2,1)}, bf16[80,512]{1,0:T(8,128)(2,1)S(1)}, u32[]{:S(2)}, u32[]{:S(2)}) collective-permute-start(bf16[80,512]{1,0:T(8,128)(2,1)} %collective-permute-done.15.refs_6_), channel_id=1, source_target_pairs={{0,136},{8,128},{128,8},{136,0},{1,137},{9,129},{129,9},{137,1},{2... | collective-permute-start | bytes 245768 | tf_op jit(solution)/shard_map/ppermute | solution.py:276
  41.1 1.6 %collective-permute-done.13.refs_4_ = bf16[144,512]{1,0:T(8,128)(2,1)} collective-permute-done((bf16[144,512]{1,0:T(8,128)(2,1)S(1)}, bf16[144,512]{1,0:T(8,128)(2,1)}, u32[]{:S(2)}, u32[]{:S(2)}) %collective-permute-start.13) | collective-permute-done | bytes 147488 | tf_op jit(solution)/shard_map/ppermute | solution.py:276
  42.7 3.2 %collective-permute-done.11.refs_2_ = bf16[144,512]{1,0:T(8,128)(2,1)} collective-permute-done((bf16[144,512]{1,0:T(8,128)(2,1)}, bf16[144,512]{1,0:T(8,128)(2,1)}, u32[]{:S(2)}, u32[]{:S(2)}) %collective-permute-start.11) | collective-permute-done | bytes 147488 | tf_op jit(solution)/shard_map/ppermute | solution.py:276
  45.9 1.1 %pad_maximum_fusion.refs_9_.refs_10_ = bf16[4,512,256]{2,1,0:T(8,128)(2,1)} fusion(bf16[4,512,128]{2,1,0:T(8,128)(2,1)S(1)} %copy-done.3, bf16[4,512,128]{2,1,0:T(8,128)(2,1)S(1)} %bitcast.11), kind=kLoop, calls=%fused_computation | loop fusion | flops 2097152 | bytes 2097152 | tf_op jit(solution)/shard_map/concatenate | solution.py:336
  48.4 4.6 %project.1.ka_ref = bf16[4,1024,384]{2,1,0:T(8,128)(2,1)} custom-call(bf16[144,512]{1,0:T(8,128)(2,1)} %copy-done.1, bf16[144,512]{1,0:T(8,128)(2,1)} %copy-done.5, bf16[144,512]{1,0:T(8,128)(2,1)} %copy-done.7, bf16[144,512]{1,0:T(8,128)(2,1)} %copy-done.4, bf16[144,512]{1,0:T(8,128)(2,1)} %copy-done.8, bf16[144,512]{1,0:T(8,128)(2,1)} %copy-done.6, ...), custom_call_target="tpu_custom_call" | custom-call | flops 1100000000 | bytes 5000000 | tf_op jit(solution)/shard_map/project/pallas_call | solution.py:88
  54.2 13.7 %attend.1 = bf16[512,640]{1,0:T(8,128)(2,1)} custom-call(bf16[512,768]{1,0:T(8,128)(2,1)} %bitcast.12, bf16[4,1024,384]{2,1,0:T(8,128)(2,1)} %project.1.ka_ref, bf16[144,512]{1,0:T(8,128)(2,1)} %collective-permute-done.9.refs_0_, bf16[144,512]{1,0:T(8,128)(2,1)} %copy-done.12, bf16[144,512]{1,0:T(8,128)(2,1)} %collective-permute-done.11.refs_2_, ...), custom_call_target="tpu_custom_call" | custom-call | flops 4000000000 | bytes 8000000 | tf_op jit(solution)/shard_map/attend/pallas_call | solution.py:195
  67.9 16.5 %all_to_all.20 = bf16[8,64,640]{2,1,0:T(8,128)(2,1)} all-to-all(bf16[8,64,640]{2,1,0:T(8,128)(2,1)} %bitcast.13), channel_id=1, replica_groups=mesh['xl'=2,'y'=4,'core'=2,'xh'=2,'z'=8] {'xl','y'}, dimensions={0} | all-to-all | bytes 1310720 | tf_op jit(solution)/shard_map/all_to_all | solution.py:339
  84.4 2.3 %combine.1 = bf16[16,4,512]{2,1,0:T(4,128)(2,1)} custom-call(bf16[512,640]{1,0:T(8,128)(2,1)} %bitcast.10), custom_call_target="tpu_custom_call" | custom-call | tf_op jit(solution)/shard_map/combine/pallas_call | solution.py:244
  86.6 14.2 %all_to_all.21 = bf16[16,4,512]{2,1,0:T(4,128)(2,1)S(1)} all-to-all(bf16[16,4,512]{2,1,0:T(4,128)(2,1)} %combine.1), channel_id=1, replica_groups=mesh['xl'=2,'y'=4,'core'=2,'xh'=2,'z'=8] {'xh','z'}, dimensions={0} | all-to-all | bytes 131072 | tf_op jit(solution)/shard_map/all_to_all | solution.py:342
  (90 shorter events, 7.2 us)
Async XLA Ops:
  1.5 5.1 %collective-permute-start = (bf16[80,512]{1,0:T(8,128)(2,1)}, bf16[80,512]{1,0:T(8,128)(2,1)S(1)}, u32[]{:S(2)}, u32[]{:S(2)}) collective-permute-start(bf16[80,512]{1,0:T(8,128)(2,1)} %pack.1), channel_id=1, source_target_pairs={{0,16},{16,0},{1,17},{17,1},{2,18},{18,2},{3,19},{19,3},{4,20},{20... | collective-permute-start | bytes 245768 | tf_op jit(solution)/shard_map/ppermute | solution.py:275
  1.5 16.9 %collective-permute-start.7 = (bf16[80,512]{1,0:T(8,128)(2,1)}, bf16[80,512]{1,0:T(8,128)(2,1)S(1)}, u32[]{:S(2)}, u32[]{:S(2)}) collective-permute-start(bf16[80,512]{1,0:T(8,128)(2,1)} %pack.1), channel_id=1, source_target_pairs={{0,136},{8,128},{128,8},{136,0},{1,137},{9,129},{129,9},{137,1},{2... | collective-permute-start | bytes 245768 | tf_op jit(solution)/shard_map/ppermute | solution.py:276
  4.3 34.4 %copy-start.2 = (bf16[4,128,512]{2,1,0:T(8,128)(2,1)S(1)}, bf16[4,128,512]{2,1,0:T(8,128)(2,1)}, u32[]{:S(2)}) copy-start(bf16[4,128,512]{2,1,0:T(8,128)(2,1)} %param.14) | copy-start | bytes 1572868
  6.7 32.3 %copy-start.1 = (bf16[144,512]{1,0:T(8,128)(2,1)}, bf16[144,512]{1,0:T(8,128)(2,1)S(1)}, u32[]{:S(2)}) copy-start(bf16[144,512]{1,0:T(8,128)(2,1)S(1)} %maximum_maximum_fusion.refs_0_) | copy-start | bytes 442372
  6.7 11.8 %collective-permute-start.3 = (bf16[144,512]{1,0:T(8,128)(2,1)S(1)}, bf16[144,512]{1,0:T(8,128)(2,1)S(1)}, u32[]{:S(2)}, u32[]{:S(2)}) collective-permute-start(bf16[144,512]{1,0:T(8,128)(2,1)S(1)} %maximum_maximum_fusion.refs_0_), channel_id=1, source_target_pairs={{0,2},{1,3},{2,4},{3,5},{4,6},{5,7},{6,0},{7,1},{16,22},{17,23},{1... | collective-permute-start | bytes 442376 | tf_op jit(solution)/shard_map/ppermute | solution.py:273
  10.3 15.2 %collective-permute-start.1 = (bf16[144,512]{1,0:T(8,128)(2,1)S(1)}, bf16[144,512]{1,0:T(8,128)(2,1)S(1)}, u32[]{:S(2)}, u32[]{:S(2)}) collective-permute-start(bf16[144,512]{1,0:T(8,128)(2,1)S(1)} %maximum_maximum_fusion.refs_0_), channel_id=1, source_target_pairs={{0,1},{1,2},{2,3},{3,4},{4,5},{5,6},{6,7},{7,0},{16,23},{17,16},{1... | collective-permute-start | bytes 442376 | tf_op jit(solution)/shard_map/ppermute | solution.py:273
  13.5 15.4 %all-to-all-start = ((bf16[16,4,768]{2,1,0:T(4,128)(2,1)}), bf16[16,4,768]{2,1,0:T(4,128)(2,1)S(1)}, u32[]{:S(2)}, u32[]{:S(2)}) async-start(bf16[16,4,768]{2,1,0:T(4,128)(2,1)} %bitcast.15), calls=%async_computation | async-start | bytes 196608 | tf_op jit(solution)/shard_map/all_to_all | solution.py:328
  18.4 16.0 %collective-permute-start.8 = (bf16[80,512]{1,0:T(8,128)(2,1)S(1)}, bf16[80,512]{1,0:T(8,128)(2,1)S(1)}, u32[]{:S(2)}, u32[]{:S(2)}) collective-permute-start(bf16[80,512]{1,0:T(8,128)(2,1)S(1)} %collective-permute-done.7.refs_7_), channel_id=1, source_target_pairs={{0,16},{16,0},{1,17},{17,1},{2,18},{18,2},{3,19},{19,3},{4,20},{20... | collective-permute-start | bytes 245768 | tf_op jit(solution)/shard_map/ppermute | solution.py:275
  18.6 27.3 %copy-start.3 = (bf16[4,512,128]{2,1,0:T(8,128)(2,1)S(1)}, bf16[4,512,128]{2,1,0:T(8,128)(2,1)}, u32[]{:S(2)}) copy-start(bf16[4,512,128]{2,1,0:T(8,128)(2,1)} %param.15) | copy-start | bytes 1572868
  18.6 16.1 %collective-permute-start.15 = (bf16[80,512]{1,0:T(8,128)(2,1)S(1)}, bf16[80,512]{1,0:T(8,128)(2,1)}, u32[]{:S(2)}, u32[]{:S(2)}) collective-permute-start(bf16[80,512]{1,0:T(8,128)(2,1)S(1)} %pad_maximum_fusion.1), channel_id=1, source_target_pairs={{0,2},{1,3},{2,4},{3,5},{4,6},{5,7},{6,0},{7,1},{16,22},{17,23},{1... | collective-permute-start | bytes 245768 | tf_op jit(solution)/shard_map/ppermute | solution.py:273
  22.0 14.9 %collective-permute-start.9 = (bf16[144,512]{1,0:T(8,128)(2,1)S(1)}, bf16[144,512]{1,0:T(8,128)(2,1)}, u32[]{:S(2)}, u32[]{:S(2)}) collective-permute-start(bf16[144,512]{1,0:T(8,128)(2,1)S(1)} %collective-permute-done.3.refs_3_), channel_id=1, source_target_pairs={{0,1},{1,2},{2,3},{3,4},{4,5},{5,6},{6,7},{7,0},{16,23},{17,16},{1... | collective-permute-start | bytes 442376 | tf_op jit(solution)/shard_map/ppermute | solution.py:273
  25.6 11.1 %collective-permute-start.5 = (bf16[144,512]{1,0:T(8,128)(2,1)S(1)}, bf16[144,512]{1,0:T(8,128)(2,1)S(1)}, u32[]{:S(2)}, u32[]{:S(2)}) collective-permute-start(bf16[144,512]{1,0:T(8,128)(2,1)S(1)} %collective-permute-done.1.refs_1_), channel_id=1, source_target_pairs={{0,136},{8,128},{128,8},{136,0},{1,137},{9,129},{129,9},{137,1},{2... | collective-permute-start | bytes 442376 | tf_op jit(solution)/shard_map/ppermute | solution.py:276
  28.9 10.2 %collective-permute-start.2 = (bf16[144,512]{1,0:T(8,128)(2,1)S(1)}, bf16[144,512]{1,0:T(8,128)(2,1)S(1)}, u32[]{:S(2)}, u32[]{:S(2)}) collective-permute-start(bf16[144,512]{1,0:T(8,128)(2,1)S(1)} %collective-permute-done.1.refs_1_), channel_id=1, source_target_pairs={{0,16},{16,0},{1,17},{17,1},{2,18},{18,2},{3,19},{19,3},{4,20},{20... | collective-permute-start | bytes 442376 | tf_op jit(solution)/shard_map/ppermute | solution.py:275
  29.9 23.2 %all-to-all-start.1 = ((bf16[8,64,768]{2,1,0:T(8,128)(2,1)}), bf16[8,64,768]{2,1,0:T(8,128)(2,1)S(1)}, u32[]{:S(2)}, u32[]{:S(2)}) async-start(bf16[8,64,768]{2,1,0:T(8,128)(2,1)} %broadcast_in_dim.90), calls=%async_computation.1 | async-start | bytes 1572864 | tf_op jit(solution)/shard_map/all_to_all | solution.py:331
  34.4 6.7 %collective-permute-start.4 = (bf16[144,512]{1,0:T(8,128)(2,1)S(1)}, bf16[144,512]{1,0:T(8,128)(2,1)S(1)}, u32[]{:S(2)}, u32[]{:S(2)}) collective-permute-start(bf16[144,512]{1,0:T(8,128)(2,1)S(1)} %collective-permute-done.3.refs_3_), channel_id=1, source_target_pairs={{0,16},{16,0},{1,17},{17,1},{2,18},{18,2},{3,19},{19,3},{4,20},{20... | collective-permute-start | bytes 442376 | tf_op jit(solution)/shard_map/ppermute | solution.py:275
  34.7 8.0 %collective-permute-start.13 = (bf16[144,512]{1,0:T(8,128)(2,1)S(1)}, bf16[144,512]{1,0:T(8,128)(2,1)}, u32[]{:S(2)}, u32[]{:S(2)}) collective-permute-start(bf16[144,512]{1,0:T(8,128)(2,1)S(1)} %collective-permute-done.3.refs_3_), channel_id=1, source_target_pairs={{0,136},{8,128},{128,8},{136,0},{1,137},{9,129},{129,9},{137,1},{2... | collective-permute-start | bytes 442376 | tf_op jit(solution)/shard_map/ppermute | solution.py:276
  36.7 11.1 %collective-permute-start.6 = (bf16[144,512]{1,0:T(8,128)(2,1)S(1)}, bf16[144,512]{1,0:T(8,128)(2,1)S(1)}, u32[]{:S(2)}, u32[]{:S(2)}) collective-permute-start(bf16[144,512]{1,0:T(8,128)(2,1)S(1)} %collective-permute-done.5.refs_5_), channel_id=1, source_target_pairs={{0,16},{16,0},{1,17},{17,1},{2,18},{18,2},{3,19},{19,3},{4,20},{20... | collective-permute-start | bytes 442376 | tf_op jit(solution)/shard_map/ppermute | solution.py:275
  36.8 9.0 %collective-permute-start.11 = (bf16[144,512]{1,0:T(8,128)(2,1)}, bf16[144,512]{1,0:T(8,128)(2,1)}, u32[]{:S(2)}, u32[]{:S(2)}) collective-permute-start(bf16[144,512]{1,0:T(8,128)(2,1)} %collective-permute-done.9.refs_0_), channel_id=1, source_target_pairs={{0,136},{8,128},{128,8},{136,0},{1,137},{9,129},{129,9},{137,1},{2... | collective-permute-start | bytes 442376 | tf_op jit(solution)/shard_map/ppermute | solution.py:276
  39.0 7.9 %collective-permute-start.17 = (bf16[80,512]{1,0:T(8,128)(2,1)}, bf16[80,512]{1,0:T(8,128)(2,1)S(1)}, u32[]{:S(2)}, u32[]{:S(2)}) collective-permute-start(bf16[80,512]{1,0:T(8,128)(2,1)} %collective-permute-done.15.refs_6_), channel_id=1, source_target_pairs={{0,136},{8,128},{128,8},{136,0},{1,137},{9,129},{129,9},{137,1},{2... | collective-permute-start | bytes 245768 | tf_op jit(solution)/shard_map/ppermute | solution.py:276
  41.1 12.0 %collective-permute-start.10 = (bf16[144,512]{1,0:T(8,128)(2,1)}, bf16[144,512]{1,0:T(8,128)(2,1)S(1)}, u32[]{:S(2)}, u32[]{:S(2)}) collective-permute-start(bf16[144,512]{1,0:T(8,128)(2,1)} %collective-permute-done.9.refs_0_), channel_id=1, source_target_pairs={{0,16},{16,0},{1,17},{17,1},{2,18},{18,2},{3,19},{19,3},{4,20},{20... | collective-permute-start | bytes 442376 | tf_op jit(solution)/shard_map/ppermute | solution.py:275
  42.7 10.4 %collective-permute-start.14 = (bf16[144,512]{1,0:T(8,128)(2,1)}, bf16[144,512]{1,0:T(8,128)(2,1)S(1)}, u32[]{:S(2)}, u32[]{:S(2)}) collective-permute-start(bf16[144,512]{1,0:T(8,128)(2,1)} %collective-permute-done.13.refs_4_), channel_id=1, source_target_pairs={{0,16},{16,0},{1,17},{17,1},{2,18},{18,2},{3,19},{19,3},{4,20},{20... | collective-permute-start | bytes 442376 | tf_op jit(solution)/shard_map/ppermute | solution.py:275
  45.9 7.3 %collective-permute-start.12 = (bf16[144,512]{1,0:T(8,128)(2,1)}, bf16[144,512]{1,0:T(8,128)(2,1)S(1)}, u32[]{:S(2)}, u32[]{:S(2)}) collective-permute-start(bf16[144,512]{1,0:T(8,128)(2,1)} %collective-permute-done.11.refs_2_), channel_id=1, source_target_pairs={{0,16},{16,0},{1,17},{17,1},{2,18},{18,2},{3,19},{19,3},{4,20},{20... | collective-permute-start | bytes 442376 | tf_op jit(solution)/shard_map/ppermute | solution.py:275
  47.0 6.1 %collective-permute-start.16 = (bf16[80,512]{1,0:T(8,128)(2,1)}, bf16[80,512]{1,0:T(8,128)(2,1)S(1)}, u32[]{:S(2)}, u32[]{:S(2)}) collective-permute-start(bf16[80,512]{1,0:T(8,128)(2,1)} %collective-permute-done.15.refs_6_), channel_id=1, source_target_pairs={{0,16},{16,0},{1,17},{17,1},{2,18},{18,2},{3,19},{19,3},{4,20},{20... | collective-permute-start | bytes 245768 | tf_op jit(solution)/shard_map/ppermute | solution.py:275
  47.8 5.3 %collective-permute-start.18 = (bf16[80,512]{1,0:T(8,128)(2,1)S(1)}, bf16[80,512]{1,0:T(8,128)(2,1)S(1)}, u32[]{:S(2)}, u32[]{:S(2)}) collective-permute-start(bf16[80,512]{1,0:T(8,128)(2,1)S(1)} %collective-permute-done.17.refs_8_), channel_id=1, source_target_pairs={{0,16},{16,0},{1,17},{17,1},{2,18},{18,2},{3,19},{19,3},{4,20},{20... | collective-permute-start | bytes 245768 | tf_op jit(solution)/shard_map/ppermute | solution.py:275
  (15 other events, 114.1 us)

commit v4 on v0

v4 whole, which is shorter than its diff:
```python
import functools
import math

import jax
import jax.numpy as jnp
from jax import lax
from jax.experimental import pallas as pl
from jax.experimental.pallas import tpu as pltpu
from jax.sharding import Mesh
from jax.sharding import PartitionSpec as P

L = 512
QN = 128
QR = 64
QD = QN + QR
VD = 128
BLOCK = 128
HEADS = 4
NEG = -1e30
SCALE = 1.0 / math.sqrt(QD)
LOG2E = math.log2(math.e)

AXES = ("xl", "y", "core", "xh", "z")
XLN, YN, CN, XHN, ZN = 2, 4, 2, 2, 8
CELLS = XLN * YN
GRP = XHN * ZN
PER = 64
TOK = 4
ROWS = CELLS * GRP * TOK
MSG = HEADS * VD
EXT = MSG + 128

HALF = 80
FOUR = 4 * PER
FULL = FOUR + 32

CHUNKS = [(0, 0)] + [(o, s) for s in (1, 2, 3) for o in (0, 1)] + [(0, 4)]
PIECES = [(j % 2, o, s, j // 2) for o, s in CHUNKS for j in range(4)]
SLOTS = len(PIECES)
KEYS = SLOTS * PER

VAT = 256
QT = 256
KT = 512


def attend_kernel(q_ref, *refs):
    chunks, refs = refs[: len(CHUNKS)], refs[len(CHUNKS) :]
    w_ref, thr_ref, o_ref, kv, sco = refs
    units = [(h, t) for h in range(HEADS) for t in range(ROWS // QT)]
    tiles = KEYS // KT
    off = lax.broadcasted_iota(jnp.int32, (64, 128), 0).astype(jnp.float32)
    lane = lax.broadcasted_iota(jnp.int32, (QT, 128), 1)

    def project(h, c):
        new = jnp.dot(chunks[c][0:FOUR, :], w_ref[h], preferred_element_type=jnp.float32)
        new = new.astype(jnp.bfloat16)
        rows = slice(c * FOUR, (c + 1) * FOUR)
        kv[h % 2, rows, 0:QN] = new[:, 0:QN]
        kv[h % 2, rows, VAT:] = new[:, QN:]

    for c in range(len(CHUNKS)):
        for r in range(FOUR // 16):
            at = FOUR + 16 * (r // 8)
            rope = chunks[c][at : at + 16, (r % 8) * QR : (r % 8 + 1) * QR]
            for b in range(2):
                kv[b, c * FOUR + r * 16 : c * FOUR + (r + 1) * 16, QN:QD] = rope
        project(0, c)

    def score(u, i, top):
        h, t = units[u]
        q = q_ref[t * QT : (t + 1) * QT, h * QD : (h + 1) * QD]
        s = lax.dot_general(
            q,
            kv[h % 2, i * KT : (i + 1) * KT, 0:QD],
            (((1,), (1,)), ((), ())),
            preferred_element_type=jnp.float32,
        )
        parts = []
        for b in range(QT // 64):
            row = t * (QT // 64) + b
            thr = thr_ref[row : row + 1, i * KT : (i + 1) * KT]
            cols = []
            for c in range(KT // 128):
                piece = s[b * 64 : (b + 1) * 64, c * 128 : (c + 1) * 128]
                cols.append(jnp.where(off >= thr[:, c * 128 : (c + 1) * 128], piece, NEG))
            parts.append(functools.reduce(jnp.maximum, cols))
            for c in range(KT // 128):
                at = i * KT + c * 128
                sco[u % 2, b * 64 : (b + 1) * 64, at : at + 128] = cols[c]
        best = jnp.concatenate(parts, axis=0)
        return best if top is None else jnp.maximum(top, best)

    def mix(u, i, mc, total, acc):
        h, t = units[u]
        p = jnp.exp2(sco[u % 2, :, i * KT : (i + 1) * KT] * (SCALE * LOG2E) - mc)
        for c in range(KT // 128):
            piece = p[:, c * 128 : (c + 1) * 128]
            total = piece if total is None else total + piece
        new = jnp.dot(
            p.astype(jnp.bfloat16),
            kv[h % 2, i * KT : (i + 1) * KT, VAT:],
            preferred_element_type=jnp.float32,
        )
        return total, new if acc is None else acc + new

    stats = [jnp.zeros((QT, 128), jnp.float32) for _ in range(ROWS // QT)]
    m = None
    for u in range(len(units) + 1):
        top = total = acc = None
        if u:
            mc = m * (SCALE * LOG2E)
        for i in range(tiles):
            if u < len(units):
                top = score(u, i, top)
            if u:
                total, acc = mix(u - 1, i, mc, total, acc)
            if u < len(units):
                h, t = units[u]
                if t == ROWS // QT - 1 and h + 1 < HEADS:
                    each = len(CHUNKS) // tiles
                    for c in range(i * each, (i + 1) * each):
                        project(h + 1, c)
        if u:
            h, t = units[u - 1]
            den = jnp.sum(total, axis=1, keepdims=True)
            lse = m * SCALE + jnp.log(den)
            o_ref[t * QT : (t + 1) * QT, h * VD : (h + 1) * VD] = (acc / den).astype(jnp.bfloat16)
            hi = lse.astype(jnp.bfloat16).astype(jnp.float32)
            mid = (lse - hi).astype(jnp.bfloat16).astype(jnp.float32)
            old = jnp.where(lane == 3 * h, hi, stats[t])
            old = jnp.where(lane == 3 * h + 1, mid, old)
            stats[t] = jnp.where(lane == 3 * h + 2, lse - hi - mid, old)
        if u < len(units):
            m = jnp.max(top, axis=1, keepdims=True)
    for t in range(ROWS // QT):
        o_ref[t * QT : (t + 1) * QT, MSG:] = stats[t].astype(jnp.bfloat16)


def attend(q, chunks, weights, thr):
    return pl.pallas_call(
        attend_kernel,
        out_shape=jax.ShapeDtypeStruct((ROWS, EXT), jnp.bfloat16),
        scratch_shapes=[
            pltpu.VMEM((2, KEYS, VAT + VD), jnp.bfloat16),
            pltpu.VMEM((2, QT, KEYS), jnp.float32),
        ],
        compiler_params=pltpu.CompilerParams(vmem_limit_bytes=32 * 1024 * 1024),
        cost_estimate=pl.CostEstimate(
            flops=6_500_000_000, bytes_accessed=6_000_000, transcendentals=4_200_000
        ),
        name="attend",
    )(q, *chunks, weights, thr)


def combine_kernel(x_ref, o_ref):
    n = GRP * TOK
    ext = [x_ref[pl.ds(c * n, n), MSG:].astype(jnp.float32) for c in range(CELLS)]
    for h in range(HEADS):
        j = 3 * h
        lse = [e[:, j : j + 1] + e[:, j + 1 : j + 2] + e[:, j + 2 : j + 3] for e in ext]
        top = functools.reduce(jnp.maximum, lse)
        part = [jnp.exp(v - top) for v in lse]
        scale = 1.0 / functools.reduce(jnp.add, part)
        acc = jnp.zeros((n, VD), jnp.float32)
        for c in range(CELLS):
            acc = acc + x_ref[pl.ds(c * n, n), pl.ds(h * VD, VD)].astype(jnp.float32) * (
                part[c] * scale
            )
        o_ref[:, :, pl.ds(h * VD, VD)] = acc.reshape(GRP, TOK, VD).astype(jnp.bfloat16)


def combine(x):
    return pl.pallas_call(
        combine_kernel,
        out_shape=jax.ShapeDtypeStruct((GRP, TOK, MSG), jnp.bfloat16),
        name="combine",
    )(x)


def pack_kernel(lat_ref, rope_ref, o_ref):
    o_ref[0:PER, :] = lat_ref[...]
    for r in range(L // QR):
        b = r % (PER // 16)
        o_ref[PER:HALF, r * QR : (r + 1) * QR] = rope_ref[b * 16 : (b + 1) * 16, :]


def pack(latents, key_rope):
    return pl.pallas_call(
        pack_kernel, out_shape=jax.ShapeDtypeStruct((HALF, L), jnp.bfloat16), name="pack"
    )(latents, key_rope)


def merge_kernel(*refs):
    o_ref = refs[-1]
    for j, ref in enumerate(refs[:-1]):
        half = slice(j % 2 * (L // 2), (j % 2 + 1) * (L // 2))
        at = FOUR + j // 2 * 16
        o_ref[j * PER : (j + 1) * PER, :] = ref[0:PER, :]
        o_ref[at : at + 16, half] = ref[PER:HALF, half]


def merge(pieces):
    return pl.pallas_call(
        merge_kernel, out_shape=jax.ShapeDtypeStruct((FULL, L), jnp.bfloat16), name="merge"
    )(*pieces)


def shift(n, k):
    return [(i, (i + k) % n) for i in range(n)]


def gather_keys(latents, key_rope, swap):
    near = [(a * 2 + b, (1 - a) * 2 + 1 - b) for a in range(2) for b in range(2)]
    up = [(i, (i + 1) % ZN) for i in range(ZN)]
    down = [(ZN + i, ZN + (i - 1) % ZN) for i in range(ZN)]
    to_core = lambda x: lax.ppermute(x, "core", shift(CN, 1))
    piece = pack(latents, key_rope)
    beside = lax.ppermute(piece, ("xl", "xh"), near)
    pieces = [piece, beside, to_core(piece), to_core(beside)]
    mine = swap(piece)
    pieces, mine = lax.optimization_barrier((pieces, mine))
    now = merge(pieces)
    got = {(0, 0): now}
    for s in range(1, 5):
        got[0, s] = now = lax.ppermute(now, ("core", "z"), up + down)
        if s < 4:
            got[1, s] = to_core(now)
    return [got[c] for c in CHUNKS], mine, got[0, 1]


def threshold_kernel(pattern_ref, stripe_ref, o_ref):
    xl, y, core = lax.axis_index("xl"), lax.axis_index("y"), lax.axis_index("core")
    xh, z = lax.axis_index("xh"), lax.axis_index("z")
    lane = lax.broadcasted_iota(jnp.int32, (1, 128), 1)
    blocks = stripe_ref.shape[0]

    def facts(swap, other, step, inner):
        side = core ^ other
        zz = lax.rem(z + jnp.where(side == 1, step, ZN - step), ZN)
        cell = ((xl ^ swap) * YN + y) * CN + (side ^ inner)
        place = cell * GRP + (xh ^ swap) * ZN + zz
        return stripe_ref[lax.shift_right_logical(place, 1)], (place & 1) * PER - core * 64

    for pair in range(SLOTS // 2):
        two = [facts(*PIECES[2 * pair + j]) for j in range(2)]
        for r in range(CELLS):
            vals = []
            for j, (kb, base) in enumerate(two):
                see = (kb < blocks - CELLS + r) & (pattern_ref[r, kb] == 1)
                same = kb == blocks - CELLS + r
                const = jnp.where(see, -BLOCK, jnp.where(same, base - j * PER, 4 * BLOCK))
                vals.append(const + lane * jnp.where(same, 1, 0))
            row = jnp.where(lane < PER, vals[0], vals[1]).astype(jnp.float32)
            o_ref[r : r + 1, pair * 128 : (pair + 1) * 128] = row


def thresholds(pattern, stripe):
    return pl.pallas_call(
        threshold_kernel,
        out_shape=jax.ShapeDtypeStruct((CELLS, KEYS), jnp.float32),
        in_specs=[pl.BlockSpec(memory_space=pltpu.SMEM)] * 2,
        name="thresholds",
    )(pattern, stripe)


def body(queries, latents, key_rope, key_up, value_up, pattern, stripe):
    cells = ("xl", "y")
    groups = ("xh", "z")
    def swap(after):
        send = queries.reshape(TOK, GRP, HEADS * QD).transpose(1, 0, 2)
        send, _ = lax.optimization_barrier((send, after))
        return lax.all_to_all(send, groups, split_axis=0, concat_axis=0, tiled=True)

    chunks, mine, mark = gather_keys(latents, key_rope, swap)
    mine = mine.reshape(GRP * TOK, HEADS * QD)
    send = jnp.broadcast_to(mine[None], (CELLS, *mine.shape))
    q = lax.all_to_all(send, cells, split_axis=0, concat_axis=0, tiled=True)
    q = q.reshape(ROWS, HEADS * QD)
    key_up, value_up, pattern, stripe, _ = lax.optimization_barrier(
        (key_up, value_up, pattern, stripe, mark)
    )
    weights = jnp.concatenate([key_up.transpose(0, 2, 1), value_up], axis=2)
    part = attend(q, chunks, weights, thresholds(pattern, stripe))
    back = lax.all_to_all(
        part.reshape(CELLS, GRP * TOK, EXT), cells, split_axis=0, concat_axis=0, tiled=True
    )
    out = lax.all_to_all(combine(back.reshape(ROWS, EXT)), groups, split_axis=0, concat_axis=0, tiled=True)
    return out.transpose(1, 0, 2).reshape(TOK, GRP * MSG)


def solution(mesh):
    fine = Mesh(mesh.devices.reshape(XLN, YN, CN, XHN, ZN), AXES)
    in_specs = (
        P(AXES, None),
        P(AXES, None),
        P(AXES, None),
        P(("xh", "z"), None, None),
        P(("xh", "z"), None, None),
        P(),
        P(),
    )
    return jax.shard_map(body, mesh=fine, in_specs=in_specs, out_specs=P(AXES, None), check_vma=False)
```

time: 288 us -> 102 us (0.35)
  waiting for transfers between devices: 145 us -> 22.6 us
  matrix products: 53.7 us -> 0 us
  blocking collectives: 58 us -> 34.7 us
  Pallas kernels: 0 us -> 17.9 us
  starting transfers between devices: 5.49 us -> 21.7 us
  between operations: 13.2 us -> 0.09 us
  other arithmetic: 9.82 us -> 1.37 us
    all_gather x3 -> x0, waiting for transfers between devices: 144 us -> none  [the longest x1 83.3 us: body(): lax.all_gather(latents, 'grp', axis=0, tiled=True)]
    dot_general x7 -> x0, matrix products: 53.7 us -> none  [the longest x1 15.1 us: compute(): jnp.einsum('rhn,nc->rhc', weights.astype(jnp.bfloat16), latent_piece, pre...]
    all_gather x1 -> x0, blocking collectives: 39.5 us -> none  [body(): lax.all_gather(key_rope, 'grp', axis=0, tiled=True)]
    ppermute x0 -> x10, waiting for transfers between devices: none -> 20.8 us  [the longest x4 16.1 us: gather_keys(): got[0, s] = now = lax.ppermute(now, ('core', 'z'), up + down)]
    pallas_call x0 -> x5, Pallas kernels: none -> 17.9 us  [the longest x1 10.1 us: attend(): pl.pallas_call(attend_kernel, out_shape=jax.ShapeDtypeStruct((ROWS, EXT),...]
    all_to_all x1 -> x2, blocking collectives: 18.5 us -> 34.7 us  [the longest x1 18.4 us: body(): lax.all_to_all(combine(back.reshape(ROWS, EXT)), groups, split_axis=0, co...]
    all_to_all x1 -> x2, starting transfers between devices: 5.41 us -> 15.5 us  [the longest x1 11 us: swap(): return lax.all_to_all(send, groups, split_axis=0, concat_axis=0, tiled=True)]
    reduce_sum x1 -> x0, other arithmetic: 9.76 us -> none  [compute(): denominator = jnp.sum(weights, axis=2)]
  transfers between devices with their start and end apart: 4 -> 12, of which waited for: 3 -> 7; matrix products, arithmetic and copies ran while one was open for 9% -> 3% of each run, Pallas kernels for 0% -> 2%
where the time goes in v4:
time: 102 us; the launch traced here: 101 us
  blocking collectives  34.7 us (34%)
  waiting for transfers between devices  22.6 us (22%)
  starting transfers between devices  21.7 us (21%)
  Pallas kernels  17.9 us (18%)
  local copies, waits for them, and re-layouts  2.64 us (3%)
  other arithmetic  1.37 us (1%)
    all_to_all x1, blocking collectives, body(): lax.all_to_all(combine(back.reshape(ROWS, EXT)), groups, split_axis=0, co...  18.4 us
    all_to_all x1, blocking collectives, body(): lax.all_to_all(part.reshape(CELLS, GRP * TOK, EXT), cells, split_axis=0,...  16.2 us
    ppermute x4, waiting for transfers between devices, gather_keys(): got[0, s] = now = lax.ppermute(now, ('core', 'z'), up + down)  16.1 us
    all_to_all x1, starting transfers between devices, swap(): return lax.all_to_all(send, groups, split_axis=0, concat_axis=0, tiled=True)  11 us
    pallas_call x1, Pallas kernels, attend(): pl.pallas_call(attend_kernel, out_shape=jax.ShapeDtypeStruct((ROWS, EXT),...  10.1 us
    all_to_all x1, starting transfers between devices, body(): q = lax.all_to_all(send, cells, split_axis=0, concat_axis=0, tiled=True)  4.5 us
    ppermute x1, waiting for transfers between devices, gather_keys(): beside = lax.ppermute(piece, ('xl', 'xh'), near)  3.42 us
    ppermute x4, starting transfers between devices, gather_keys(): got[0, s] = now = lax.ppermute(now, ('core', 'z'), up + down)  2.93 us
  transfers between devices with their start and end apart: 12, of which 7 were waited for; matrix products, arithmetic and copies ran while one was open for 3% of the time, Pallas kernels for 2%

profile of v4, /device:TPU:32, one launch (start us, length us, event | category | flops | bytes accessed | tf_op | source)
XLA Modules:
  0.0 101.0 jit_solution(15013172368501234497)
XLA Ops:
  0.0 1.5 %pack.1.refs_0_ = bf16[80,512]{1,0:T(8,128)(2,1)} custom-call(bf16[64,512]{1,0:T(8,128)(2,1)} %lat_ref.1, bf16[64,64]{1,0:T(8,128)(2,1)} %rope_ref.1), custom_call_target="tpu_custom_call" | custom-call | tf_op jit(solution)/shard_map/pack/pallas_call | solution.py:189
  1.5 11.0 %all-to-all-start = ((bf16[16,4,768]{2,1,0:T(4,128)(2,1)}), bf16[16,4,768]{2,1,0:T(4,128)(2,1)S(1)}, u32[]{:S(2)}, u32[]{:S(2)}) async-start(bf16[16,4,768]{2,1,0:T(4,128)(2,1)} %bitcast.15), calls=%async_computation | async-start | bytes 196608 | tf_op jit(solution)/shard_map/all_to_all | solution.py:273
  12.6 2.7 %collective-permute-start = (bf16[80,512]{1,0:T(8,128)(2,1)}, bf16[80,512]{1,0:T(8,128)(2,1)S(1)}, u32[]{:S(2)}, u32[]{:S(2)}) collective-permute-start(bf16[80,512]{1,0:T(8,128)(2,1)} %pack.1.refs_0_), channel_id=1, source_target_pairs={{0,136},{8,128},{128,8},{136,0},{1,137},{9,129},{129,9},{137,1},{2... | collective-permute-start | bytes 245768 | tf_op jit(solution)/shard_map/ppermute | solution.py:219
  15.3 3.4 %collective-permute-done.refs_1_ = bf16[80,512]{1,0:T(8,128)(2,1)S(1)} collective-permute-done((bf16[80,512]{1,0:T(8,128)(2,1)}, bf16[80,512]{1,0:T(8,128)(2,1)S(1)}, u32[]{:S(2)}, u32[]{:S(2)}) %collective-permute-start) | collective-permute-done | bytes 81952 | tf_op jit(solution)/shard_map/ppermute | solution.py:219
  18.7 1.3 %collective-permute-done.2.refs_3_ = bf16[80,512]{1,0:T(8,128)(2,1)S(1)} collective-permute-done((bf16[80,512]{1,0:T(8,128)(2,1)S(1)}, bf16[80,512]{1,0:T(8,128)(2,1)S(1)}, u32[]{:S(2)}, u32[]{:S(2)}) %collective-permute-start.2) | collective-permute-done | bytes 81952 | tf_op jit(solution)/shard_map/ppermute | solution.py:217
  20.0 1.8 %all-to-all-done = bf16[16,4,768]{2,1,0:T(4,128)(2,1)S(1)} async-done(((bf16[16,4,768]{2,1,0:T(4,128)(2,1)}), bf16[16,4,768]{2,1,0:T(4,128)(2,1)S(1)}, u32[]{:S(2)}, u32[]{:S(2)}) %all-to-all-start) | async-done | bytes 98336 | tf_op jit(solution)/shard_map/all_to_all | solution.py:273
  21.8 1.7 %merge.1.refs_0_ = bf16[288,512]{1,0:T(8,128)(2,1)} custom-call(bf16[80,512]{1,0:T(8,128)(2,1)} %pack.1.refs_0_, bf16[80,512]{1,0:T(8,128)(2,1)} %copy-done.3, bf16[80,512]{1,0:T(8,128)(2,1)} %copy-done.4, bf16[80,512]{1,0:T(8,128)(2,1)} %copy-done.5), custom_call_target="tpu_custom_call" | custom-call | tf_op jit(solution)/shard_map/merge/pallas_call | solution.py:204
  23.6 0.8 collective-permute-start.3
  24.3 6.2 %collective-permute-done.3.refs_1_ = bf16[288,512]{1,0:T(8,128)(2,1)S(1)} collective-permute-done((bf16[288,512]{1,0:T(8,128)(2,1)}, bf16[288,512]{1,0:T(8,128)(2,1)S(1)}, u32[]{:S(2)}, u32[]{:S(2)}) %collective-permute-start.3) | collective-permute-done | bytes 294944 | tf_op jit(solution)/shard_map/ppermute | solution.py:226
  30.5 0.8 collective-permute-start.5
  31.3 0.9 broadcast_in_dim.8
  32.2 4.5 %all-to-all-start.1 = ((bf16[8,64,768]{2,1,0:T(8,128)(2,1)}), bf16[8,64,768]{2,1,0:T(8,128)(2,1)S(1)}, u32[]{:S(2)}, u32[]{:S(2)}) async-start(bf16[8,64,768]{2,1,0:T(8,128)(2,1)} %broadcast_in_dim.8), calls=%async_computation.1 | async-start | bytes 1572864 | tf_op jit(solution)/shard_map/all_to_all | solution.py:278
  37.3 0.8 collective-permute-start.7
  38.6 6.7 %collective-permute-done.7.refs_5_ = bf16[288,512]{1,0:T(8,128)(2,1)S(1)} collective-permute-done((bf16[288,512]{1,0:T(8,128)(2,1)S(1)}, bf16[288,512]{1,0:T(8,128)(2,1)S(1)}, u32[]{:S(2)}, u32[]{:S(2)}) %collective-permute-start.7) | collective-permute-done | bytes 294944 | tf_op jit(solution)/shard_map/ppermute | solution.py:226
  45.3 0.7 collective-permute-start.9
  45.9 1.0 %copy.10 = bf16[4,128,512]{1,2,0:T(8,128)(2,1)} copy(bf16[4,128,512]{2,1,0:T(8,128)(2,1)S(1)} %copy-done.2) | data formatting | bytes 1048576 | tf_op jit(solution)/shard_map/optimization_barrier | solution.py:280
  47.0 2.3 %thresholds.1.refs_9_ = f32[8,2048]{1,0:T(8,128)} custom-call(s32[8,128]{1,0:T(8,128)} %pattern_ref, s32[128]{0:T(128)} %stripe_ref), custom_call_target="tpu_custom_call" | custom-call | tf_op jit(solution)/shard_map/thresholds/pallas_call | solution.py:259
  49.2 1.4 %pad_maximum_fusion.refs_8_ = bf16[4,512,256]{2,1,0:T(8,128)(2,1)S(1)} fusion(bf16[4,512,128]{2,1,0:T(8,128)(2,1)} %param.11, bf16[4,512,128]{2,1,0:T(8,128)(2,1)} %bitcast.13), kind=kLoop, calls=%fused_computation | loop fusion | flops 2097152 | bytes 2097152 | tf_op jit(solution)/shard_map/concatenate | solution.py:283
  50.7 2.7 %collective-permute-done.9.refs_7_ = bf16[288,512]{1,0:T(8,128)(2,1)} collective-permute-done((bf16[288,512]{1,0:T(8,128)(2,1)S(1)}, bf16[288,512]{1,0:T(8,128)(2,1)}, u32[]{:S(2)}, u32[]{:S(2)}) %collective-permute-start.9) | collective-permute-done | bytes 294944 | tf_op jit(solution)/shard_map/ppermute | solution.py:226
  53.3 10.1 %attend.1 = bf16[512,640]{1,0:T(8,128)(2,1)S(1)} custom-call(bf16[512,768]{1,0:T(8,128)(2,1)S(1)} %bitcast.10, bf16[288,512]{1,0:T(8,128)(2,1)S(1)} %copy-done, bf16[288,512]{1,0:T(8,128)(2,1)S(1)} %collective-permute-done.3.refs_1_, bf16[288,512]{1,0:T(8,128)(2,1)S(1)} %collective-permute-done.4.refs_2_, ...), custom_call_target="tpu_custom_call" | custom-call | flops 6499999744 | bytes 6000000 | tf_op jit(solution)/shard_map/attend/pallas_call | solution.py:141
  63.4 16.2 %all_to_all.20 = bf16[8,64,640]{2,1,0:T(8,128)(2,1)} all-to-all(bf16[8,64,640]{2,1,0:T(8,128)(2,1)S(1)} %bitcast.11), channel_id=1, replica_groups=mesh['xl'=2,'y'=4,'core'=2,'xh'=2,'z'=8] {'xl','y'}, dimensions={0} | all-to-all | bytes 1310720 | tf_op jit(solution)/shard_map/all_to_all | solution.py:285
  79.7 2.3 %combine.1 = bf16[16,4,512]{2,1,0:T(4,128)(2,1)} custom-call(bf16[512,640]{1,0:T(8,128)(2,1)} %bitcast.12), custom_call_target="tpu_custom_call" | custom-call | tf_op jit(solution)/shard_map/combine/pallas_call | solution.py:174
  81.9 18.4 %all_to_all.21 = bf16[16,4,512]{2,1,0:T(4,128)(2,1)S(1)} all-to-all(bf16[16,4,512]{2,1,0:T(4,128)(2,1)} %combine.1), channel_id=1, replica_groups=mesh['xl'=2,'y'=4,'core'=2,'xh'=2,'z'=8] {'xh','z'}, dimensions={0} | all-to-all | bytes 131072 | tf_op jit(solution)/shard_map/all_to_all | solution.py:288
  100.4 0.6 copy.12
  (24 shorter events, 1.2 us)
Async XLA Ops:
  1.5 20.3 %all-to-all-start = ((bf16[16,4,768]{2,1,0:T(4,128)(2,1)}), bf16[16,4,768]{2,1,0:T(4,128)(2,1)S(1)}, u32[]{:S(2)}, u32[]{:S(2)}) async-start(bf16[16,4,768]{2,1,0:T(4,128)(2,1)} %bitcast.15), calls=%async_computation | async-start | bytes 196608 | tf_op jit(solution)/shard_map/all_to_all | solution.py:273
  12.6 6.1 %collective-permute-start = (bf16[80,512]{1,0:T(8,128)(2,1)}, bf16[80,512]{1,0:T(8,128)(2,1)S(1)}, u32[]{:S(2)}, u32[]{:S(2)}) collective-permute-start(bf16[80,512]{1,0:T(8,128)(2,1)} %pack.1.refs_0_), channel_id=1, source_target_pairs={{0,136},{8,128},{128,8},{136,0},{1,137},{9,129},{129,9},{137,1},{2... | collective-permute-start | bytes 245768 | tf_op jit(solution)/shard_map/ppermute | solution.py:219
  15.3 3.4 %collective-permute-start.1 = (bf16[80,512]{1,0:T(8,128)(2,1)}, bf16[80,512]{1,0:T(8,128)(2,1)S(1)}, u32[]{:S(2)}, u32[]{:S(2)}) collective-permute-start(bf16[80,512]{1,0:T(8,128)(2,1)} %pack.1.refs_0_), channel_id=1, source_target_pairs={{0,16},{16,0},{1,17},{17,1},{2,18},{18,2},{3,19},{19,3},{4,20},{20... | collective-permute-start | bytes 245768 | tf_op jit(solution)/shard_map/ppermute | solution.py:217
  18.7 3.1 %copy-start.3 = (bf16[80,512]{1,0:T(8,128)(2,1)}, bf16[80,512]{1,0:T(8,128)(2,1)S(1)}, u32[]{:S(2)}) copy-start(bf16[80,512]{1,0:T(8,128)(2,1)S(1)} %collective-permute-done.refs_1_) | copy-start | bytes 245764
  18.7 1.3 %collective-permute-start.2 = (bf16[80,512]{1,0:T(8,128)(2,1)S(1)}, bf16[80,512]{1,0:T(8,128)(2,1)S(1)}, u32[]{:S(2)}, u32[]{:S(2)}) collective-permute-start(bf16[80,512]{1,0:T(8,128)(2,1)S(1)} %collective-permute-done.refs_1_), channel_id=1, source_target_pairs={{0,16},{16,0},{1,17},{17,1},{2,18},{18,2},{3,19},{19,3},{4,20},{20... | collective-permute-start | bytes 245768 | tf_op jit(solution)/shard_map/ppermute | solution.py:217
  18.7 3.1 %copy-start.4 = (bf16[80,512]{1,0:T(8,128)(2,1)}, bf16[80,512]{1,0:T(8,128)(2,1)S(1)}, u32[]{:S(2)}) copy-start(bf16[80,512]{1,0:T(8,128)(2,1)S(1)} %collective-permute-done.1.refs_2_) | copy-start | bytes 245764
  20.0 1.8 %copy-start.5 = (bf16[80,512]{1,0:T(8,128)(2,1)}, bf16[80,512]{1,0:T(8,128)(2,1)S(1)}, u32[]{:S(2)}) copy-start(bf16[80,512]{1,0:T(8,128)(2,1)S(1)} %collective-permute-done.2.refs_3_) | copy-start | bytes 245764
  23.6 6.9 %collective-permute-start.3 = (bf16[288,512]{1,0:T(8,128)(2,1)}, bf16[288,512]{1,0:T(8,128)(2,1)S(1)}, u32[]{:S(2)}, u32[]{:S(2)}) collective-permute-start(bf16[288,512]{1,0:T(8,128)(2,1)} %merge.1.refs_0_), channel_id=1, source_target_pairs={{0,1},{1,2},{2,3},{3,4},{4,5},{5,6},{6,7},{7,0},{16,23},{17,16},{1... | collective-permute-start | bytes 884744 | tf_op jit(solution)/shard_map/ppermute | solution.py:226
  30.5 6.9 %collective-permute-start.5 = (bf16[288,512]{1,0:T(8,128)(2,1)S(1)}, bf16[288,512]{1,0:T(8,128)(2,1)S(1)}, u32[]{:S(2)}, u32[]{:S(2)}) collective-permute-start(bf16[288,512]{1,0:T(8,128)(2,1)S(1)} %collective-permute-done.3.refs_1_), channel_id=1, source_target_pairs={{0,1},{1,2},{2,3},{3,4},{4,5},{5,6},{6,7},{7,0},{16,23},{17,16},{1... | collective-permute-start | bytes 884744 | tf_op jit(solution)/shard_map/ppermute | solution.py:226
  31.3 14.7 %copy-start.2 = (bf16[4,128,512]{2,1,0:T(8,128)(2,1)S(1)}, bf16[4,128,512]{2,1,0:T(8,128)(2,1)}, u32[]{:S(2)}) copy-start(bf16[4,128,512]{2,1,0:T(8,128)(2,1)} %param.10) | copy-start | bytes 1572868
  32.2 18.4 %all-to-all-start.1 = ((bf16[8,64,768]{2,1,0:T(8,128)(2,1)}), bf16[8,64,768]{2,1,0:T(8,128)(2,1)S(1)}, u32[]{:S(2)}, u32[]{:S(2)}) async-start(bf16[8,64,768]{2,1,0:T(8,128)(2,1)} %broadcast_in_dim.8), calls=%async_computation.1 | async-start | bytes 1572864 | tf_op jit(solution)/shard_map/all_to_all | solution.py:278
  37.3 7.9 %collective-permute-start.7 = (bf16[288,512]{1,0:T(8,128)(2,1)S(1)}, bf16[288,512]{1,0:T(8,128)(2,1)S(1)}, u32[]{:S(2)}, u32[]{:S(2)}) collective-permute-start(bf16[288,512]{1,0:T(8,128)(2,1)S(1)} %collective-permute-done.5.refs_3_), channel_id=1, source_target_pairs={{0,1},{1,2},{2,3},{3,4},{4,5},{5,6},{6,7},{7,0},{16,23},{17,16},{1... | collective-permute-start | bytes 884744 | tf_op jit(solution)/shard_map/ppermute | solution.py:226
  38.1 12.5 %collective-permute-start.4 = (bf16[288,512]{1,0:T(8,128)(2,1)S(1)}, bf16[288,512]{1,0:T(8,128)(2,1)S(1)}, u32[]{:S(2)}, u32[]{:S(2)}) collective-permute-start(bf16[288,512]{1,0:T(8,128)(2,1)S(1)} %collective-permute-done.3.refs_1_), channel_id=1, source_target_pairs={{0,16},{16,0},{1,17},{17,1},{2,18},{18,2},{3,19},{19,3},{4,20},{20... | collective-permute-start | bytes 884744 | tf_op jit(solution)/shard_map/ppermute | solution.py:217
  38.1 12.5 %collective-permute-start.6 = (bf16[288,512]{1,0:T(8,128)(2,1)S(1)}, bf16[288,512]{1,0:T(8,128)(2,1)}, u32[]{:S(2)}, u32[]{:S(2)}) collective-permute-start(bf16[288,512]{1,0:T(8,128)(2,1)S(1)} %collective-permute-done.5.refs_3_), channel_id=1, source_target_pairs={{0,16},{16,0},{1,17},{17,1},{2,18},{18,2},{3,19},{19,3},{4,20},{20... | collective-permute-start | bytes 884744 | tf_op jit(solution)/shard_map/ppermute | solution.py:217
  45.3 5.4 %collective-permute-start.8 = (bf16[288,512]{1,0:T(8,128)(2,1)S(1)}, bf16[288,512]{1,0:T(8,128)(2,1)}, u32[]{:S(2)}, u32[]{:S(2)}) collective-permute-start(bf16[288,512]{1,0:T(8,128)(2,1)S(1)} %collective-permute-done.7.refs_5_), channel_id=1, source_target_pairs={{0,16},{16,0},{1,17},{17,1},{2,18},{18,2},{3,19},{19,3},{4,20},{20... | collective-permute-start | bytes 884744 | tf_op jit(solution)/shard_map/ppermute | solution.py:217
  45.3 8.0 %collective-permute-start.9 = (bf16[288,512]{1,0:T(8,128)(2,1)S(1)}, bf16[288,512]{1,0:T(8,128)(2,1)}, u32[]{:S(2)}, u32[]{:S(2)}) collective-permute-start(bf16[288,512]{1,0:T(8,128)(2,1)S(1)} %collective-permute-done.7.refs_5_), channel_id=1, source_target_pairs={{0,1},{1,2},{2,3},{3,4},{4,5},{5,6},{6,7},{7,0},{16,23},{17,16},{1... | collective-permute-start | bytes 884744 | tf_op jit(solution)/shard_map/ppermute | solution.py:226
  49.2 4.1 %copy-start = (bf16[288,512]{1,0:T(8,128)(2,1)S(1)}, bf16[288,512]{1,0:T(8,128)(2,1)}, u32[]{:S(2)}) copy-start(bf16[288,512]{1,0:T(8,128)(2,1)} %merge.1.refs_0_) | copy-start | bytes 884740
  49.2 4.1 %copy-start.1 = (f32[8,2048]{1,0:T(8,128)S(1)}, f32[8,2048]{1,0:T(8,128)}, u32[]{:S(2)}) copy-start(f32[8,2048]{1,0:T(8,128)} %thresholds.1.refs_9_) | copy-start | bytes 196612

commit v5 on v4

--- a/solution.py
+++ b/solution.py
@@ -34,21 +34,26 @@
 FOUR = 4 * PER
 FULL = FOUR + 32
 
-CHUNKS = [(0, 0)] + [(o, s) for s in (1, 2, 3) for o in (0, 1)] + [(0, 4)]
+EARLY = [(0, 0)] + [(o, s) for s in (1, 2) for o in (0, 1)]
+LATE = [(0, 3), (1, 3), (0, 4)]
+CHUNKS = EARLY + LATE
 PIECES = [(j % 2, o, s, j // 2) for o, s in CHUNKS for j in range(4)]
 SLOTS = len(PIECES)
 KEYS = SLOTS * PER
 
 VAT = 256
 QT = 256
-KT = 512
-
-
-def attend_kernel(q_ref, *refs):
-    chunks, refs = refs[: len(CHUNKS)], refs[len(CHUNKS) :]
-    w_ref, thr_ref, o_ref, kv, sco = refs
+KT = FOUR
+SMALL = pltpu.CompilerParams(vmem_limit_bytes=8 * 1024 * 1024)
+
+
+def attend_kernel(count, first, *refs):
+    chunks, refs = refs[:count], refs[count:]
+    if first:
+        q_ref, w_ref, thr_ref, old_ref, lse_ref, o_ref, kv, sco = refs
+    else:
+        q_ref, w_ref, thr_ref, o_ref, lse_ref, kv, sco = refs
     units = [(h, t) for h in range(HEADS) for t in range(ROWS // QT)]
-    tiles = KEYS // KT
     off = lax.broadcasted_iota(jnp.int32, (64, 128), 0).astype(jnp.float32)
     lane = lax.broadcasted_iota(jnp.int32, (QT, 128), 1)
 
@@ -59,7 +64,7 @@
         kv[h % 2, rows, 0:QN] = new[:, 0:QN]
         kv[h % 2, rows, VAT:] = new[:, QN:]
 
-    for c in range(len(CHUNKS)):
+    for c in range(count):
         for r in range(FOUR // 16):
             at = FOUR + 16 * (r // 8)
             rope = chunks[c][at : at + 16, (r % 8) * QR : (r % 8 + 1) * QR]
@@ -79,7 +84,8 @@
         parts = []
         for b in range(QT // 64):
             row = t * (QT // 64) + b
-            thr = thr_ref[row : row + 1, i * KT : (i + 1) * KT]
+            at = (first + i) * KT
+            thr = thr_ref[row : row + 1, at : at + KT]
             cols = []
             for c in range(KT // 128):
                 piece = s[b * 64 : (b + 1) * 64, c * 128 : (c + 1) * 128]
@@ -110,7 +116,7 @@
         top = total = acc = None
         if u:
             mc = m * (SCALE * LOG2E)
-        for i in range(tiles):
+        for i in range(count):
             if u < len(units):
                 top = score(u, i, top)
             if u:
@@ -118,39 +124,60 @@
             if u < len(units):
                 h, t = units[u]
                 if t == ROWS // QT - 1 and h + 1 < HEADS:
-                    each = len(CHUNKS) // tiles
-                    for c in range(i * each, (i + 1) * each):
-                        project(h + 1, c)
+                    project(h + 1, i)
         if u:
             h, t = units[u - 1]
+            rows = slice(t * QT, (t + 1) * QT)
             den = jnp.sum(total, axis=1, keepdims=True)
             lse = m * SCALE + jnp.log(den)
-            o_ref[t * QT : (t + 1) * QT, h * VD : (h + 1) * VD] = (acc / den).astype(jnp.bfloat16)
-            hi = lse.astype(jnp.bfloat16).astype(jnp.float32)
-            mid = (lse - hi).astype(jnp.bfloat16).astype(jnp.float32)
-            old = jnp.where(lane == 3 * h, hi, stats[t])
-            old = jnp.where(lane == 3 * h + 1, mid, old)
-            stats[t] = jnp.where(lane == 3 * h + 2, lse - hi - mid, old)
+            out = acc / den
+            cols = slice(h * VD, (h + 1) * VD)
+            if first:
+                before = lse_ref[rows, h : h + 1]
+                both = jnp.maximum(before, lse)
+                part, rest = jnp.exp(lse - both), jnp.exp(before - both)
+                out = (out * part + old_ref[rows, cols] * rest) / (part + rest)
+                lse = both + jnp.log(part + rest)
+                hi = lse.astype(jnp.bfloat16).astype(jnp.float32)
+                mid = (lse - hi).astype(jnp.bfloat16).astype(jnp.float32)
+                old = jnp.where(lane == 3 * h, hi, stats[t])
+                old = jnp.where(lane == 3 * h + 1, mid, old)
+                stats[t] = jnp.where(lane == 3 * h + 2, lse - hi - mid, old)
+            else:
+                stats[t] = jnp.where(lane == h, lse, stats[t])
+            o_ref[rows, cols] = out.astype(o_ref.dtype)
         if u < len(units):
             m = jnp.max(top, axis=1, keepdims=True)
     for t in range(ROWS // QT):
-        o_ref[t * QT : (t + 1) * QT, MSG:] = stats[t].astype(jnp.bfloat16)
-
-
-def attend(q, chunks, weights, thr):
-    return pl.pallas_call(
-        attend_kernel,
-        out_shape=jax.ShapeDtypeStruct((ROWS, EXT), jnp.bfloat16),
+        if first:
+            o_ref[t * QT : (t + 1) * QT, MSG:] = stats[t].astype(jnp.bfloat16)
+        else:
+            lse_ref[t * QT : (t + 1) * QT, :] = stats[t]
+
+
+def attend(chunks, q, weights, thr, before=()):
+    count = len(chunks)
+    first = len(CHUNKS) - count if before else 0
+    if before:
+        shape = jax.ShapeDtypeStruct((ROWS, EXT), jnp.bfloat16)
+    else:
+        shape = (
+            jax.ShapeDtypeStruct((ROWS, MSG), jnp.float32),
+            jax.ShapeDtypeStruct((ROWS, 128), jnp.float32),
+        )
+    return pl.pallas_call(
+        functools.partial(attend_kernel, count, first),
+        out_shape=shape,
         scratch_shapes=[
-            pltpu.VMEM((2, KEYS, VAT + VD), jnp.bfloat16),
-            pltpu.VMEM((2, QT, KEYS), jnp.float32),
+            pltpu.VMEM((2, count * FOUR, VAT + VD), jnp.bfloat16),
+            pltpu.VMEM((2, QT, count * FOUR), jnp.float32),
         ],
-        compiler_params=pltpu.CompilerParams(vmem_limit_bytes=32 * 1024 * 1024),
+        compiler_params=pltpu.CompilerParams(vmem_limit_bytes=24 * 1024 * 1024),
         cost_estimate=pl.CostEstimate(
-            flops=6_500_000_000, bytes_accessed=6_000_000, transcendentals=4_200_000
+            flops=1_000_000 * count, bytes_accessed=1_000 * count, transcendentals=1_000 * count
         ),
-        name="attend",
-    )(q, *chunks, weights, thr)
+        name="attend_late" if before else "attend_early",
+    )(*chunks, q, weights, thr, *before)
 
 
 def combine_kernel(x_ref, o_ref):
@@ -174,6 +201,7 @@
     return pl.pallas_call(
         combine_kernel,
         out_shape=jax.ShapeDtypeStruct((GRP, TOK, MSG), jnp.bfloat16),
+        compiler_params=SMALL,
         name="combine",
     )(x)
 
@@ -187,7 +215,10 @@
 
 def pack(latents, key_rope):
     return pl.pallas_call(
-        pack_kernel, out_shape=jax.ShapeDtypeStruct((HALF, L), jnp.bfloat16), name="pack"
+        pack_kernel,
+        out_shape=jax.ShapeDtypeStruct((HALF, L), jnp.bfloat16),
+        compiler_params=SMALL,
+        name="pack",
     )(latents, key_rope)
 
 
@@ -202,7 +233,10 @@
 
 def merge(pieces):
     return pl.pallas_call(
-        merge_kernel, out_shape=jax.ShapeDtypeStruct((FULL, L), jnp.bfloat16), name="merge"
+        merge_kernel,
+        out_shape=jax.ShapeDtypeStruct((FULL, L), jnp.bfloat16),
+        compiler_params=SMALL,
+        name="merge",
     )(*pieces)
 
 
@@ -212,21 +246,25 @@
 
 def gather_keys(latents, key_rope, swap):
     near = [(a * 2 + b, (1 - a) * 2 + 1 - b) for a in range(2) for b in range(2)]
-    up = [(i, (i + 1) % ZN) for i in range(ZN)]
-    down = [(ZN + i, ZN + (i - 1) % ZN) for i in range(ZN)]
     to_core = lambda x: lax.ppermute(x, "core", shift(CN, 1))
+
+    def round_z(x, n):
+        up = [(i, (i + n) % ZN) for i in range(ZN)]
+        down = [(ZN + i, ZN + (i - n) % ZN) for i in range(ZN)]
+        return lax.ppermute(x, ("core", "z"), up + down)
+
     piece = pack(latents, key_rope)
-    beside = lax.ppermute(piece, ("xl", "xh"), near)
-    pieces = [piece, beside, to_core(piece), to_core(beside)]
-    mine = swap(piece)
+    beside, mate = lax.ppermute(piece, ("xl", "xh"), near), to_core(piece)
+    pieces = [piece, beside, mate, to_core(beside)]
+    mine = swap(mate)
     pieces, mine = lax.optimization_barrier((pieces, mine))
     now = merge(pieces)
-    got = {(0, 0): now}
-    for s in range(1, 5):
-        got[0, s] = now = lax.ppermute(now, ("core", "z"), up + down)
-        if s < 4:
-            got[1, s] = to_core(now)
-    return [got[c] for c in CHUNKS], mine, got[0, 1]
+    got = {(0, 0): now, (0, 1): round_z(now, 1), (0, 2): round_z(now, 2)}
+    got[0, 3] = round_z(got[0, 2], 1)
+    got[0, 4] = round_z(got[0, 2], 2)
+    for s in (1, 2):
+        got[1, s] = to_core(got[0, s])
+    return got, to_core, mine, beside
 
 
 def threshold_kernel(pattern_ref, stripe_ref, o_ref):
@@ -260,6 +298,7 @@
         threshold_kernel,
         out_shape=jax.ShapeDtypeStruct((CELLS, KEYS), jnp.float32),
         in_specs=[pl.BlockSpec(memory_space=pltpu.SMEM)] * 2,
+        compiler_params=SMALL,
         name="thresholds",
     )(pattern, stripe)
 
@@ -272,7 +311,7 @@
         send, _ = lax.optimization_barrier((send, after))
         return lax.all_to_all(send, groups, split_axis=0, concat_axis=0, tiled=True)
 
-    chunks, mine, mark = gather_keys(latents, key_rope, swap)
+    got, to_core, mine, mark = gather_keys(latents, key_rope, swap)
     mine = mine.reshape(GRP * TOK, HEADS * QD)
     send = jnp.broadcast_to(mine[None], (CELLS, *mine.shape))
     q = lax.all_to_all(send, cells, split_axis=0, concat_axis=0, tiled=True)
@@ -281,7 +320,11 @@
         (key_up, value_up, pattern, stripe, mark)
     )
     weights = jnp.concatenate([key_up.transpose(0, 2, 1), value_up], axis=2)
-    part = attend(q, chunks, weights, thresholds(pattern, stripe))
+    thr = thresholds(pattern, stripe)
+    before = attend([got[c] for c in EARLY], q, weights, thr)
+    (got[0, 3], got[0, 4]), before = lax.optimization_barrier(((got[0, 3], got[0, 4]), before))
+    got[1, 3] = to_core(got[0, 3])
+    part = attend([got[c] for c in LATE], q, weights, thr, before)
     back = lax.all_to_all(
         part.reshape(CELLS, GRP * TOK, EXT), cells, split_axis=0, concat_axis=0, tiled=True
     )

time: 102 us -> 98.6 us (0.967)
  Pallas kernels: 17.9 us -> 13.7 us
  waiting for transfers between devices: 22.6 us -> 20.8 us
  local copies, waits for them, and re-layouts: 2.64 us -> 4.19 us
    ppermute x5, waiting for transfers between devices: 19.5 us -> 14.5 us  [the longest x4 11.3 us: round_z(): return lax.ppermute(x, ('core', 'z'), up + down)]
    ppermute x5, waiting for transfers between devices: 1.27 us -> 4.11 us  [gather_keys(): to_core = lambda x: lax.ppermute(x, 'core', shift(CN, 1))]
    pallas_call x1, Pallas kernels: 2.26 us -> 0.53 us  [combine(): pl.pallas_call(combine_kernel, out_shape=jax.ShapeDtypeStruct((GRP, TOK,...]
    pallas_call x1, Pallas kernels: 1.73 us -> 0.02 us  [merge(): pl.pallas_call(merge_kernel, out_shape=jax.ShapeDtypeStruct((FULL, L), jn...]
    unnamed x13 -> x11, local copies, waits for them, and re-layouts: 0.65 us -> 2.2 us
    pallas_call x1 -> x2, Pallas kernels: 10.1 us -> 11.6 us  [attend(): pl.pallas_call(functools.partial(attend_kernel, count, first), out_shape=...]
    pallas_call x1, Pallas kernels: 1.54 us -> 0.08 us  [pack(): pl.pallas_call(pack_kernel, out_shape=jax.ShapeDtypeStruct((HALF, L), jnp...]
  transfers between devices with their start and end apart: 12 -> 12, of which waited for: 7 -> 7; matrix products, arithmetic and copies ran while one was open for 3% -> 2% of each run, Pallas kernels for 2% -> 8%
where the time goes in v5:
time: 98.6 us; the launch traced here: 98.2 us
  blocking collectives  35.3 us (36%)
  starting transfers between devices  22.7 us (23%)
  waiting for transfers between devices  20.8 us (21%)
  Pallas kernels  13.7 us (14%)
  local copies, waits for them, and re-layouts  4.19 us (4%)
  other arithmetic  1.32 us (1%)
    all_to_all x1, blocking collectives, body(): lax.all_to_all(combine(back.reshape(ROWS, EXT)), groups, split_axis=0, co...  18.3 us
    all_to_all x1, blocking collectives, body(): lax.all_to_all(part.reshape(CELLS, GRP * TOK, EXT), cells, split_axis=0,...  17 us
    pallas_call x2, Pallas kernels, attend(): pl.pallas_call(functools.partial(attend_kernel, count, first), out_shape=...  11.6 us
    ppermute x4, waiting for transfers between devices, round_z(): return lax.ppermute(x, ('core', 'z'), up + down)  11.3 us
    all_to_all x1, starting transfers between devices, swap(): return lax.all_to_all(send, groups, split_axis=0, concat_axis=0, tiled=True)  11 us
    all_to_all x1, starting transfers between devices, body(): q = lax.all_to_all(send, cells, split_axis=0, concat_axis=0, tiled=True)  4.63 us
    ppermute x5, waiting for transfers between devices, gather_keys(): to_core = lambda x: lax.ppermute(x, 'core', shift(CN, 1))  4.11 us
    ppermute x4, starting transfers between devices, round_z(): return lax.ppermute(x, ('core', 'z'), up + down)  3.94 us
  transfers between devices with their start and end apart: 12, of which 7 were waited for; matrix products, arithmetic and copies ran while one was open for 2% of the time, Pallas kernels for 8%

profile of v5, /device:TPU:32, one launch (start us, length us, event | category | flops | bytes accessed | tf_op | source)
XLA Modules:
  0.0 98.2 jit_solution(14120720594856156325)
XLA Ops:
  0.0 0.8 copy-done
  0.8 0.7 copy-done.1
  1.7 1.3 %collective-permute-done.1.refs_2_ = bf16[80,512]{1,0:T(8,128)(2,1)S(1)} collective-permute-done((bf16[80,512]{1,0:T(8,128)(2,1)S(1)}, bf16[80,512]{1,0:T(8,128)(2,1)S(1)}, u32[]{:S(2)}, u32[]{:S(2)}) %collective-permute-start.1) | collective-permute-done | bytes 81952 | tf_op jit(solution)/shard_map/ppermute | solution.py:249
  2.9 11.0 %all-to-all-start = ((bf16[16,4,768]{2,1,0:T(4,128)(2,1)}), bf16[16,4,768]{2,1,0:T(4,128)(2,1)S(1)}, u32[]{:S(2)}, u32[]{:S(2)}) async-start(bf16[16,4,768]{2,1,0:T(4,128)(2,1)} %bitcast.16), calls=%async_computation | async-start | bytes 196608 | tf_op jit(solution)/shard_map/all_to_all | solution.py:312
  14.0 2.7 %collective-permute-start = (bf16[80,512]{1,0:T(8,128)(2,1)S(1)}, bf16[80,512]{1,0:T(8,128)(2,1)S(1)}, u32[]{:S(2)}, u32[]{:S(2)}) collective-permute-start(bf16[80,512]{1,0:T(8,128)(2,1)S(1)} %pack.1.refs_0_), channel_id=1, source_target_pairs={{0,136},{8,128},{128,8},{136,0},{1,137},{9,129},{129,9},{137,1},{2... | collective-permute-start | bytes 245768 | tf_op jit(solution)/shard_map/ppermute | solution.py:257
  16.7 3.1 %collective-permute-done.refs_1_ = bf16[80,512]{1,0:T(8,128)(2,1)S(1)} collective-permute-done((bf16[80,512]{1,0:T(8,128)(2,1)S(1)}, bf16[80,512]{1,0:T(8,128)(2,1)S(1)}, u32[]{:S(2)}, u32[]{:S(2)}) %collective-permute-start) | collective-permute-done | bytes 81952 | tf_op jit(solution)/shard_map/ppermute | solution.py:257
  19.8 1.3 %collective-permute-done.2.refs_3_ = bf16[80,512]{1,0:T(8,128)(2,1)S(1)} collective-permute-done((bf16[80,512]{1,0:T(8,128)(2,1)S(1)}, bf16[80,512]{1,0:T(8,128)(2,1)S(1)}, u32[]{:S(2)}, u32[]{:S(2)}) %collective-permute-start.2) | collective-permute-done | bytes 81952 | tf_op jit(solution)/shard_map/ppermute | solution.py:249
  21.1 2.2 %all-to-all-done = bf16[16,4,768]{2,1,0:T(4,128)(2,1)S(1)} async-done(((bf16[16,4,768]{2,1,0:T(4,128)(2,1)}), bf16[16,4,768]{2,1,0:T(4,128)(2,1)S(1)}, u32[]{:S(2)}, u32[]{:S(2)}) %all-to-all-start) | async-done | bytes 98336 | tf_op jit(solution)/shard_map/all_to_all | solution.py:312
  23.4 0.9 broadcast_in_dim.8
  24.3 4.6 %all-to-all-start.1 = ((bf16[8,64,768]{2,1,0:T(8,128)(2,1)}), bf16[8,64,768]{2,1,0:T(8,128)(2,1)S(1)}, u32[]{:S(2)}, u32[]{:S(2)}) async-start(bf16[8,64,768]{2,1,0:T(8,128)(2,1)} %broadcast_in_dim.8), calls=%async_computation.1 | async-start | bytes 1572864 | tf_op jit(solution)/shard_map/all_to_all | solution.py:317
  29.0 0.6 collective-permute-start.6
  29.6 2.7 %collective-permute-start.3 = (bf16[288,512]{1,0:T(8,128)(2,1)S(1)}, bf16[288,512]{1,0:T(8,128)(2,1)S(1)}, u32[]{:S(2)}, u32[]{:S(2)}) collective-permute-start(bf16[288,512]{1,0:T(8,128)(2,1)S(1)} %merge.1.refs_0_), channel_id=1, source_target_pairs={{0,2},{1,3},{2,4},{3,5},{4,6},{5,7},{6,0},{7,1},{16,22},{17,23},{1... | collective-permute-start | bytes 884744 | tf_op jit(solution)/shard_map/ppermute | solution.py:254
  32.2 3.6 %collective-permute-done.6.refs_1_ = bf16[288,512]{1,0:T(8,128)(2,1)S(1)} collective-permute-done((bf16[288,512]{1,0:T(8,128)(2,1)S(1)}, bf16[288,512]{1,0:T(8,128)(2,1)S(1)}, u32[]{:S(2)}, u32[]{:S(2)}) %collective-permute-start.6) | collective-permute-done | bytes 294944 | tf_op jit(solution)/shard_map/ppermute | solution.py:254
  35.8 7.8 %collective-permute-done.3.refs_3_ = bf16[288,512]{1,0:T(8,128)(2,1)S(1)} collective-permute-done((bf16[288,512]{1,0:T(8,128)(2,1)S(1)}, bf16[288,512]{1,0:T(8,128)(2,1)S(1)}, u32[]{:S(2)}, u32[]{:S(2)}) %collective-permute-start.3) | collective-permute-done | bytes 294944 | tf_op jit(solution)/shard_map/ppermute | solution.py:254
  43.6 0.7 collective-permute-start.5
  44.3 1.0 %copy.10 = bf16[4,128,512]{1,2,0:T(8,128)(2,1)} copy(bf16[4,128,512]{2,1,0:T(8,128)(2,1)S(1)} %copy-done.4) | data formatting | bytes 1048576 | tf_op jit(solution)/shard_map/optimization_barrier | solution.py:319
  45.3 1.5 %thresholds.1.refs_7_.refs_5_ = f32[8,2048]{1,0:T(8,128)S(1)} custom-call(s32[8,128]{1,0:T(8,128)S(1)} %copy-done.2, s32[128]{0:T(128)S(1)} %copy-done.3), custom_call_target="tpu_custom_call" | custom-call | tf_op jit(solution)/shard_map/thresholds/pallas_call | solution.py:297
  46.8 1.3 %pad_maximum_fusion.refs_6_.refs_4_ = bf16[4,512,256]{2,1,0:T(8,128)(2,1)S(1)} fusion(bf16[4,512,128]{2,1,0:T(8,128)(2,1)} %param.11, bf16[4,512,128]{2,1,0:T(8,128)(2,1)} %bitcast.14), kind=kLoop, calls=%fused_computation | loop fusion | flops 2097152 | bytes 2097152 | tf_op jit(solution)/shard_map/concatenate | solution.py:322
  48.2 6.7 %attend_early.1 = (f32[512,512]{1,0:T(8,128)S(1)}, f32[512,128]{1,0:T(8,128)S(1)}) custom-call(bf16[288,512]{1,0:T(8,128)(2,1)S(1)} %merge.1.refs_0_, bf16[288,512]{1,0:T(8,128)(2,1)S(1)} %collective-permute-done.6.refs_1_, bf16[288,512]{1,0:T(8,128)(2,1)} %collective-permute-done.7.refs_2_, bf16[288,512]{1,0:T(8,128)(2,1)S(1)} %collective-permute-done.3.refs_3_, ...), custom_call_target="tpu_custom_call" | custom-call | flops 5000000 | bytes 5000 | tf_op jit(solution)/shard_map/attend_early/pallas_call | solution.py:168
  55.2 1.6 %collective-permute-done.9.refs_1_ = bf16[288,512]{1,0:T(8,128)(2,1)S(1)} collective-permute-done((bf16[288,512]{1,0:T(8,128)(2,1)S(1)}, bf16[288,512]{1,0:T(8,128)(2,1)S(1)}, u32[]{:S(2)}, u32[]{:S(2)}) %collective-permute-start.9) | collective-permute-done | bytes 294944 | tf_op jit(solution)/shard_map/ppermute | solution.py:249
  56.8 4.9 %attend_late.1 = bf16[512,640]{1,0:T(8,128)(2,1)S(1)} custom-call(bf16[288,512]{1,0:T(8,128)(2,1)S(1)} %collective-permute-done.4.refs_0_, bf16[288,512]{1,0:T(8,128)(2,1)S(1)} %collective-permute-done.9.refs_1_, bf16[288,512]{1,0:T(8,128)(2,1)S(1)} %collective-permute-done.5.refs_2_, bf16[512,768]{1,0:T(8,128)(2,1)S(1)} %bitcast.11, ...), custom_call_target="tpu_custom_call" | custom-call | flops 3000000 | bytes 3000 | tf_op jit(solution)/shard_map/attend_late/pallas_call | solution.py:168
  61.7 17.0 %all_to_all.20 = bf16[8,64,640]{2,1,0:T(8,128)(2,1)S(1)} all-to-all(bf16[8,64,640]{2,1,0:T(8,128)(2,1)S(1)} %bitcast.12), channel_id=1, replica_groups=mesh['xl'=2,'y'=4,'core'=2,'xh'=2,'z'=8] {'xl','y'}, dimensions={0} | all-to-all | bytes 1310720 | tf_op jit(solution)/shard_map/all_to_all | solution.py:328
  79.2 18.3 %all_to_all.21 = bf16[16,4,512]{2,1,0:T(4,128)(2,1)S(1)} all-to-all(bf16[16,4,512]{2,1,0:T(4,128)(2,1)S(1)} %combine.1), channel_id=1, replica_groups=mesh['xl'=2,'y'=4,'core'=2,'xh'=2,'z'=8] {'xh','z'}, dimensions={0} | all-to-all | bytes 131072 | tf_op jit(solution)/shard_map/all_to_all | solution.py:331
  97.5 0.6 copy.12
  (23 shorter events, 1.0 us)
Async XLA Ops:
  0.0 0.8 copy-start
  0.8 0.7 copy-start.1
  1.6 1.3 %collective-permute-start.1 = (bf16[80,512]{1,0:T(8,128)(2,1)S(1)}, bf16[80,512]{1,0:T(8,128)(2,1)S(1)}, u32[]{:S(2)}, u32[]{:S(2)}) collective-permute-start(bf16[80,512]{1,0:T(8,128)(2,1)S(1)} %pack.1.refs_0_), channel_id=1, source_target_pairs={{0,16},{16,0},{1,17},{17,1},{2,18},{18,2},{3,19},{19,3},{4,20},{20... | collective-permute-start | bytes 245768 | tf_op jit(solution)/shard_map/ppermute | solution.py:249
  2.9 20.4 %all-to-all-start = ((bf16[16,4,768]{2,1,0:T(4,128)(2,1)}), bf16[16,4,768]{2,1,0:T(4,128)(2,1)S(1)}, u32[]{:S(2)}, u32[]{:S(2)}) async-start(bf16[16,4,768]{2,1,0:T(4,128)(2,1)} %bitcast.16), calls=%async_computation | async-start | bytes 196608 | tf_op jit(solution)/shard_map/all_to_all | solution.py:312
  14.0 5.9 %collective-permute-start = (bf16[80,512]{1,0:T(8,128)(2,1)S(1)}, bf16[80,512]{1,0:T(8,128)(2,1)S(1)}, u32[]{:S(2)}, u32[]{:S(2)}) collective-permute-start(bf16[80,512]{1,0:T(8,128)(2,1)S(1)} %pack.1.refs_0_), channel_id=1, source_target_pairs={{0,136},{8,128},{128,8},{136,0},{1,137},{9,129},{129,9},{137,1},{2... | collective-permute-start | bytes 245768 | tf_op jit(solution)/shard_map/ppermute | solution.py:257
  19.8 1.3 %collective-permute-start.2 = (bf16[80,512]{1,0:T(8,128)(2,1)S(1)}, bf16[80,512]{1,0:T(8,128)(2,1)S(1)}, u32[]{:S(2)}, u32[]{:S(2)}) collective-permute-start(bf16[80,512]{1,0:T(8,128)(2,1)S(1)} %collective-permute-done.refs_1_), channel_id=1, source_target_pairs={{0,16},{16,0},{1,17},{17,1},{2,18},{18,2},{3,19},{19,3},{4,20},{20... | collective-permute-start | bytes 245768 | tf_op jit(solution)/shard_map/ppermute | solution.py:249
  24.3 20.0 %copy-start.4 = (bf16[4,128,512]{2,1,0:T(8,128)(2,1)S(1)}, bf16[4,128,512]{2,1,0:T(8,128)(2,1)}, u32[]{:S(2)}) copy-start(bf16[4,128,512]{2,1,0:T(8,128)(2,1)} %param.10) | copy-start | bytes 1572868
  24.3 23.9 %all-to-all-start.1 = ((bf16[8,64,768]{2,1,0:T(8,128)(2,1)}), bf16[8,64,768]{2,1,0:T(8,128)(2,1)S(1)}, u32[]{:S(2)}, u32[]{:S(2)}) async-start(bf16[8,64,768]{2,1,0:T(8,128)(2,1)} %broadcast_in_dim.8), calls=%async_computation.1 | async-start | bytes 1572864 | tf_op jit(solution)/shard_map/all_to_all | solution.py:317
  28.9 16.4 %copy-start.2 = (s32[8,128]{1,0:T(8,128)S(1)}, s32[8,128]{1,0:T(8,128)}, u32[]{:S(2)}) copy-start(s32[8,128]{1,0:T(8,128)} %pattern_ref) | copy-start | bytes 12292
  28.9 16.4 %copy-start.3 = (s32[128]{0:T(128)S(1)}, s32[128]{0:T(128)}, u32[]{:S(2)}) copy-start(s32[128]{0:T(128)} %stripe_ref) | copy-start | bytes 1540
  29.0 6.8 %collective-permute-start.6 = (bf16[288,512]{1,0:T(8,128)(2,1)S(1)}, bf16[288,512]{1,0:T(8,128)(2,1)S(1)}, u32[]{:S(2)}, u32[]{:S(2)}) collective-permute-start(bf16[288,512]{1,0:T(8,128)(2,1)S(1)} %merge.1.refs_0_), channel_id=1, source_target_pairs={{0,1},{1,2},{2,3},{3,4},{4,5},{5,6},{6,7},{7,0},{16,23},{17,16},{1... | collective-permute-start | bytes 884744 | tf_op jit(solution)/shard_map/ppermute | solution.py:254
  29.6 14.0 %collective-permute-start.3 = (bf16[288,512]{1,0:T(8,128)(2,1)S(1)}, bf16[288,512]{1,0:T(8,128)(2,1)S(1)}, u32[]{:S(2)}, u32[]{:S(2)}) collective-permute-start(bf16[288,512]{1,0:T(8,128)(2,1)S(1)} %merge.1.refs_0_), channel_id=1, source_target_pairs={{0,2},{1,3},{2,4},{3,5},{4,6},{5,7},{6,0},{7,1},{16,22},{17,23},{1... | collective-permute-start | bytes 884744 | tf_op jit(solution)/shard_map/ppermute | solution.py:254
  35.8 12.4 %collective-permute-start.7 = (bf16[288,512]{1,0:T(8,128)(2,1)S(1)}, bf16[288,512]{1,0:T(8,128)(2,1)}, u32[]{:S(2)}, u32[]{:S(2)}) collective-permute-start(bf16[288,512]{1,0:T(8,128)(2,1)S(1)} %collective-permute-done.6.refs_1_), channel_id=1, source_target_pairs={{0,16},{16,0},{1,17},{17,1},{2,18},{18,2},{3,19},{19,3},{4,20},{20... | collective-permute-start | bytes 884744 | tf_op jit(solution)/shard_map/ppermute | solution.py:249
  43.6 4.6 %collective-permute-start.8 = (bf16[288,512]{1,0:T(8,128)(2,1)S(1)}, bf16[288,512]{1,0:T(8,128)(2,1)}, u32[]{:S(2)}, u32[]{:S(2)}) collective-permute-start(bf16[288,512]{1,0:T(8,128)(2,1)S(1)} %collective-permute-done.3.refs_3_), channel_id=1, source_target_pairs={{0,16},{16,0},{1,17},{17,1},{2,18},{18,2},{3,19},{19,3},{4,20},{20... | collective-permute-start | bytes 884744 | tf_op jit(solution)/shard_map/ppermute | solution.py:249
  43.6 11.3 %collective-permute-start.4 = (bf16[288,512]{1,0:T(8,128)(2,1)S(1)}, bf16[288,512]{1,0:T(8,128)(2,1)S(1)}, u32[]{:S(2)}, u32[]{:S(2)}) collective-permute-start(bf16[288,512]{1,0:T(8,128)(2,1)S(1)} %collective-permute-done.3.refs_3_), channel_id=1, source_target_pairs={{0,1},{1,2},{2,3},{3,4},{4,5},{5,6},{6,7},{7,0},{16,23},{17,16},{1... | collective-permute-start | bytes 884744 | tf_op jit(solution)/shard_map/ppermute | solution.py:254
  43.6 11.3 %collective-permute-start.5 = (bf16[288,512]{1,0:T(8,128)(2,1)S(1)}, bf16[288,512]{1,0:T(8,128)(2,1)S(1)}, u32[]{:S(2)}, u32[]{:S(2)}) collective-permute-start(bf16[288,512]{1,0:T(8,128)(2,1)S(1)} %collective-permute-done.3.refs_3_), channel_id=1, source_target_pairs={{0,2},{1,3},{2,4},{3,5},{4,6},{5,7},{6,0},{7,1},{16,22},{17,23},{1... | collective-permute-start | bytes 884744 | tf_op jit(solution)/shard_map/ppermute | solution.py:254
  54.9 1.9 %collective-permute-start.9 = (bf16[288,512]{1,0:T(8,128)(2,1)S(1)}, bf16[288,512]{1,0:T(8,128)(2,1)S(1)}, u32[]{:S(2)}, u32[]{:S(2)}) collective-permute-start(bf16[288,512]{1,0:T(8,128)(2,1)S(1)} %collective-permute-done.4.refs_0_), channel_id=1, source_target_pairs={{0,16},{16,0},{1,17},{17,1},{2,18},{18,2},{3,19},{19,3},{4,20},{20... | collective-permute-start | bytes 884744 | tf_op jit(solution)/shard_map/ppermute | solution.py:249

commit v6 on v5

--- a/solution.py
+++ b/solution.py
@@ -257,11 +257,12 @@
     beside, mate = lax.ppermute(piece, ("xl", "xh"), near), to_core(piece)
     pieces = [piece, beside, mate, to_core(beside)]
     mine = swap(mate)
-    pieces, mine = lax.optimization_barrier((pieces, mine))
     now = merge(pieces)
     got = {(0, 0): now, (0, 1): round_z(now, 1), (0, 2): round_z(now, 2)}
-    got[0, 3] = round_z(got[0, 2], 1)
-    got[0, 4] = round_z(got[0, 2], 2)
+    got[0, 1], got[0, 2], mine = lax.optimization_barrier((got[0, 1], got[0, 2], mine))
+    after = got[0, 2]
+    got[0, 3] = round_z(after, 1)
+    got[0, 4] = round_z(after, 2)
     for s in (1, 2):
         got[1, s] = to_core(got[0, s])
     return got, to_core, mine, beside

time: 98.6 us -> 93.6 us (0.949)
  waiting for transfers between devices: 20.8 us -> 9.63 us
  blocking collectives: 35.3 us -> 45.5 us
  starting transfers between devices: 22.7 us -> 18.6 us
    all_to_all x0 -> x1, blocking collectives: none -> 15.3 us  [swap(): return lax.all_to_all(send, groups, split_axis=0, concat_axis=0, tiled=True)]
    ppermute x4, waiting for transfers between devices: 11.3 us -> 0.01 us  [round_z(): return lax.ppermute(x, ('core', 'z'), up + down)]
    all_to_all x1 -> x0, starting transfers between devices: 11 us -> none  [swap(): return lax.all_to_all(send, groups, split_axis=0, concat_axis=0, tiled=True)]
    ppermute x4, starting transfers between devices: 3.94 us -> 9.12 us  [round_z(): return lax.ppermute(x, ('core', 'z'), up + down)]
    all_to_all x1, waiting for transfers between devices: 0.01 us -> 3.89 us  [body(): q = lax.all_to_all(send, cells, split_axis=0, concat_axis=0, tiled=True)]
    all_to_all x1, blocking collectives: 18.3 us -> 15.4 us  [body(): lax.all_to_all(combine(back.reshape(ROWS, EXT)), groups, split_axis=0, co...]
    all_to_all x1 -> x0, waiting for transfers between devices: 2.21 us -> none  [swap(): return lax.all_to_all(send, groups, split_axis=0, concat_axis=0, tiled=True)]
    all_to_all x1, blocking collectives: 17 us -> 14.9 us  [body(): lax.all_to_all(part.reshape(CELLS, GRP * TOK, EXT), cells, split_axis=0,...]
  transfers between devices with their start and end apart: 12 -> 11, of which waited for: 7 -> 4; matrix products, arithmetic and copies ran while one was open for 2% -> 3% of each run, Pallas kernels for 8% -> 9%
where the time goes in v6:
time: 93.6 us; the launch traced here: 93.1 us
  blocking collectives  45.5 us (49%)
  starting transfers between devices  18.6 us (20%)
  Pallas kernels  13.7 us (15%)
  waiting for transfers between devices  9.63 us (10%)
  local copies, waits for them, and re-layouts  4.19 us (4%)
  other arithmetic  1.32 us (1%)
    all_to_all x1, blocking collectives, body(): lax.all_to_all(combine(back.reshape(ROWS, EXT)), groups, split_axis=0, co...  15.4 us
    all_to_all x1, blocking collectives, swap(): return lax.all_to_all(send, groups, split_axis=0, concat_axis=0, tiled=True)  15.3 us
    all_to_all x1, blocking collectives, body(): lax.all_to_all(part.reshape(CELLS, GRP * TOK, EXT), cells, split_axis=0,...  14.9 us
    pallas_call x2, Pallas kernels, attend(): pl.pallas_call(functools.partial(attend_kernel, count, first), out_shape=...  11.6 us
    ppermute x4, starting transfers between devices, round_z(): return lax.ppermute(x, ('core', 'z'), up + down)  9.12 us
    all_to_all x1, starting transfers between devices, body(): q = lax.all_to_all(send, cells, split_axis=0, concat_axis=0, tiled=True)  5.84 us
    all_to_all x1, waiting for transfers between devices, body(): q = lax.all_to_all(send, cells, split_axis=0, concat_axis=0, tiled=True)  3.89 us
    ppermute x1, waiting for transfers between devices, gather_keys(): beside, mate = (lax.ppermute(piece, ('xl', 'xh'), near), to_core(piece))  2.89 us
  transfers between devices with their start and end apart: 11, of which 4 were waited for; matrix products, arithmetic and copies ran while one was open for 3% of the time, Pallas kernels for 9%

profile of v6, /device:TPU:32, one launch (start us, length us, event | category | flops | bytes accessed | tf_op | source)
XLA Modules:
  0.0 93.1 jit_solution(13368903876822922838)
XLA Ops:
  0.0 0.8 copy-done
  0.8 0.7 copy-done.1
  1.6 2.8 %collective-permute-start = (bf16[80,512]{1,0:T(8,128)(2,1)S(1)}, bf16[80,512]{1,0:T(8,128)(2,1)S(1)}, u32[]{:S(2)}, u32[]{:S(2)}) collective-permute-start(bf16[80,512]{1,0:T(8,128)(2,1)S(1)} %pack.1.refs_0_), channel_id=1, source_target_pairs={{0,136},{8,128},{128,8},{136,0},{1,137},{9,129},{129,9},{137,1},{2... | collective-permute-start | bytes 245768 | tf_op jit(solution)/shard_map/ppermute | solution.py:257
  4.4 2.9 %collective-permute-done.refs_1_ = bf16[80,512]{1,0:T(8,128)(2,1)S(1)} collective-permute-done((bf16[80,512]{1,0:T(8,128)(2,1)S(1)}, bf16[80,512]{1,0:T(8,128)(2,1)S(1)}, u32[]{:S(2)}, u32[]{:S(2)}) %collective-permute-start) | collective-permute-done | bytes 81952 | tf_op jit(solution)/shard_map/ppermute | solution.py:257
  7.3 1.3 %collective-permute-done.2.refs_3_ = bf16[80,512]{1,0:T(8,128)(2,1)S(1)} collective-permute-done((bf16[80,512]{1,0:T(8,128)(2,1)S(1)}, bf16[80,512]{1,0:T(8,128)(2,1)S(1)}, u32[]{:S(2)}, u32[]{:S(2)}) %collective-permute-start.2) | collective-permute-done | bytes 81952 | tf_op jit(solution)/shard_map/ppermute | solution.py:249
  8.6 2.0 %collective-permute-start.3 = (bf16[288,512]{1,0:T(8,128)(2,1)S(1)}, bf16[288,512]{1,0:T(8,128)(2,1)S(1)}, u32[]{:S(2)}, u32[]{:S(2)}) collective-permute-start(bf16[288,512]{1,0:T(8,128)(2,1)S(1)} %merge.1.refs_0_), channel_id=1, source_target_pairs={{0,1},{1,2},{2,3},{3,4},{4,5},{5,6},{6,7},{7,0},{16,23},{17,16},{1... | collective-permute-start | bytes 884744 | tf_op jit(solution)/shard_map/ppermute | solution.py:254
  10.6 4.5 %collective-permute-start.4 = (bf16[288,512]{1,0:T(8,128)(2,1)S(1)}, bf16[288,512]{1,0:T(8,128)(2,1)S(1)}, u32[]{:S(2)}, u32[]{:S(2)}) collective-permute-start(bf16[288,512]{1,0:T(8,128)(2,1)S(1)} %merge.1.refs_0_), channel_id=1, source_target_pairs={{0,2},{1,3},{2,4},{3,5},{4,6},{5,7},{6,0},{7,1},{16,22},{17,23},{1... | collective-permute-start | bytes 884744 | tf_op jit(solution)/shard_map/ppermute | solution.py:254
  15.1 15.3 %all_to_all.20 = bf16[16,4,768]{2,1,0:T(4,128)(2,1)S(1)} all-to-all(bf16[16,4,768]{2,1,0:T(4,128)(2,1)} %bitcast.16), channel_id=1, replica_groups=mesh['xl'=2,'y'=4,'core'=2,'xh'=2,'z'=8] {'xh','z'}, dimensions={0} | all-to-all | bytes 196608 | tf_op jit(solution)/shard_map/all_to_all | solution.py:313
  30.4 1.0 %broadcast_in_dim.8 = bf16[8,64,768]{2,1,0:T(8,128)(2,1)} broadcast(bf16[64,768]{1,0:T(8,128)(2,1)S(1)} %broadcast_in_dim.7), dimensions={1,2} | broadcast | bytes 884736 | tf_op jit(solution)/shard_map/broadcast_in_dim | solution.py:317
  31.4 5.8 %all-to-all-start.1 = ((bf16[8,64,768]{2,1,0:T(8,128)(2,1)}), bf16[8,64,768]{2,1,0:T(8,128)(2,1)S(1)}, u32[]{:S(2)}, u32[]{:S(2)}) async-start(bf16[8,64,768]{2,1,0:T(8,128)(2,1)} %broadcast_in_dim.8), calls=%async_computation.1 | async-start | bytes 1572864 | tf_op jit(solution)/shard_map/all_to_all | solution.py:318
  37.2 0.5 collective-permute-start.7
  37.7 0.6 collective-permute-start.5
  38.3 2.1 %collective-permute-start.6 = (bf16[288,512]{1,0:T(8,128)(2,1)S(1)}, bf16[288,512]{1,0:T(8,128)(2,1)S(1)}, u32[]{:S(2)}, u32[]{:S(2)}) collective-permute-start(bf16[288,512]{1,0:T(8,128)(2,1)S(1)} %collective-permute-done.4.refs_3_), channel_id=1, source_target_pairs={{0,2},{1,3},{2,4},{3,5},{4,6},{5,7},{6,0},{7,1},{16,22},{17,23},{1... | collective-permute-start | bytes 884744 | tf_op jit(solution)/shard_map/ppermute | solution.py:254
  40.4 1.0 %copy.10 = bf16[4,128,512]{1,2,0:T(8,128)(2,1)} copy(bf16[4,128,512]{2,1,0:T(8,128)(2,1)S(1)} %copy-done.4) | data formatting | bytes 1048576 | tf_op jit(solution)/shard_map/optimization_barrier | solution.py:320
  41.4 1.5 %thresholds.1.refs_7_.refs_5_ = f32[8,2048]{1,0:T(8,128)S(1)} custom-call(s32[8,128]{1,0:T(8,128)S(1)} %copy-done.2, s32[128]{0:T(128)S(1)} %copy-done.3), custom_call_target="tpu_custom_call" | custom-call | tf_op jit(solution)/shard_map/thresholds/pallas_call | solution.py:298
  42.9 1.3 %pad_maximum_fusion.refs_6_.refs_4_ = bf16[4,512,256]{2,1,0:T(8,128)(2,1)S(1)} fusion(bf16[4,512,128]{2,1,0:T(8,128)(2,1)} %param.11, bf16[4,512,128]{2,1,0:T(8,128)(2,1)} %bitcast.14), kind=kLoop, calls=%fused_computation | loop fusion | flops 2097152 | bytes 2097152 | tf_op jit(solution)/shard_map/concatenate | solution.py:323
  44.3 3.9 %all-to-all-done.1 = bf16[8,64,768]{2,1,0:T(8,128)(2,1)S(1)} async-done(((bf16[8,64,768]{2,1,0:T(8,128)(2,1)}), bf16[8,64,768]{2,1,0:T(8,128)(2,1)S(1)}, u32[]{:S(2)}, u32[]{:S(2)}) %all-to-all-start.1) | async-done | bytes 786464 | tf_op jit(solution)/shard_map/all_to_all | solution.py:318
  48.1 6.7 %attend_early.1 = (f32[512,512]{1,0:T(8,128)S(1)}, f32[512,128]{1,0:T(8,128)S(1)}) custom-call(bf16[288,512]{1,0:T(8,128)(2,1)S(1)} %merge.1.refs_0_, bf16[288,512]{1,0:T(8,128)(2,1)S(1)} %collective-permute-done.3.refs_1_, bf16[288,512]{1,0:T(8,128)(2,1)} %collective-permute-done.7.refs_2_, bf16[288,512]{1,0:T(8,128)(2,1)S(1)} %collective-permute-done.4.refs_3_, ...), custom_call_target="tpu_custom_call" | custom-call | flops 5000000 | bytes 5000 | tf_op jit(solution)/shard_map/attend_early/pallas_call | solution.py:168
  55.2 1.6 %collective-permute-done.9.refs_1_ = bf16[288,512]{1,0:T(8,128)(2,1)S(1)} collective-permute-done((bf16[288,512]{1,0:T(8,128)(2,1)S(1)}, bf16[288,512]{1,0:T(8,128)(2,1)S(1)}, u32[]{:S(2)}, u32[]{:S(2)}) %collective-permute-start.9) | collective-permute-done | bytes 294944 | tf_op jit(solution)/shard_map/ppermute | solution.py:249
  56.7 4.9 %attend_late.1 = bf16[512,640]{1,0:T(8,128)(2,1)S(1)} custom-call(bf16[288,512]{1,0:T(8,128)(2,1)S(1)} %collective-permute-done.5.refs_0_, bf16[288,512]{1,0:T(8,128)(2,1)S(1)} %collective-permute-done.9.refs_1_, bf16[288,512]{1,0:T(8,128)(2,1)S(1)} %collective-permute-done.6.refs_2_, bf16[512,768]{1,0:T(8,128)(2,1)S(1)} %bitcast.11, ...), custom_call_target="tpu_custom_call" | custom-call | flops 3000000 | bytes 3000 | tf_op jit(solution)/shard_map/attend_late/pallas_call | solution.py:168
  61.7 14.9 %all_to_all.21 = bf16[8,64,640]{2,1,0:T(8,128)(2,1)S(1)} all-to-all(bf16[8,64,640]{2,1,0:T(8,128)(2,1)S(1)} %bitcast.12), channel_id=1, replica_groups=mesh['xl'=2,'y'=4,'core'=2,'xh'=2,'z'=8] {'xl','y'}, dimensions={0} | all-to-all | bytes 1310720 | tf_op jit(solution)/shard_map/all_to_all | solution.py:329
  76.5 0.5 combine.1
  77.1 15.4 %all_to_all.22 = bf16[16,4,512]{2,1,0:T(4,128)(2,1)S(1)} all-to-all(bf16[16,4,512]{2,1,0:T(4,128)(2,1)S(1)} %combine.1), channel_id=1, replica_groups=mesh['xl'=2,'y'=4,'core'=2,'xh'=2,'z'=8] {'xh','z'}, dimensions={0} | all-to-all | bytes 131072 | tf_op jit(solution)/shard_map/all_to_all | solution.py:332
  92.5 0.6 copy.12
  (22 shorter events, 0.5 us)
Async XLA Ops:
  0.0 0.8 copy-start
  0.8 0.7 copy-start.1
  1.6 5.7 %collective-permute-start = (bf16[80,512]{1,0:T(8,128)(2,1)S(1)}, bf16[80,512]{1,0:T(8,128)(2,1)S(1)}, u32[]{:S(2)}, u32[]{:S(2)}) collective-permute-start(bf16[80,512]{1,0:T(8,128)(2,1)S(1)} %pack.1.refs_0_), channel_id=1, source_target_pairs={{0,136},{8,128},{128,8},{136,0},{1,137},{9,129},{129,9},{137,1},{2... | collective-permute-start | bytes 245768 | tf_op jit(solution)/shard_map/ppermute | solution.py:257
  4.4 2.9 %collective-permute-start.1 = (bf16[80,512]{1,0:T(8,128)(2,1)S(1)}, bf16[80,512]{1,0:T(8,128)(2,1)S(1)}, u32[]{:S(2)}, u32[]{:S(2)}) collective-permute-start(bf16[80,512]{1,0:T(8,128)(2,1)S(1)} %pack.1.refs_0_), channel_id=1, source_target_pairs={{0,16},{16,0},{1,17},{17,1},{2,18},{18,2},{3,19},{19,3},{4,20},{20... | collective-permute-start | bytes 245768 | tf_op jit(solution)/shard_map/ppermute | solution.py:249
  7.3 1.3 %collective-permute-start.2 = (bf16[80,512]{1,0:T(8,128)(2,1)S(1)}, bf16[80,512]{1,0:T(8,128)(2,1)S(1)}, u32[]{:S(2)}, u32[]{:S(2)}) collective-permute-start(bf16[80,512]{1,0:T(8,128)(2,1)S(1)} %collective-permute-done.refs_1_), channel_id=1, source_target_pairs={{0,16},{16,0},{1,17},{17,1},{2,18},{18,2},{3,19},{19,3},{4,20},{20... | collective-permute-start | bytes 245768 | tf_op jit(solution)/shard_map/ppermute | solution.py:249
  8.6 21.7 %collective-permute-start.3 = (bf16[288,512]{1,0:T(8,128)(2,1)S(1)}, bf16[288,512]{1,0:T(8,128)(2,1)S(1)}, u32[]{:S(2)}, u32[]{:S(2)}) collective-permute-start(bf16[288,512]{1,0:T(8,128)(2,1)S(1)} %merge.1.refs_0_), channel_id=1, source_target_pairs={{0,1},{1,2},{2,3},{3,4},{4,5},{5,6},{6,7},{7,0},{16,23},{17,16},{1... | collective-permute-start | bytes 884744 | tf_op jit(solution)/shard_map/ppermute | solution.py:254
  10.6 19.7 %collective-permute-start.4 = (bf16[288,512]{1,0:T(8,128)(2,1)S(1)}, bf16[288,512]{1,0:T(8,128)(2,1)S(1)}, u32[]{:S(2)}, u32[]{:S(2)}) collective-permute-start(bf16[288,512]{1,0:T(8,128)(2,1)S(1)} %merge.1.refs_0_), channel_id=1, source_target_pairs={{0,2},{1,3},{2,4},{3,5},{4,6},{5,7},{6,0},{7,1},{16,22},{17,23},{1... | collective-permute-start | bytes 884744 | tf_op jit(solution)/shard_map/ppermute | solution.py:254
  30.4 10.0 %copy-start.4 = (bf16[4,128,512]{2,1,0:T(8,128)(2,1)S(1)}, bf16[4,128,512]{2,1,0:T(8,128)(2,1)}, u32[]{:S(2)}) copy-start(bf16[4,128,512]{2,1,0:T(8,128)(2,1)} %param.10) | copy-start | bytes 1572868
  31.4 10.0 %copy-start.2 = (s32[8,128]{1,0:T(8,128)S(1)}, s32[8,128]{1,0:T(8,128)}, u32[]{:S(2)}) copy-start(s32[8,128]{1,0:T(8,128)} %pattern_ref) | copy-start | bytes 12292
  31.4 10.0 %copy-start.3 = (s32[128]{0:T(128)S(1)}, s32[128]{0:T(128)}, u32[]{:S(2)}) copy-start(s32[128]{0:T(128)} %stripe_ref) | copy-start | bytes 1540
  31.4 16.8 %all-to-all-start.1 = ((bf16[8,64,768]{2,1,0:T(8,128)(2,1)}), bf16[8,64,768]{2,1,0:T(8,128)(2,1)S(1)}, u32[]{:S(2)}, u32[]{:S(2)}) async-start(bf16[8,64,768]{2,1,0:T(8,128)(2,1)} %broadcast_in_dim.8), calls=%async_computation.1 | async-start | bytes 1572864 | tf_op jit(solution)/shard_map/all_to_all | solution.py:318
  37.2 7.0 %collective-permute-start.8 = (bf16[288,512]{1,0:T(8,128)(2,1)S(1)}, bf16[288,512]{1,0:T(8,128)(2,1)}, u32[]{:S(2)}, u32[]{:S(2)}) collective-permute-start(bf16[288,512]{1,0:T(8,128)(2,1)S(1)} %collective-permute-done.4.refs_3_), channel_id=1, source_target_pairs={{0,16},{16,0},{1,17},{17,1},{2,18},{18,2},{3,19},{19,3},{4,20},{20... | collective-permute-start | bytes 884744 | tf_op jit(solution)/shard_map/ppermute | solution.py:249
  37.2 7.0 %collective-permute-start.7 = (bf16[288,512]{1,0:T(8,128)(2,1)S(1)}, bf16[288,512]{1,0:T(8,128)(2,1)}, u32[]{:S(2)}, u32[]{:S(2)}) collective-permute-start(bf16[288,512]{1,0:T(8,128)(2,1)S(1)} %collective-permute-done.3.refs_1_), channel_id=1, source_target_pairs={{0,16},{16,0},{1,17},{17,1},{2,18},{18,2},{3,19},{19,3},{4,20},{20... | collective-permute-start | bytes 884744 | tf_op jit(solution)/shard_map/ppermute | solution.py:249
  37.7 17.1 %collective-permute-start.5 = (bf16[288,512]{1,0:T(8,128)(2,1)S(1)}, bf16[288,512]{1,0:T(8,128)(2,1)S(1)}, u32[]{:S(2)}, u32[]{:S(2)}) collective-permute-start(bf16[288,512]{1,0:T(8,128)(2,1)S(1)} %collective-permute-done.4.refs_3_), channel_id=1, source_target_pairs={{0,1},{1,2},{2,3},{3,4},{4,5},{5,6},{6,7},{7,0},{16,23},{17,16},{1... | collective-permute-start | bytes 884744 | tf_op jit(solution)/shard_map/ppermute | solution.py:254
  38.3 16.6 %collective-permute-start.6 = (bf16[288,512]{1,0:T(8,128)(2,1)S(1)}, bf16[288,512]{1,0:T(8,128)(2,1)S(1)}, u32[]{:S(2)}, u32[]{:S(2)}) collective-permute-start(bf16[288,512]{1,0:T(8,128)(2,1)S(1)} %collective-permute-done.4.refs_3_), channel_id=1, source_target_pairs={{0,2},{1,3},{2,4},{3,5},{4,6},{5,7},{6,0},{7,1},{16,22},{17,23},{1... | collective-permute-start | bytes 884744 | tf_op jit(solution)/shard_map/ppermute | solution.py:254
  54.8 1.9 %collective-permute-start.9 = (bf16[288,512]{1,0:T(8,128)(2,1)S(1)}, bf16[288,512]{1,0:T(8,128)(2,1)S(1)}, u32[]{:S(2)}, u32[]{:S(2)}) collective-permute-start(bf16[288,512]{1,0:T(8,128)(2,1)S(1)} %collective-permute-done.5.refs_0_), channel_id=1, source_target_pairs={{0,16},{16,0},{1,17},{17,1},{2,18},{18,2},{3,19},{19,3},{4,20},{20... | collective-permute-start | bytes 884744 | tf_op jit(solution)/shard_map/ppermute | solution.py:249

commit v7 on v5

--- a/solution.py
+++ b/solution.py
@@ -35,9 +35,8 @@
 FULL = FOUR + 32
 
 EARLY = [(0, 0)] + [(o, s) for s in (1, 2) for o in (0, 1)]
-LATE = [(0, 3), (1, 3), (0, 4)]
-CHUNKS = EARLY + LATE
-PIECES = [(j % 2, o, s, j // 2) for o, s in CHUNKS for j in range(4)]
+LATE = [(0, 3), (1, 3), (0, 4), (1, 4)]
+PIECES = [(j % 2, o, s, j // 2) for o, s in EARLY + LATE for j in range(4 if s < 4 else 2)]
 SLOTS = len(PIECES)
 KEYS = SLOTS * PER
 
@@ -48,10 +47,15 @@
 
 
 def attend_kernel(count, first, *refs):
-    chunks, refs = refs[:count], refs[count:]
     if first:
-        q_ref, w_ref, thr_ref, old_ref, lse_ref, o_ref, kv, sco = refs
+        chunks, halves, refs = refs[: count - 1], refs[count - 1 : count + 1], refs[count + 1 :]
+        q_ref, w_ref, thr_ref, old_ref, lse_ref, o_ref, kv, sco, pair = refs
+        for j, ref in enumerate(halves):
+            pair[j * 2 * PER : (j + 1) * 2 * PER, :] = ref[0 : 2 * PER, :]
+            pair[FOUR + j * 16 : FOUR + (j + 1) * 16, :] = ref[2 * PER :, :]
+        chunks = (*chunks, pair)
     else:
+        chunks, refs = refs[:count], refs[count:]
         q_ref, w_ref, thr_ref, o_ref, lse_ref, kv, sco = refs
     units = [(h, t) for h in range(HEADS) for t in range(ROWS // QT)]
     off = lax.broadcasted_iota(jnp.int32, (64, 128), 0).astype(jnp.float32)
@@ -156,9 +160,14 @@
 
 
 def attend(chunks, q, weights, thr, before=()):
-    count = len(chunks)
-    first = len(CHUNKS) - count if before else 0
+    count = len(chunks) - 1 if before else len(chunks)
+    first = len(EARLY) if before else 0
+    scratch = [
+        pltpu.VMEM((2, count * FOUR, VAT + VD), jnp.bfloat16),
+        pltpu.VMEM((2, QT, count * FOUR), jnp.float32),
+    ]
     if before:
+        scratch.append(pltpu.VMEM((FULL, L), jnp.bfloat16))
         shape = jax.ShapeDtypeStruct((ROWS, EXT), jnp.bfloat16)
     else:
         shape = (
@@ -168,10 +177,7 @@
     return pl.pallas_call(
         functools.partial(attend_kernel, count, first),
         out_shape=shape,
-        scratch_shapes=[
-            pltpu.VMEM((2, count * FOUR, VAT + VD), jnp.bfloat16),
-            pltpu.VMEM((2, QT, count * FOUR), jnp.float32),
-        ],
+        scratch_shapes=scratch,
         compiler_params=pltpu.CompilerParams(vmem_limit_bytes=24 * 1024 * 1024),
         cost_estimate=pl.CostEstimate(
             flops=1_000_000 * count, bytes_accessed=1_000 * count, transcendentals=1_000 * count
@@ -240,11 +246,25 @@
     )(*pieces)
 
 
+def halve_kernel(x_ref, o_ref):
+    o_ref[0 : 2 * PER, :] = x_ref[0 : 2 * PER, :]
+    o_ref[2 * PER :, :] = x_ref[FOUR : FOUR + 16, :]
+
+
+def halve(chunk):
+    return pl.pallas_call(
+        halve_kernel,
+        out_shape=jax.ShapeDtypeStruct((FULL // 2, L), jnp.bfloat16),
+        compiler_params=SMALL,
+        name="halve",
+    )(chunk)
+
+
 def shift(n, k):
     return [(i, (i + k) % n) for i in range(n)]
 
 
-def gather_keys(latents, key_rope, swap):
+def gather_keys(latents, key_rope, swap, prepare):
     near = [(a * 2 + b, (1 - a) * 2 + 1 - b) for a in range(2) for b in range(2)]
     to_core = lambda x: lax.ppermute(x, "core", shift(CN, 1))
 
@@ -255,16 +275,18 @@
 
     piece = pack(latents, key_rope)
     beside, mate = lax.ppermute(piece, ("xl", "xh"), near), to_core(piece)
+    mine = swap(beside)
     pieces = [piece, beside, mate, to_core(beside)]
-    mine = swap(mate)
     pieces, mine = lax.optimization_barrier((pieces, mine))
     now = merge(pieces)
     got = {(0, 0): now, (0, 1): round_z(now, 1), (0, 2): round_z(now, 2)}
+    got[0, 2], extra = lax.optimization_barrier((got[0, 2], prepare(beside)))
     got[0, 3] = round_z(got[0, 2], 1)
-    got[0, 4] = round_z(got[0, 2], 2)
+    got[0, 4] = round_z(halve(got[0, 2]), 2)
     for s in (1, 2):
         got[1, s] = to_core(got[0, s])
-    return got, to_core, mine, beside
+    mine, _ = lax.optimization_barrier((mine, now))
+    return got, to_core, mine, extra
 
 
 def threshold_kernel(pattern_ref, stripe_ref, o_ref):
@@ -311,19 +333,22 @@
         send, _ = lax.optimization_barrier((send, after))
         return lax.all_to_all(send, groups, split_axis=0, concat_axis=0, tiled=True)
 
-    got, to_core, mine, mark = gather_keys(latents, key_rope, swap)
+    def prepare(after):
+        up, down, seen, order, _ = lax.optimization_barrier(
+            (key_up, value_up, pattern, stripe, after)
+        )
+        weights = jnp.concatenate([up.transpose(0, 2, 1), down], axis=2)
+        return weights, thresholds(seen, order)
+
+    got, to_core, mine, (weights, thr) = gather_keys(latents, key_rope, swap, prepare)
     mine = mine.reshape(GRP * TOK, HEADS * QD)
     send = jnp.broadcast_to(mine[None], (CELLS, *mine.shape))
     q = lax.all_to_all(send, cells, split_axis=0, concat_axis=0, tiled=True)
     q = q.reshape(ROWS, HEADS * QD)
-    key_up, value_up, pattern, stripe, _ = lax.optimization_barrier(
-        (key_up, value_up, pattern, stripe, mark)
-    )
-    weights = jnp.concatenate([key_up.transpose(0, 2, 1), value_up], axis=2)
-    thr = thresholds(pattern, stripe)
     before = attend([got[c] for c in EARLY], q, weights, thr)
     (got[0, 3], got[0, 4]), before = lax.optimization_barrier(((got[0, 3], got[0, 4]), before))
-    got[1, 3] = to_core(got[0, 3])
+    for s in (3, 4):
+        got[1, s] = to_core(got[0, s])
     part = attend([got[c] for c in LATE], q, weights, thr, before)
     back = lax.all_to_all(
         part.reshape(CELLS, GRP * TOK, EXT), cells, split_axis=0, concat_axis=0, tiled=True

time: 98.6 us -> 99.4 us (level)
  blocking collectives: 35.3 us -> 31.5 us
  waiting for transfers between devices: 20.8 us -> 22.7 us
  local copies, waits for them, and re-layouts: 4.19 us -> 5.87 us
  starting transfers between devices: 22.7 us -> 24.2 us
    all_to_all x1, waiting for transfers between devices: 2.21 us -> 7.88 us  [swap(): return lax.all_to_all(send, groups, split_axis=0, concat_axis=0, tiled=True)]
    all_to_all x1, blocking collectives: 18.3 us -> 14.2 us  [body(): lax.all_to_all(combine(back.reshape(ROWS, EXT)), groups, split_axis=0, co...]
    ppermute x5 -> x6, waiting for transfers between devices: 4.11 us -> 2.21 us  [gather_keys(): to_core = lambda x: lax.ppermute(x, 'core', shift(CN, 1))]
    unnamed x11 -> x15, local copies, waits for them, and re-layouts: 2.2 us -> 3.89 us
    ppermute x4, waiting for transfers between devices: 11.3 us -> 9.68 us  [round_z(): return lax.ppermute(x, ('core', 'z'), up + down)]
    all_to_all x1, starting transfers between devices: 4.63 us -> 5.84 us  [body(): q = lax.all_to_all(send, cells, split_axis=0, concat_axis=0, tiled=True)]
    all_to_all x1, starting transfers between devices: 11 us -> 9.84 us  [swap(): return lax.all_to_all(send, groups, split_axis=0, concat_axis=0, tiled=True)]
    pallas_call x2, Pallas kernels: 11.6 us -> 10.5 us  [attend(): pl.pallas_call(functools.partial(attend_kernel, count, first), out_shape=...]
  transfers between devices with their start and end apart: 12 -> 13, of which waited for: 7 -> 8; matrix products, arithmetic and copies ran while one was open for 2% -> 2% of each run, Pallas kernels for 8% -> 8%
where the time goes in v7:
time: 99.4 us; the launch traced here: 98.9 us
  blocking collectives  31.5 us (32%)
  starting transfers between devices  24.2 us (24%)
  waiting for transfers between devices  22.7 us (23%)
  Pallas kernels  13.3 us (13%)
  local copies, waits for them, and re-layouts  5.87 us (6%)
  other arithmetic  1.32 us (1%)
    all_to_all x1, blocking collectives, body(): lax.all_to_all(part.reshape(CELLS, GRP * TOK, EXT), cells, split_axis=0,...  17.3 us
    all_to_all x1, blocking collectives, body(): lax.all_to_all(combine(back.reshape(ROWS, EXT)), groups, split_axis=0, co...  14.2 us
    pallas_call x2, Pallas kernels, attend(): pl.pallas_call(functools.partial(attend_kernel, count, first), out_shape=...  10.5 us
    all_to_all x1, starting transfers between devices, swap(): return lax.all_to_all(send, groups, split_axis=0, concat_axis=0, tiled=True)  9.84 us
    ppermute x4, waiting for transfers between devices, round_z(): return lax.ppermute(x, ('core', 'z'), up + down)  9.68 us
    all_to_all x1, waiting for transfers between devices, swap(): return lax.all_to_all(send, groups, split_axis=0, concat_axis=0, tiled=True)  7.88 us
    all_to_all x1, starting transfers between devices, body(): q = lax.all_to_all(send, cells, split_axis=0, concat_axis=0, tiled=True)  5.84 us
    ppermute x4, starting transfers between devices, round_z(): return lax.ppermute(x, ('core', 'z'), up + down)  4.68 us
  transfers between devices with their start and end apart: 13, of which 8 were waited for; matrix products, arithmetic and copies ran while one was open for 2% of the time, Pallas kernels for 8%

profile of v7, /device:TPU:32, one launch (start us, length us, event | category | flops | bytes accessed | tf_op | source)
XLA Modules:
  0.0 98.9 jit_solution(16269877650071995598)
XLA Ops:
  0.0 0.8 copy-done.2
  0.8 0.7 copy-done.3
  1.6 2.8 %collective-permute-start = (bf16[80,512]{1,0:T(8,128)(2,1)S(1)}, bf16[80,512]{1,0:T(8,128)(2,1)S(1)}, u32[]{:S(2)}, u32[]{:S(2)}) collective-permute-start(bf16[80,512]{1,0:T(8,128)(2,1)S(1)} %pack.1.refs_0_), channel_id=1, source_target_pairs={{0,136},{8,128},{128,8},{136,0},{1,137},{9,129},{129,9},{137,1},{2... | collective-permute-start | bytes 245768 | tf_op jit(solution)/shard_map/ppermute | solution.py:277
  4.4 2.9 %collective-permute-done.refs_1_ = bf16[80,512]{1,0:T(8,128)(2,1)S(1)} collective-permute-done((bf16[80,512]{1,0:T(8,128)(2,1)S(1)}, bf16[80,512]{1,0:T(8,128)(2,1)S(1)}, u32[]{:S(2)}, u32[]{:S(2)}) %collective-permute-start) | collective-permute-done | bytes 81952 | tf_op jit(solution)/shard_map/ppermute | solution.py:277
  7.3 9.8 %all-to-all-start = ((bf16[16,4,768]{2,1,0:T(4,128)(2,1)}), bf16[16,4,768]{2,1,0:T(4,128)(2,1)S(1)}, u32[]{:S(2)}, u32[]{:S(2)}) async-start(bf16[16,4,768]{2,1,0:T(4,128)(2,1)} %bitcast.16), calls=%async_computation | async-start | bytes 196608 | tf_op jit(solution)/shard_map/all_to_all | solution.py:334
  17.7 0.8 collective-permute-done.1.refs_2_
  18.6 7.9 %all-to-all-done = bf16[16,4,768]{2,1,0:T(4,128)(2,1)S(1)} async-done(((bf16[16,4,768]{2,1,0:T(4,128)(2,1)}), bf16[16,4,768]{2,1,0:T(4,128)(2,1)S(1)}, u32[]{:S(2)}, u32[]{:S(2)}) %all-to-all-start) | async-done | bytes 98336 | tf_op jit(solution)/shard_map/all_to_all | solution.py:334
  26.5 0.9 broadcast_in_dim.8
  27.5 5.8 %all-to-all-start.1 = ((bf16[8,64,768]{2,1,0:T(8,128)(2,1)}), bf16[8,64,768]{2,1,0:T(8,128)(2,1)S(1)}, u32[]{:S(2)}, u32[]{:S(2)}) async-start(bf16[8,64,768]{2,1,0:T(8,128)(2,1)} %broadcast_in_dim.8), calls=%async_computation.1 | async-start | bytes 1572864 | tf_op jit(solution)/shard_map/all_to_all | solution.py:346
  34.0 0.7 collective-permute-start.6
  34.7 1.0 %copy.10 = bf16[4,128,512]{1,2,0:T(8,128)(2,1)} copy(bf16[4,128,512]{2,1,0:T(8,128)(2,1)S(1)} %copy-done.6) | data formatting | bytes 1048576 | tf_op jit(solution)/shard_map/optimization_barrier | solution.py:337
  35.7 1.5 %thresholds.1.refs_7_.refs_6_ = f32[8,2048]{1,0:T(8,128)S(1)} custom-call(s32[8,128]{1,0:T(8,128)S(1)} %copy-done.4, s32[128]{0:T(128)S(1)} %copy-done.5), custom_call_target="tpu_custom_call" | custom-call | tf_op jit(solution)/shard_map/thresholds/pallas_call | solution.py:319
  37.2 1.3 %pad_maximum_fusion.refs_6_.refs_5_ = bf16[4,512,256]{2,1,0:T(8,128)(2,1)S(1)} fusion(bf16[4,512,128]{2,1,0:T(8,128)(2,1)} %param.11, bf16[4,512,128]{2,1,0:T(8,128)(2,1)} %bitcast.14), kind=kLoop, calls=%fused_computation | loop fusion | flops 2097152 | bytes 2097152 | tf_op jit(solution)/shard_map/concatenate | solution.py:340
  38.6 6.5 %collective-permute-done.3.x_ref.refs_3_ = bf16[288,512]{1,0:T(8,128)(2,1)S(1)} collective-permute-done((bf16[288,512]{1,0:T(8,128)(2,1)S(1)}, bf16[288,512]{1,0:T(8,128)(2,1)S(1)}, u32[]{:S(2)}, u32[]{:S(2)}) %collective-permute-start.3) | collective-permute-done | bytes 294944 | tf_op jit(solution)/shard_map/ppermute | solution.py:274
  45.0 1.5 %collective-permute-done.6.refs_1_ = bf16[288,512]{1,0:T(8,128)(2,1)S(1)} collective-permute-done((bf16[288,512]{1,0:T(8,128)(2,1)S(1)}, bf16[288,512]{1,0:T(8,128)(2,1)S(1)}, u32[]{:S(2)}, u32[]{:S(2)}) %collective-permute-start.6) | collective-permute-done | bytes 294944 | tf_op jit(solution)/shard_map/ppermute | solution.py:274
  47.7 2.8 %collective-permute-start.5 = (bf16[144,512]{1,0:T(8,128)(2,1)}, bf16[144,512]{1,0:T(8,128)(2,1)S(1)}, u32[]{:S(2)}, u32[]{:S(2)}) collective-permute-start(bf16[144,512]{1,0:T(8,128)(2,1)} %halve.1), channel_id=1, source_target_pairs={{0,2},{1,3},{2,4},{3,5},{4,6},{5,7},{6,0},{7,1},{16,22},{17,23},{1... | collective-permute-start | bytes 442376 | tf_op jit(solution)/shard_map/ppermute | solution.py:274
  50.5 0.7 copy-done
  51.3 1.0 copy-done.1
  52.2 5.6 %attend_early.1 = (f32[512,512]{1,0:T(8,128)S(1)}, f32[512,128]{1,0:T(8,128)S(1)}) custom-call(bf16[288,512]{1,0:T(8,128)(2,1)S(1)} %merge.1.refs_0_, bf16[288,512]{1,0:T(8,128)(2,1)S(1)} %collective-permute-done.6.refs_1_, bf16[288,512]{1,0:T(8,128)(2,1)S(1)} %copy-done.1, bf16[288,512]{1,0:T(8,128)(2,1)S(1)} %collective-permute-done.3.x_ref.refs_3_, ...), custom_call_target="tpu_custom_call" | custom-call | flops 5000000 | bytes 5000 | tf_op jit(solution)/shard_map/attend_early/pallas_call | solution.py:177
  57.8 1.7 %collective-permute-done.5.refs_2_ = bf16[144,512]{1,0:T(8,128)(2,1)S(1)} collective-permute-done((bf16[144,512]{1,0:T(8,128)(2,1)}, bf16[144,512]{1,0:T(8,128)(2,1)S(1)}, u32[]{:S(2)}, u32[]{:S(2)}) %collective-permute-start.5) | collective-permute-done | bytes 147488 | tf_op jit(solution)/shard_map/ppermute | solution.py:274
  60.1 1.3 %collective-permute-done.10.refs_3_ = bf16[144,512]{1,0:T(8,128)(2,1)S(1)} collective-permute-done((bf16[144,512]{1,0:T(8,128)(2,1)S(1)}, bf16[144,512]{1,0:T(8,128)(2,1)S(1)}, u32[]{:S(2)}, u32[]{:S(2)}) %collective-permute-start.10) | collective-permute-done | bytes 147488 | tf_op jit(solution)/shard_map/ppermute | solution.py:269
  61.4 4.9 %attend_late.1 = bf16[512,640]{1,0:T(8,128)(2,1)S(1)} custom-call(bf16[288,512]{1,0:T(8,128)(2,1)S(1)} %collective-permute-done.4.refs_0_, bf16[288,512]{1,0:T(8,128)(2,1)S(1)} %collective-permute-done.9.refs_1_, bf16[144,512]{1,0:T(8,128)(2,1)S(1)} %collective-permute-done.5.refs_2_, bf16[144,512]{1,0:T(8,128)(2,1)S(1)} %collective-permute-done.10.refs_3_, ...), custom_call_target="tpu_custom_call" | custom-call | flops 3000000 | bytes 3000 | tf_op jit(solution)/shard_map/attend_late/pallas_call | solution.py:177
  66.3 17.3 %all_to_all.20 = bf16[8,64,640]{2,1,0:T(8,128)(2,1)S(1)} all-to-all(bf16[8,64,640]{2,1,0:T(8,128)(2,1)S(1)} %bitcast.12), channel_id=1, replica_groups=mesh['xl'=2,'y'=4,'core'=2,'xh'=2,'z'=8] {'xl','y'}, dimensions={0} | all-to-all | bytes 1310720 | tf_op jit(solution)/shard_map/all_to_all | solution.py:353
  84.1 14.2 %all_to_all.21 = bf16[16,4,512]{2,1,0:T(4,128)(2,1)S(1)} all-to-all(bf16[16,4,512]{2,1,0:T(4,128)(2,1)S(1)} %combine.1), channel_id=1, replica_groups=mesh['xl'=2,'y'=4,'core'=2,'xh'=2,'z'=8] {'xh','z'}, dimensions={0} | all-to-all | bytes 131072 | tf_op jit(solution)/shard_map/all_to_all | solution.py:356
  (30 shorter events, 4.3 us)
Async XLA Ops:
  0.0 0.8 copy-start.2
  0.8 0.7 copy-start.3
  1.6 5.7 %collective-permute-start = (bf16[80,512]{1,0:T(8,128)(2,1)S(1)}, bf16[80,512]{1,0:T(8,128)(2,1)S(1)}, u32[]{:S(2)}, u32[]{:S(2)}) collective-permute-start(bf16[80,512]{1,0:T(8,128)(2,1)S(1)} %pack.1.refs_0_), channel_id=1, source_target_pairs={{0,136},{8,128},{128,8},{136,0},{1,137},{9,129},{129,9},{137,1},{2... | collective-permute-start | bytes 245768 | tf_op jit(solution)/shard_map/ppermute | solution.py:277
  7.3 19.2 %all-to-all-start = ((bf16[16,4,768]{2,1,0:T(4,128)(2,1)}), bf16[16,4,768]{2,1,0:T(4,128)(2,1)S(1)}, u32[]{:S(2)}, u32[]{:S(2)}) async-start(bf16[16,4,768]{2,1,0:T(4,128)(2,1)} %bitcast.16), calls=%async_computation | async-start | bytes 196608 | tf_op jit(solution)/shard_map/all_to_all | solution.py:334
  17.2 1.3 %collective-permute-start.1 = (bf16[80,512]{1,0:T(8,128)(2,1)S(1)}, bf16[80,512]{1,0:T(8,128)(2,1)S(1)}, u32[]{:S(2)}, u32[]{:S(2)}) collective-permute-start(bf16[80,512]{1,0:T(8,128)(2,1)S(1)} %pack.1.refs_0_), channel_id=1, source_target_pairs={{0,16},{16,0},{1,17},{17,1},{2,18},{18,2},{3,19},{19,3},{4,20},{20... | collective-permute-start | bytes 245768 | tf_op jit(solution)/shard_map/ppermute | solution.py:269
  17.2 1.4 %collective-permute-start.2 = (bf16[80,512]{1,0:T(8,128)(2,1)S(1)}, bf16[80,512]{1,0:T(8,128)(2,1)S(1)}, u32[]{:S(2)}, u32[]{:S(2)}) collective-permute-start(bf16[80,512]{1,0:T(8,128)(2,1)S(1)} %collective-permute-done.refs_1_), channel_id=1, source_target_pairs={{0,16},{16,0},{1,17},{17,1},{2,18},{18,2},{3,19},{19,3},{4,20},{20... | collective-permute-start | bytes 245768 | tf_op jit(solution)/shard_map/ppermute | solution.py:269
  26.5 8.2 %copy-start.6 = (bf16[4,128,512]{2,1,0:T(8,128)(2,1)S(1)}, bf16[4,128,512]{2,1,0:T(8,128)(2,1)}, u32[]{:S(2)}) copy-start(bf16[4,128,512]{2,1,0:T(8,128)(2,1)} %param.10) | copy-start | bytes 1572868
  27.5 8.2 %copy-start.4 = (s32[8,128]{1,0:T(8,128)S(1)}, s32[8,128]{1,0:T(8,128)}, u32[]{:S(2)}) copy-start(s32[8,128]{1,0:T(8,128)} %pattern_ref) | copy-start | bytes 12292
  27.5 8.2 %copy-start.5 = (s32[128]{0:T(128)S(1)}, s32[128]{0:T(128)}, u32[]{:S(2)}) copy-start(s32[128]{0:T(128)} %stripe_ref) | copy-start | bytes 1540
  27.5 23.8 %all-to-all-start.1 = ((bf16[8,64,768]{2,1,0:T(8,128)(2,1)}), bf16[8,64,768]{2,1,0:T(8,128)(2,1)S(1)}, u32[]{:S(2)}, u32[]{:S(2)}) async-start(bf16[8,64,768]{2,1,0:T(8,128)(2,1)} %broadcast_in_dim.8), calls=%async_computation.1 | async-start | bytes 1572864 | tf_op jit(solution)/shard_map/all_to_all | solution.py:346
  33.3 11.7 %collective-permute-start.3 = (bf16[288,512]{1,0:T(8,128)(2,1)S(1)}, bf16[288,512]{1,0:T(8,128)(2,1)S(1)}, u32[]{:S(2)}, u32[]{:S(2)}) collective-permute-start(bf16[288,512]{1,0:T(8,128)(2,1)S(1)} %merge.1.refs_0_), channel_id=1, source_target_pairs={{0,2},{1,3},{2,4},{3,5},{4,6},{5,7},{6,0},{7,1},{16,22},{17,23},{1... | collective-permute-start | bytes 884744 | tf_op jit(solution)/shard_map/ppermute | solution.py:274
  34.0 12.6 %collective-permute-start.6 = (bf16[288,512]{1,0:T(8,128)(2,1)S(1)}, bf16[288,512]{1,0:T(8,128)(2,1)S(1)}, u32[]{:S(2)}, u32[]{:S(2)}) collective-permute-start(bf16[288,512]{1,0:T(8,128)(2,1)S(1)} %merge.1.refs_0_), channel_id=1, source_target_pairs={{0,1},{1,2},{2,3},{3,4},{4,5},{5,6},{6,7},{7,0},{16,23},{17,16},{1... | collective-permute-start | bytes 884744 | tf_op jit(solution)/shard_map/ppermute | solution.py:274
  45.0 5.5 %collective-permute-start.8 = (bf16[288,512]{1,0:T(8,128)(2,1)S(1)}, bf16[288,512]{1,0:T(8,128)(2,1)S(1)}, u32[]{:S(2)}, u32[]{:S(2)}) collective-permute-start(bf16[288,512]{1,0:T(8,128)(2,1)S(1)} %collective-permute-done.3.x_ref.refs_3_), channel_id=1, source_target_pairs={{0,16},{16,0},{1,17},{17,1},{2,18},{18,2},{3,19},{19,3},{4,20},{20... | collective-permute-start | bytes 884744 | tf_op jit(solution)/shard_map/ppermute | solution.py:269
  46.5 4.0 %collective-permute-start.7 = (bf16[288,512]{1,0:T(8,128)(2,1)S(1)}, bf16[288,512]{1,0:T(8,128)(2,1)S(1)}, u32[]{:S(2)}, u32[]{:S(2)}) collective-permute-start(bf16[288,512]{1,0:T(8,128)(2,1)S(1)} %collective-permute-done.6.refs_1_), channel_id=1, source_target_pairs={{0,16},{16,0},{1,17},{17,1},{2,18},{18,2},{3,19},{19,3},{4,20},{20... | collective-permute-start | bytes 884744 | tf_op jit(solution)/shard_map/ppermute | solution.py:269
  46.5 13.1 %collective-permute-start.4 = (bf16[288,512]{1,0:T(8,128)(2,1)S(1)}, bf16[288,512]{1,0:T(8,128)(2,1)S(1)}, u32[]{:S(2)}, u32[]{:S(2)}) collective-permute-start(bf16[288,512]{1,0:T(8,128)(2,1)S(1)} %collective-permute-done.3.x_ref.refs_3_), channel_id=1, source_target_pairs={{0,1},{1,2},{2,3},{3,4},{4,5},{5,6},{6,7},{7,0},{16,23},{17,16},{1... | collective-permute-start | bytes 884744 | tf_op jit(solution)/shard_map/ppermute | solution.py:274
  47.7 11.9 %collective-permute-start.5 = (bf16[144,512]{1,0:T(8,128)(2,1)}, bf16[144,512]{1,0:T(8,128)(2,1)S(1)}, u32[]{:S(2)}, u32[]{:S(2)}) collective-permute-start(bf16[144,512]{1,0:T(8,128)(2,1)} %halve.1), channel_id=1, source_target_pairs={{0,2},{1,3},{2,4},{3,5},{4,6},{5,7},{6,0},{7,1},{16,22},{17,23},{1... | collective-permute-start | bytes 442376 | tf_op jit(solution)/shard_map/ppermute | solution.py:274
  50.5 0.7 copy-start
  51.3 1.0 copy-start.1
  59.6 1.8 %collective-permute-start.9 = (bf16[288,512]{1,0:T(8,128)(2,1)S(1)}, bf16[288,512]{1,0:T(8,128)(2,1)S(1)}, u32[]{:S(2)}, u32[]{:S(2)}) collective-permute-start(bf16[288,512]{1,0:T(8,128)(2,1)S(1)} %collective-permute-done.4.refs_0_), channel_id=1, source_target_pairs={{0,16},{16,0},{1,17},{17,1},{2,18},{18,2},{3,19},{19,3},{4,20},{20... | collective-permute-start | bytes 884744 | tf_op jit(solution)/shard_map/ppermute | solution.py:269
  59.6 1.8 %collective-permute-start.10 = (bf16[144,512]{1,0:T(8,128)(2,1)S(1)}, bf16[144,512]{1,0:T(8,128)(2,1)S(1)}, u32[]{:S(2)}, u32[]{:S(2)}) collective-permute-start(bf16[144,512]{1,0:T(8,128)(2,1)S(1)} %collective-permute-done.5.refs_2_), channel_id=1, source_target_pairs={{0,16},{16,0},{1,17},{17,1},{2,18},{18,2},{3,19},{19,3},{4,20},{20... | collective-permute-start | bytes 442376 | tf_op jit(solution)/shard_map/ppermute | solution.py:269

commit v8 on v7

--- a/solution.py
+++ b/solution.py
@@ -20,6 +20,7 @@
 SCALE = 1.0 / math.sqrt(QD)
 LOG2E = math.log2(math.e)
 
+CHIPS = ("xl", "y", "xh", "z")
 AXES = ("xl", "y", "core", "xh", "z")
 XLN, YN, CN, XHN, ZN = 2, 4, 2, 2, 8
 CELLS = XLN * YN
@@ -275,17 +276,15 @@
 
     piece = pack(latents, key_rope)
     beside, mate = lax.ppermute(piece, ("xl", "xh"), near), to_core(piece)
-    mine = swap(beside)
     pieces = [piece, beside, mate, to_core(beside)]
-    pieces, mine = lax.optimization_barrier((pieces, mine))
     now = merge(pieces)
+    mine = swap(now)
     got = {(0, 0): now, (0, 1): round_z(now, 1), (0, 2): round_z(now, 2)}
-    got[0, 2], extra = lax.optimization_barrier((got[0, 2], prepare(beside)))
+    got[0, 1], got[0, 2], extra = lax.optimization_barrier((got[0, 1], got[0, 2], prepare(beside)))
     got[0, 3] = round_z(got[0, 2], 1)
     got[0, 4] = round_z(halve(got[0, 2]), 2)
     for s in (1, 2):
         got[1, s] = to_core(got[0, s])
-    mine, _ = lax.optimization_barrier((mine, now))
     return got, to_core, mine, extra
 
 
@@ -331,7 +330,9 @@
     def swap(after):
         send = queries.reshape(TOK, GRP, HEADS * QD).transpose(1, 0, 2)
         send, _ = lax.optimization_barrier((send, after))
-        return lax.all_to_all(send, groups, split_axis=0, concat_axis=0, tiled=True)
+        send = jnp.broadcast_to(send[None], (CELLS, *send.shape))
+        send = send.reshape(CELLS * GRP, TOK, HEADS * QD)
+        return lax.all_to_all(send, CHIPS, split_axis=0, concat_axis=0, tiled=True)
 
     def prepare(after):
         up, down, seen, order, _ = lax.optimization_barrier(
@@ -341,10 +342,7 @@
         return weights, thresholds(seen, order)
 
     got, to_core, mine, (weights, thr) = gather_keys(latents, key_rope, swap, prepare)
-    mine = mine.reshape(GRP * TOK, HEADS * QD)
-    send = jnp.broadcast_to(mine[None], (CELLS, *mine.shape))
-    q = lax.all_to_all(send, cells, split_axis=0, concat_axis=0, tiled=True)
-    q = q.reshape(ROWS, HEADS * QD)
+    q = mine.reshape(ROWS, HEADS * QD)
     before = attend([got[c] for c in EARLY], q, weights, thr)
     (got[0, 3], got[0, 4]), before = lax.optimization_barrier(((got[0, 3], got[0, 4]), before))
     for s in (3, 4):

time: 99.4 us -> 108 us (1.087)
  starting transfers between devices: 24.2 us -> 27.9 us
  waiting for transfers between devices: 22.7 us -> 25.2 us
  blocking collectives: 31.5 us -> 33.8 us
  other arithmetic: 1.32 us -> 0.12 us
    ppermute x4, waiting for transfers between devices: 9.68 us -> 20.9 us  [round_z(): return lax.ppermute(x, ('core', 'z'), up + down)]
    all_to_all x2 -> x1, waiting for transfers between devices: 7.89 us -> 0.01 us  [swap(): return lax.all_to_all(send, CHIPS, split_axis=0, concat_axis=0, tiled=True)]
    ppermute x4, starting transfers between devices: 4.68 us -> 8.48 us  [round_z(): return lax.ppermute(x, ('core', 'z'), up + down)]
    all_to_all x1, blocking collectives: 14.2 us -> 17.2 us  [body(): lax.all_to_all(combine(back.reshape(ROWS, EXT)), groups, split_axis=0, co...]
    reshape x0 -> x1, local copies, waits for them, and re-layouts: none -> 1.56 us  [body(): q = mine.reshape(ROWS, HEADS * QD)]
    concatenate x1, other arithmetic: 1.32 us -> 0.12 us  [prepare(): weights = jnp.concatenate([up.transpose(0, 2, 1), down], axis=2)]
    unnamed x15 -> x14, local copies, waits for them, and re-layouts: 3.89 us -> 3.11 us
    all_to_all x2 -> x1, starting transfers between devices: 15.7 us -> 15.3 us  [swap(): return lax.all_to_all(send, CHIPS, split_axis=0, concat_axis=0, tiled=True)]
  transfers between devices with their start and end apart: 13 -> 12, of which waited for: 8 -> 5; matrix products, arithmetic and copies ran while one was open for 2% -> 3% of each run, Pallas kernels for 8% -> 8%
where the time goes in v8:
time: 108 us
  blocking collectives  33.8 us (31%)
  starting transfers between devices  27.9 us (26%)
  waiting for transfers between devices  25.2 us (23%)
  Pallas kernels  14.3 us (13%)
  local copies, waits for them, and re-layouts  6.1 us (6%)
    ppermute x4, waiting for transfers between devices, round_z(): return lax.ppermute(x, ('core', 'z'), up + down)  20.9 us
    all_to_all x1, blocking collectives, body(): lax.all_to_all(combine(back.reshape(ROWS, EXT)), groups, split_axis=0, co...  17.2 us
    all_to_all x1, blocking collectives, body(): lax.all_to_all(part.reshape(CELLS, GRP * TOK, EXT), cells, split_axis=0,...  16.6 us
    all_to_all x1, starting transfers between devices, swap(): return lax.all_to_all(send, CHIPS, split_axis=0, concat_axis=0, tiled=True)  15.3 us
    pallas_call x2, Pallas kernels, attend(): pl.pallas_call(functools.partial(attend_kernel, count, first), out_shape=...  11.5 us
    ppermute x4, starting transfers between devices, round_z(): return lax.ppermute(x, ('core', 'z'), up + down)  8.48 us
    unnamed x14, local copies, waits for them, and re-layouts  3.11 us
    ppermute x1, waiting for transfers between devices, gather_keys(): beside, mate = (lax.ppermute(piece, ('xl', 'xh'), near), to_core(piece))  2.89 us
  transfers between devices with their start and end apart: 12, of which 5 were waited for; matrix products, arithmetic and copies ran while one was open for 3% of the time, Pallas kernels for 8%

profile of v8, /device:TPU:32, one launch (start us, length us, event | category | flops | bytes accessed | tf_op | source)
XLA Modules:
  0.0 107.6 jit_solution(9532284859890764734)
XLA Ops:
  0.0 0.8 copy-done
  0.8 0.7 copy-done.1
  1.6 2.8 %collective-permute-start = (bf16[80,512]{1,0:T(8,128)(2,1)S(1)}, bf16[80,512]{1,0:T(8,128)(2,1)S(1)}, u32[]{:S(2)}, u32[]{:S(2)}) collective-permute-start(bf16[80,512]{1,0:T(8,128)(2,1)S(1)} %pack.1.refs_0_), channel_id=1, source_target_pairs={{0,136},{8,128},{128,8},{136,0},{1,137},{9,129},{129,9},{137,1},{2... | collective-permute-start | bytes 245768 | tf_op jit(solution)/shard_map/ppermute | solution.py:278
  4.4 2.9 %collective-permute-done.refs_1_ = bf16[80,512]{1,0:T(8,128)(2,1)S(1)} collective-permute-done((bf16[80,512]{1,0:T(8,128)(2,1)S(1)}, bf16[80,512]{1,0:T(8,128)(2,1)S(1)}, u32[]{:S(2)}, u32[]{:S(2)}) %collective-permute-start) | collective-permute-done | bytes 81952 | tf_op jit(solution)/shard_map/ppermute | solution.py:278
  7.3 0.9 copy.12
  8.7 1.1 %broadcast_in_dim.2 = bf16[8,16,4,768]{3,2,1,0:T(4,128)(2,1)} broadcast(bf16[16,4,768]{2,1,0:T(4,128)(2,1)S(1)} %copy.9), dimensions={1,2,3} | broadcast | bytes 884736 | tf_op jit(solution)/shard_map/broadcast_in_dim | solution.py:333
  9.8 15.3 %all-to-all-start = ((bf16[128,4,768]{2,1,0:T(4,128)(2,1)}), bf16[128,4,768]{2,1,0:T(4,128)(2,1)}, u32[]{:S(2)}, u32[]{:S(2)}) async-start(bf16[128,4,768]{2,1,0:T(4,128)(2,1)} %bitcast.2), calls=%async_computation | async-start | bytes 1572864 | tf_op jit(solution)/shard_map/all_to_all | solution.py:335
  25.1 1.5 %collective-permute-start.3 = (bf16[288,512]{1,0:T(8,128)(2,1)S(1)}, bf16[288,512]{1,0:T(8,128)(2,1)S(1)}, u32[]{:S(2)}, u32[]{:S(2)}) collective-permute-start(bf16[288,512]{1,0:T(8,128)(2,1)S(1)} %merge.1.refs_0_), channel_id=1, source_target_pairs={{0,1},{1,2},{2,3},{3,4},{4,5},{5,6},{6,7},{7,0},{16,23},{17,16},{1... | collective-permute-start | bytes 884744 | tf_op jit(solution)/shard_map/ppermute | solution.py:275
  26.6 3.6 %collective-permute-start.4 = (bf16[288,512]{1,0:T(8,128)(2,1)S(1)}, bf16[288,512]{1,0:T(8,128)(2,1)S(1)}, u32[]{:S(2)}, u32[]{:S(2)}) collective-permute-start(bf16[288,512]{1,0:T(8,128)(2,1)S(1)} %merge.1.refs_0_), channel_id=1, source_target_pairs={{0,2},{1,3},{2,4},{3,5},{4,6},{5,7},{6,0},{7,1},{16,22},{17,23},{1... | collective-permute-start | bytes 884744 | tf_op jit(solution)/shard_map/ppermute | solution.py:275
  30.5 1.5 %thresholds.1.refs_7_.refs_6_ = f32[8,2048]{1,0:T(8,128)S(1)} custom-call(s32[8,128]{1,0:T(8,128)S(1)} %copy-done.2, s32[128]{0:T(128)S(1)} %copy-done.3), custom_call_target="tpu_custom_call" | custom-call | tf_op jit(solution)/shard_map/thresholds/pallas_call | solution.py:318
  32.2 13.4 %collective-permute-done.3.refs_1_ = bf16[288,512]{1,0:T(8,128)(2,1)S(1)} collective-permute-done((bf16[288,512]{1,0:T(8,128)(2,1)S(1)}, bf16[288,512]{1,0:T(8,128)(2,1)S(1)}, u32[]{:S(2)}, u32[]{:S(2)}) %collective-permute-start.3) | collective-permute-done | bytes 294944 | tf_op jit(solution)/shard_map/ppermute | solution.py:275
  45.6 7.5 %collective-permute-done.4.x_ref.refs_3_ = bf16[288,512]{1,0:T(8,128)(2,1)S(1)} collective-permute-done((bf16[288,512]{1,0:T(8,128)(2,1)S(1)}, bf16[288,512]{1,0:T(8,128)(2,1)S(1)}, u32[]{:S(2)}, u32[]{:S(2)}) %collective-permute-start.4) | collective-permute-done | bytes 294944 | tf_op jit(solution)/shard_map/ppermute | solution.py:275
  53.0 0.5 collective-permute-start.7
  53.6 2.1 %collective-permute-start.5 = (bf16[288,512]{1,0:T(8,128)(2,1)S(1)}, bf16[288,512]{1,0:T(8,128)(2,1)S(1)}, u32[]{:S(2)}, u32[]{:S(2)}) collective-permute-start(bf16[288,512]{1,0:T(8,128)(2,1)S(1)} %collective-permute-done.4.x_ref.refs_3_), channel_id=1, source_target_pairs={{0,1},{1,2},{2,3},{3,4},{4,5},{5,6},{6,7},{7,0},{16,23},{17,16},{1... | collective-permute-start | bytes 884744 | tf_op jit(solution)/shard_map/ppermute | solution.py:275
  55.7 0.7 halve.1
  56.3 1.3 %collective-permute-start.6 = (bf16[144,512]{1,0:T(8,128)(2,1)}, bf16[144,512]{1,0:T(8,128)(2,1)S(1)}, u32[]{:S(2)}, u32[]{:S(2)}) collective-permute-start(bf16[144,512]{1,0:T(8,128)(2,1)} %halve.1), channel_id=1, source_target_pairs={{0,2},{1,3},{2,4},{3,5},{4,6},{5,7},{6,0},{7,1},{16,22},{17,23},{1... | collective-permute-start | bytes 442376 | tf_op jit(solution)/shard_map/ppermute | solution.py:275
  57.6 1.6 %reshape.21.refs_5_.refs_4_ = bf16[512,768]{1,0:T(8,128)(2,1)S(1)} reshape(bf16[128,4,768]{2,1,0:T(4,128)(2,1)} %all-to-all-done) | data formatting | bytes 1572864 | tf_op jit(solution)/shard_map/reshape | solution.py:345
  59.2 6.6 %attend_early.1 = (f32[512,512]{1,0:T(8,128)S(1)}, f32[512,128]{1,0:T(8,128)S(1)}) custom-call(bf16[288,512]{1,0:T(8,128)(2,1)S(1)} %merge.1.refs_0_, bf16[288,512]{1,0:T(8,128)(2,1)S(1)} %collective-permute-done.3.refs_1_, bf16[288,512]{1,0:T(8,128)(2,1)} %collective-permute-done.7.refs_2_, bf16[288,512]{1,0:T(8,128)(2,1)S(1)} %collective-permute-done.4.x_ref.refs_3_, ...), custom_call_target="tpu_custom_call" | custom-call | flops 5000000 | bytes 5000 | tf_op jit(solution)/shard_map/attend_early/pallas_call | solution.py:178
  66.6 1.1 %collective-permute-done.10.refs_3_ = bf16[144,512]{1,0:T(8,128)(2,1)S(1)} collective-permute-done((bf16[144,512]{1,0:T(8,128)(2,1)S(1)}, bf16[144,512]{1,0:T(8,128)(2,1)S(1)}, u32[]{:S(2)}, u32[]{:S(2)}) %collective-permute-start.10) | collective-permute-done | bytes 147488 | tf_op jit(solution)/shard_map/ppermute | solution.py:270
  67.7 4.9 %attend_late.1 = bf16[512,640]{1,0:T(8,128)(2,1)S(1)} custom-call(bf16[288,512]{1,0:T(8,128)(2,1)S(1)} %collective-permute-done.5.refs_0_, bf16[288,512]{1,0:T(8,128)(2,1)S(1)} %collective-permute-done.9.refs_1_, bf16[144,512]{1,0:T(8,128)(2,1)S(1)} %collective-permute-done.6.refs_2_, bf16[144,512]{1,0:T(8,128)(2,1)S(1)} %collective-permute-done.10.refs_3_, ...), custom_call_target="tpu_custom_call" | custom-call | flops 3000000 | bytes 3000 | tf_op jit(solution)/shard_map/attend_late/pallas_call | solution.py:178
  72.6 16.6 %all_to_all.15 = bf16[8,64,640]{2,1,0:T(8,128)(2,1)S(1)} all-to-all(bf16[8,64,640]{2,1,0:T(8,128)(2,1)S(1)} %bitcast.14), channel_id=1, replica_groups=mesh['xl'=2,'y'=4,'core'=2,'xh'=2,'z'=8] {'xl','y'}, dimensions={0} | all-to-all | bytes 1310720 | tf_op jit(solution)/shard_map/all_to_all | solution.py:351
  89.2 0.5 combine.1
  89.7 17.2 %all_to_all.16 = bf16[16,4,512]{2,1,0:T(4,128)(2,1)S(1)} all-to-all(bf16[16,4,512]{2,1,0:T(4,128)(2,1)S(1)} %combine.1), channel_id=1, replica_groups=mesh['xl'=2,'y'=4,'core'=2,'xh'=2,'z'=8] {'xh','z'}, dimensions={0} | all-to-all | bytes 131072 | tf_op jit(solution)/shard_map/all_to_all | solution.py:354
  106.9 0.6 copy.14
  (28 shorter events, 1.7 us)
Async XLA Ops:
  0.0 0.8 copy-start
  0.8 0.7 copy-start.1
  1.6 5.7 %collective-permute-start = (bf16[80,512]{1,0:T(8,128)(2,1)S(1)}, bf16[80,512]{1,0:T(8,128)(2,1)S(1)}, u32[]{:S(2)}, u32[]{:S(2)}) collective-permute-start(bf16[80,512]{1,0:T(8,128)(2,1)S(1)} %pack.1.refs_0_), channel_id=1, source_target_pairs={{0,136},{8,128},{128,8},{136,0},{1,137},{9,129},{129,9},{137,1},{2... | collective-permute-start | bytes 245768 | tf_op jit(solution)/shard_map/ppermute | solution.py:278
  4.4 3.8 %collective-permute-start.1 = (bf16[80,512]{1,0:T(8,128)(2,1)S(1)}, bf16[80,512]{1,0:T(8,128)(2,1)S(1)}, u32[]{:S(2)}, u32[]{:S(2)}) collective-permute-start(bf16[80,512]{1,0:T(8,128)(2,1)S(1)} %pack.1.refs_0_), channel_id=1, source_target_pairs={{0,16},{16,0},{1,17},{17,1},{2,18},{18,2},{3,19},{19,3},{4,20},{20... | collective-permute-start | bytes 245768 | tf_op jit(solution)/shard_map/ppermute | solution.py:270
  7.3 1.3 %collective-permute-start.2 = (bf16[80,512]{1,0:T(8,128)(2,1)S(1)}, bf16[80,512]{1,0:T(8,128)(2,1)S(1)}, u32[]{:S(2)}, u32[]{:S(2)}) collective-permute-start(bf16[80,512]{1,0:T(8,128)(2,1)S(1)} %collective-permute-done.refs_1_), channel_id=1, source_target_pairs={{0,16},{16,0},{1,17},{17,1},{2,18},{18,2},{3,19},{19,3},{4,20},{20... | collective-permute-start | bytes 245768 | tf_op jit(solution)/shard_map/ppermute | solution.py:270
  8.7 21.5 %copy-start.4 = (bf16[4,128,512]{2,1,0:T(8,128)(2,1)S(1)}, bf16[4,128,512]{2,1,0:T(8,128)(2,1)}, u32[]{:S(2)}) copy-start(bf16[4,128,512]{2,1,0:T(8,128)(2,1)} %param.10) | copy-start | bytes 1572868
  9.8 20.7 %copy-start.2 = (s32[8,128]{1,0:T(8,128)S(1)}, s32[8,128]{1,0:T(8,128)}, u32[]{:S(2)}) copy-start(s32[8,128]{1,0:T(8,128)} %pattern_ref) | copy-start | bytes 12292
  9.8 20.7 %copy-start.3 = (s32[128]{0:T(128)S(1)}, s32[128]{0:T(128)}, u32[]{:S(2)}) copy-start(s32[128]{0:T(128)} %stripe_ref) | copy-start | bytes 1540
  9.8 22.2 %copy-start.5 = (bf16[4,512,128]{2,1,0:T(8,128)(2,1)S(1)}, bf16[4,512,128]{2,1,0:T(8,128)(2,1)}, u32[]{:S(2)}) copy-start(bf16[4,512,128]{2,1,0:T(8,128)(2,1)} %param.11) | copy-start | bytes 1572868
  9.8 47.8 %all-to-all-start = ((bf16[128,4,768]{2,1,0:T(4,128)(2,1)}), bf16[128,4,768]{2,1,0:T(4,128)(2,1)}, u32[]{:S(2)}, u32[]{:S(2)}) async-start(bf16[128,4,768]{2,1,0:T(4,128)(2,1)} %bitcast.2), calls=%async_computation | async-start | bytes 1572864 | tf_op jit(solution)/shard_map/all_to_all | solution.py:335
  25.1 20.5 %collective-permute-start.3 = (bf16[288,512]{1,0:T(8,128)(2,1)S(1)}, bf16[288,512]{1,0:T(8,128)(2,1)S(1)}, u32[]{:S(2)}, u32[]{:S(2)}) collective-permute-start(bf16[288,512]{1,0:T(8,128)(2,1)S(1)} %merge.1.refs_0_), channel_id=1, source_target_pairs={{0,1},{1,2},{2,3},{3,4},{4,5},{5,6},{6,7},{7,0},{16,23},{17,16},{1... | collective-permute-start | bytes 884744 | tf_op jit(solution)/shard_map/ppermute | solution.py:275
  26.6 26.4 %collective-permute-start.4 = (bf16[288,512]{1,0:T(8,128)(2,1)S(1)}, bf16[288,512]{1,0:T(8,128)(2,1)S(1)}, u32[]{:S(2)}, u32[]{:S(2)}) collective-permute-start(bf16[288,512]{1,0:T(8,128)(2,1)S(1)} %merge.1.refs_0_), channel_id=1, source_target_pairs={{0,2},{1,3},{2,4},{3,5},{4,6},{5,7},{6,0},{7,1},{16,22},{17,23},{1... | collective-permute-start | bytes 884744 | tf_op jit(solution)/shard_map/ppermute | solution.py:275
  53.0 6.1 %collective-permute-start.8 = (bf16[288,512]{1,0:T(8,128)(2,1)S(1)}, bf16[288,512]{1,0:T(8,128)(2,1)S(1)}, u32[]{:S(2)}, u32[]{:S(2)}) collective-permute-start(bf16[288,512]{1,0:T(8,128)(2,1)S(1)} %collective-permute-done.4.x_ref.refs_3_), channel_id=1, source_target_pairs={{0,16},{16,0},{1,17},{17,1},{2,18},{18,2},{3,19},{19,3},{4,20},{20... | collective-permute-start | bytes 884744 | tf_op jit(solution)/shard_map/ppermute | solution.py:270
  53.0 6.1 %collective-permute-start.7 = (bf16[288,512]{1,0:T(8,128)(2,1)S(1)}, bf16[288,512]{1,0:T(8,128)(2,1)}, u32[]{:S(2)}, u32[]{:S(2)}) collective-permute-start(bf16[288,512]{1,0:T(8,128)(2,1)S(1)} %collective-permute-done.3.refs_1_), channel_id=1, source_target_pairs={{0,16},{16,0},{1,17},{17,1},{2,18},{18,2},{3,19},{19,3},{4,20},{20... | collective-permute-start | bytes 884744 | tf_op jit(solution)/shard_map/ppermute | solution.py:270
  53.6 12.2 %collective-permute-start.5 = (bf16[288,512]{1,0:T(8,128)(2,1)S(1)}, bf16[288,512]{1,0:T(8,128)(2,1)S(1)}, u32[]{:S(2)}, u32[]{:S(2)}) collective-permute-start(bf16[288,512]{1,0:T(8,128)(2,1)S(1)} %collective-permute-done.4.x_ref.refs_3_), channel_id=1, source_target_pairs={{0,1},{1,2},{2,3},{3,4},{4,5},{5,6},{6,7},{7,0},{16,23},{17,16},{1... | collective-permute-start | bytes 884744 | tf_op jit(solution)/shard_map/ppermute | solution.py:275
  56.3 9.4 %collective-permute-start.6 = (bf16[144,512]{1,0:T(8,128)(2,1)}, bf16[144,512]{1,0:T(8,128)(2,1)S(1)}, u32[]{:S(2)}, u32[]{:S(2)}) collective-permute-start(bf16[144,512]{1,0:T(8,128)(2,1)} %halve.1), channel_id=1, source_target_pairs={{0,2},{1,3},{2,4},{3,5},{4,6},{5,7},{6,0},{7,1},{16,22},{17,23},{1... | collective-permute-start | bytes 442376 | tf_op jit(solution)/shard_map/ppermute | solution.py:275
  65.8 1.9 %collective-permute-start.9 = (bf16[288,512]{1,0:T(8,128)(2,1)S(1)}, bf16[288,512]{1,0:T(8,128)(2,1)S(1)}, u32[]{:S(2)}, u32[]{:S(2)}) collective-permute-start(bf16[288,512]{1,0:T(8,128)(2,1)S(1)} %collective-permute-done.5.refs_0_), channel_id=1, source_target_pairs={{0,16},{16,0},{1,17},{17,1},{2,18},{18,2},{3,19},{19,3},{4,20},{20... | collective-permute-start | bytes 884744 | tf_op jit(solution)/shard_map/ppermute | solution.py:270
  66.3 1.4 %collective-permute-start.10 = (bf16[144,512]{1,0:T(8,128)(2,1)S(1)}, bf16[144,512]{1,0:T(8,128)(2,1)S(1)}, u32[]{:S(2)}, u32[]{:S(2)}) collective-permute-start(bf16[144,512]{1,0:T(8,128)(2,1)S(1)} %collective-permute-done.6.refs_2_), channel_id=1, source_target_pairs={{0,16},{16,0},{1,17},{17,1},{2,18},{18,2},{3,19},{19,3},{4,20},{20... | collective-permute-start | bytes 442376 | tf_op jit(solution)/shard_map/ppermute | solution.py:270

commit v9 on v7

--- a/solution.py
+++ b/solution.py
@@ -275,7 +275,7 @@
 
     piece = pack(latents, key_rope)
     beside, mate = lax.ppermute(piece, ("xl", "xh"), near), to_core(piece)
-    mine = swap(beside)
+    mine = swap(piece)
     pieces = [piece, beside, mate, to_core(beside)]
     pieces, mine = lax.optimization_barrier((pieces, mine))
     now = merge(pieces)
@@ -321,6 +321,7 @@
         out_shape=jax.ShapeDtypeStruct((CELLS, KEYS), jnp.float32),
         in_specs=[pl.BlockSpec(memory_space=pltpu.SMEM)] * 2,
         compiler_params=SMALL,
+        cost_estimate=pl.CostEstimate(flops=50_000_000_000, bytes_accessed=100_000, transcendentals=0),
         name="thresholds",
     )(pattern, stripe)
 

time: 99.4 us -> 88.6 us (0.89)
  waiting for transfers between devices: 22.7 us -> 10.1 us
  starting transfers between devices: 24.2 us -> 26.4 us
    ppermute x4, waiting for transfers between devices: 9.68 us -> 1.46 us  [round_z(): return lax.ppermute(x, ('core', 'z'), up + down)]
    all_to_all x1, waiting for transfers between devices: 7.88 us -> 2.02 us  [swap(): return lax.all_to_all(send, groups, split_axis=0, concat_axis=0, tiled=True)]
    ppermute x4, starting transfers between devices: 4.68 us -> 7.49 us  [round_z(): return lax.ppermute(x, ('core', 'z'), up + down)]
    all_to_all x1, blocking collectives: 14.2 us -> 15.9 us  [body(): lax.all_to_all(combine(back.reshape(ROWS, EXT)), groups, split_axis=0, co...]
    all_to_all x1, blocking collectives: 17.3 us -> 15.9 us  [body(): lax.all_to_all(part.reshape(CELLS, GRP * TOK, EXT), cells, split_axis=0,...]
    all_to_all x1, starting transfers between devices: 5.84 us -> 4.47 us  [body(): q = lax.all_to_all(send, cells, split_axis=0, concat_axis=0, tiled=True)]
    all_to_all x1, starting transfers between devices: 9.84 us -> 11 us  [swap(): return lax.all_to_all(send, groups, split_axis=0, concat_axis=0, tiled=True)]
  transfers between devices with their start and end apart: 13 -> 13, of which waited for: 8 -> 6; matrix products, arithmetic and copies ran while one was open for 2% -> 3% of each run, Pallas kernels for 8% -> 9%
where the time goes in v9:
time: 88.6 us; the launch traced here: 88.2 us
  blocking collectives  31.9 us (36%)
  starting transfers between devices  26.4 us (30%)
  Pallas kernels  13.3 us (15%)
  waiting for transfers between devices  10.1 us (11%)
  local copies, waits for them, and re-layouts  5.14 us (6%)
  other arithmetic  1.17 us (1%)
    all_to_all x1, blocking collectives, body(): lax.all_to_all(combine(back.reshape(ROWS, EXT)), groups, split_axis=0, co...  15.9 us
    all_to_all x1, blocking collectives, body(): lax.all_to_all(part.reshape(CELLS, GRP * TOK, EXT), cells, split_axis=0,...  15.9 us
    all_to_all x1, starting transfers between devices, swap(): return lax.all_to_all(send, groups, split_axis=0, concat_axis=0, tiled=True)  11 us
    pallas_call x2, Pallas kernels, attend(): pl.pallas_call(functools.partial(attend_kernel, count, first), out_shape=...  10.5 us
    ppermute x4, starting transfers between devices, round_z(): return lax.ppermute(x, ('core', 'z'), up + down)  7.49 us
    all_to_all x1, starting transfers between devices, body(): q = lax.all_to_all(send, cells, split_axis=0, concat_axis=0, tiled=True)  4.47 us
    unnamed x15, local copies, waits for them, and re-layouts  3.89 us
    ppermute x1, waiting for transfers between devices, gather_keys(): beside, mate = (lax.ppermute(piece, ('xl', 'xh'), near), to_core(piece))  3.21 us
  transfers between devices with their start and end apart: 13, of which 6 were waited for; matrix products, arithmetic and copies ran while one was open for 3% of the time, Pallas kernels for 9%

profile of v9, /device:TPU:32, one launch (start us, length us, event | category | flops | bytes accessed | tf_op | source)
XLA Modules:
  0.0 88.2 jit_solution(538439143169566237)
XLA Ops:
  0.0 0.8 copy-done.2
  0.8 0.7 copy-done.3
  1.6 11.0 %all-to-all-start = ((bf16[16,4,768]{2,1,0:T(4,128)(2,1)}), bf16[16,4,768]{2,1,0:T(4,128)(2,1)S(1)}, u32[]{:S(2)}, u32[]{:S(2)}) async-start(bf16[16,4,768]{2,1,0:T(4,128)(2,1)} %bitcast.16), calls=%async_computation | async-start | bytes 196608 | tf_op jit(solution)/shard_map/all_to_all | solution.py:335
  12.7 2.7 %collective-permute-start = (bf16[80,512]{1,0:T(8,128)(2,1)S(1)}, bf16[80,512]{1,0:T(8,128)(2,1)S(1)}, u32[]{:S(2)}, u32[]{:S(2)}) collective-permute-start(bf16[80,512]{1,0:T(8,128)(2,1)S(1)} %pack.1.refs_0_), channel_id=1, source_target_pairs={{0,136},{8,128},{128,8},{136,0},{1,137},{9,129},{129,9},{137,1},{2... | collective-permute-start | bytes 245768 | tf_op jit(solution)/shard_map/ppermute | solution.py:277
  15.4 3.2 %collective-permute-done.refs_1_ = bf16[80,512]{1,0:T(8,128)(2,1)S(1)} collective-permute-done((bf16[80,512]{1,0:T(8,128)(2,1)S(1)}, bf16[80,512]{1,0:T(8,128)(2,1)S(1)}, u32[]{:S(2)}, u32[]{:S(2)}) %collective-permute-start) | collective-permute-done | bytes 81952 | tf_op jit(solution)/shard_map/ppermute | solution.py:277
  18.6 1.3 %collective-permute-done.2.refs_3_ = bf16[80,512]{1,0:T(8,128)(2,1)S(1)} collective-permute-done((bf16[80,512]{1,0:T(8,128)(2,1)S(1)}, bf16[80,512]{1,0:T(8,128)(2,1)S(1)}, u32[]{:S(2)}, u32[]{:S(2)}) %collective-permute-start.2) | collective-permute-done | bytes 81952 | tf_op jit(solution)/shard_map/ppermute | solution.py:269
  19.9 2.0 %all-to-all-done = bf16[16,4,768]{2,1,0:T(4,128)(2,1)S(1)} async-done(((bf16[16,4,768]{2,1,0:T(4,128)(2,1)}), bf16[16,4,768]{2,1,0:T(4,128)(2,1)S(1)}, u32[]{:S(2)}, u32[]{:S(2)}) %all-to-all-start) | async-done | bytes 98336 | tf_op jit(solution)/shard_map/all_to_all | solution.py:335
  21.9 0.8 collective-permute-start.3
  22.7 2.5 %collective-permute-start.6 = (bf16[288,512]{1,0:T(8,128)(2,1)S(1)}, bf16[288,512]{1,0:T(8,128)(2,1)S(1)}, u32[]{:S(2)}, u32[]{:S(2)}) collective-permute-start(bf16[288,512]{1,0:T(8,128)(2,1)S(1)} %merge.1.refs_0_), channel_id=1, source_target_pairs={{0,1},{1,2},{2,3},{3,4},{4,5},{5,6},{6,7},{7,0},{16,23},{17,16},{1... | collective-permute-start | bytes 884744 | tf_op jit(solution)/shard_map/ppermute | solution.py:274
  25.3 0.9 %broadcast_in_dim.8 = bf16[8,64,768]{2,1,0:T(8,128)(2,1)} broadcast(bf16[64,768]{1,0:T(8,128)(2,1)S(1)} %broadcast_in_dim.7), dimensions={1,2} | broadcast | bytes 884736 | tf_op jit(solution)/shard_map/broadcast_in_dim | solution.py:346
  26.2 4.5 %all-to-all-start.1 = ((bf16[8,64,768]{2,1,0:T(8,128)(2,1)}), bf16[8,64,768]{2,1,0:T(8,128)(2,1)S(1)}, u32[]{:S(2)}, u32[]{:S(2)}) async-start(bf16[8,64,768]{2,1,0:T(8,128)(2,1)} %broadcast_in_dim.8), calls=%async_computation.1 | async-start | bytes 1572864 | tf_op jit(solution)/shard_map/all_to_all | solution.py:347
  30.7 1.5 %thresholds.1.refs_7_.refs_6_ = f32[8,2048]{1,0:T(8,128)S(1)} custom-call(s32[8,128]{1,0:T(8,128)S(1)} %copy-done.4, s32[128]{0:T(128)S(1)} %copy-done.5), custom_call_target="tpu_custom_call" | custom-call | flops 49999998976 | bytes 100000 | tf_op jit(solution)/shard_map/thresholds/pallas_call | solution.py:319
  32.5 1.2 %pad_maximum_fusion.refs_6_.refs_5_ = bf16[4,512,256]{2,1,0:T(8,128)(2,1)S(1)} fusion(bf16[4,512,128]{2,1,0:T(8,128)(2,1)} %param.11, bf16[4,512,128]{2,1,0:T(8,128)(2,1)S(1)} %bitcast.14), kind=kLoop, calls=%fused_computation | loop fusion | flops 2097152 | bytes 2097152 | tf_op jit(solution)/shard_map/concatenate | solution.py:341
  33.8 1.5 %collective-permute-done.6.refs_1_ = bf16[288,512]{1,0:T(8,128)(2,1)S(1)} collective-permute-done((bf16[288,512]{1,0:T(8,128)(2,1)S(1)}, bf16[288,512]{1,0:T(8,128)(2,1)S(1)}, u32[]{:S(2)}, u32[]{:S(2)}) %collective-permute-start.6) | collective-permute-done | bytes 294944 | tf_op jit(solution)/shard_map/ppermute | solution.py:274
  35.8 0.7 halve.1
  36.5 3.7 %collective-permute-start.5 = (bf16[144,512]{1,0:T(8,128)(2,1)}, bf16[144,512]{1,0:T(8,128)(2,1)S(1)}, u32[]{:S(2)}, u32[]{:S(2)}) collective-permute-start(bf16[144,512]{1,0:T(8,128)(2,1)} %halve.1), channel_id=1, source_target_pairs={{0,2},{1,3},{2,4},{3,5},{4,6},{5,7},{6,0},{7,1},{16,22},{17,23},{1... | collective-permute-start | bytes 442376 | tf_op jit(solution)/shard_map/ppermute | solution.py:274
  40.2 0.7 copy-done
  40.9 0.9 all-to-all-done.1
  41.7 1.0 %copy-done.1 = bf16[288,512]{1,0:T(8,128)(2,1)S(1)} copy-done((bf16[288,512]{1,0:T(8,128)(2,1)S(1)}, bf16[288,512]{1,0:T(8,128)(2,1)}, u32[]{:S(2)}) %copy-start.1) | copy-done | bytes 294936
  42.7 5.6 %attend_early.1 = (f32[512,512]{1,0:T(8,128)S(1)}, f32[512,128]{1,0:T(8,128)S(1)}) custom-call(bf16[288,512]{1,0:T(8,128)(2,1)S(1)} %merge.1.refs_0_, bf16[288,512]{1,0:T(8,128)(2,1)S(1)} %collective-permute-done.6.refs_1_, bf16[288,512]{1,0:T(8,128)(2,1)S(1)} %copy-done.1, bf16[288,512]{1,0:T(8,128)(2,1)S(1)} %collective-permute-done.3.x_ref.refs_3_, ...), custom_call_target="tpu_custom_call" | custom-call | flops 5000000 | bytes 5000 | tf_op jit(solution)/shard_map/attend_early/pallas_call | solution.py:177
  49.0 1.3 %collective-permute-done.10.refs_3_ = bf16[144,512]{1,0:T(8,128)(2,1)S(1)} collective-permute-done((bf16[144,512]{1,0:T(8,128)(2,1)S(1)}, bf16[144,512]{1,0:T(8,128)(2,1)S(1)}, u32[]{:S(2)}, u32[]{:S(2)}) %collective-permute-start.10) | collective-permute-done | bytes 147488 | tf_op jit(solution)/shard_map/ppermute | solution.py:269
  50.2 4.9 %attend_late.1 = bf16[512,640]{1,0:T(8,128)(2,1)S(1)} custom-call(bf16[288,512]{1,0:T(8,128)(2,1)S(1)} %collective-permute-done.4.refs_0_, bf16[288,512]{1,0:T(8,128)(2,1)S(1)} %collective-permute-done.9.refs_1_, bf16[144,512]{1,0:T(8,128)(2,1)S(1)} %collective-permute-done.5.refs_2_, bf16[144,512]{1,0:T(8,128)(2,1)S(1)} %collective-permute-done.10.refs_3_, ...), custom_call_target="tpu_custom_call" | custom-call | flops 3000000 | bytes 3000 | tf_op jit(solution)/shard_map/attend_late/pallas_call | solution.py:177
  55.1 15.9 %all_to_all.20 = bf16[8,64,640]{2,1,0:T(8,128)(2,1)S(1)} all-to-all(bf16[8,64,640]{2,1,0:T(8,128)(2,1)S(1)} %bitcast.12), channel_id=1, replica_groups=mesh['xl'=2,'y'=4,'core'=2,'xh'=2,'z'=8] {'xl','y'}, dimensions={0} | all-to-all | bytes 1310720 | tf_op jit(solution)/shard_map/all_to_all | solution.py:354
  71.6 15.9 %all_to_all.21 = bf16[16,4,512]{2,1,0:T(4,128)(2,1)S(1)} all-to-all(bf16[16,4,512]{2,1,0:T(4,128)(2,1)S(1)} %combine.1), channel_id=1, replica_groups=mesh['xl'=2,'y'=4,'core'=2,'xh'=2,'z'=8] {'xh','z'}, dimensions={0} | all-to-all | bytes 131072 | tf_op jit(solution)/shard_map/all_to_all | solution.py:357
  (30 shorter events, 2.8 us)
Async XLA Ops:
  0.0 0.8 copy-start.2
  0.8 0.7 copy-start.3
  1.6 20.3 %all-to-all-start = ((bf16[16,4,768]{2,1,0:T(4,128)(2,1)}), bf16[16,4,768]{2,1,0:T(4,128)(2,1)S(1)}, u32[]{:S(2)}, u32[]{:S(2)}) async-start(bf16[16,4,768]{2,1,0:T(4,128)(2,1)} %bitcast.16), calls=%async_computation | async-start | bytes 196608 | tf_op jit(solution)/shard_map/all_to_all | solution.py:335
  12.7 5.9 %collective-permute-start = (bf16[80,512]{1,0:T(8,128)(2,1)S(1)}, bf16[80,512]{1,0:T(8,128)(2,1)S(1)}, u32[]{:S(2)}, u32[]{:S(2)}) collective-permute-start(bf16[80,512]{1,0:T(8,128)(2,1)S(1)} %pack.1.refs_0_), channel_id=1, source_target_pairs={{0,136},{8,128},{128,8},{136,0},{1,137},{9,129},{129,9},{137,1},{2... | collective-permute-start | bytes 245768 | tf_op jit(solution)/shard_map/ppermute | solution.py:277
  15.4 3.2 %collective-permute-start.1 = (bf16[80,512]{1,0:T(8,128)(2,1)S(1)}, bf16[80,512]{1,0:T(8,128)(2,1)S(1)}, u32[]{:S(2)}, u32[]{:S(2)}) collective-permute-start(bf16[80,512]{1,0:T(8,128)(2,1)S(1)} %pack.1.refs_0_), channel_id=1, source_target_pairs={{0,16},{16,0},{1,17},{17,1},{2,18},{18,2},{3,19},{19,3},{4,20},{20... | collective-permute-start | bytes 245768 | tf_op jit(solution)/shard_map/ppermute | solution.py:269
  18.6 1.3 %collective-permute-start.2 = (bf16[80,512]{1,0:T(8,128)(2,1)S(1)}, bf16[80,512]{1,0:T(8,128)(2,1)S(1)}, u32[]{:S(2)}, u32[]{:S(2)}) collective-permute-start(bf16[80,512]{1,0:T(8,128)(2,1)S(1)} %collective-permute-done.refs_1_), channel_id=1, source_target_pairs={{0,16},{16,0},{1,17},{17,1},{2,18},{18,2},{3,19},{19,3},{4,20},{20... | collective-permute-start | bytes 245768 | tf_op jit(solution)/shard_map/ppermute | solution.py:269
  21.9 11.8 %collective-permute-start.3 = (bf16[288,512]{1,0:T(8,128)(2,1)S(1)}, bf16[288,512]{1,0:T(8,128)(2,1)S(1)}, u32[]{:S(2)}, u32[]{:S(2)}) collective-permute-start(bf16[288,512]{1,0:T(8,128)(2,1)S(1)} %merge.1.refs_0_), channel_id=1, source_target_pairs={{0,2},{1,3},{2,4},{3,5},{4,6},{5,7},{6,0},{7,1},{16,22},{17,23},{1... | collective-permute-start | bytes 884744 | tf_op jit(solution)/shard_map/ppermute | solution.py:274
  22.7 12.6 %collective-permute-start.6 = (bf16[288,512]{1,0:T(8,128)(2,1)S(1)}, bf16[288,512]{1,0:T(8,128)(2,1)S(1)}, u32[]{:S(2)}, u32[]{:S(2)}) collective-permute-start(bf16[288,512]{1,0:T(8,128)(2,1)S(1)} %merge.1.refs_0_), channel_id=1, source_target_pairs={{0,1},{1,2},{2,3},{3,4},{4,5},{5,6},{6,7},{7,0},{16,23},{17,16},{1... | collective-permute-start | bytes 884744 | tf_op jit(solution)/shard_map/ppermute | solution.py:274
  25.2 5.4 %copy-start.4 = (s32[8,128]{1,0:T(8,128)S(1)}, s32[8,128]{1,0:T(8,128)}, u32[]{:S(2)}) copy-start(s32[8,128]{1,0:T(8,128)} %pattern_ref) | copy-start | bytes 12292
  25.3 5.4 %copy-start.5 = (s32[128]{0:T(128)S(1)}, s32[128]{0:T(128)}, u32[]{:S(2)}) copy-start(s32[128]{0:T(128)} %stripe_ref) | copy-start | bytes 1540
  26.2 15.5 %all-to-all-start.1 = ((bf16[8,64,768]{2,1,0:T(8,128)(2,1)}), bf16[8,64,768]{2,1,0:T(8,128)(2,1)S(1)}, u32[]{:S(2)}, u32[]{:S(2)}) async-start(bf16[8,64,768]{2,1,0:T(8,128)(2,1)} %broadcast_in_dim.8), calls=%async_computation.1 | async-start | bytes 1572864 | tf_op jit(solution)/shard_map/all_to_all | solution.py:347
  30.7 1.6 %copy-start.6 = (bf16[4,128,512]{2,1,0:T(8,128)(2,1)S(1)}, bf16[4,128,512]{2,1,0:T(8,128)(2,1)}, u32[]{:S(2)}) copy-start(bf16[4,128,512]{2,1,0:T(8,128)(2,1)} %param.10) | copy-start | bytes 1572868
  33.7 6.4 %collective-permute-start.8 = (bf16[288,512]{1,0:T(8,128)(2,1)S(1)}, bf16[288,512]{1,0:T(8,128)(2,1)S(1)}, u32[]{:S(2)}, u32[]{:S(2)}) collective-permute-start(bf16[288,512]{1,0:T(8,128)(2,1)S(1)} %collective-permute-done.3.x_ref.refs_3_), channel_id=1, source_target_pairs={{0,16},{16,0},{1,17},{17,1},{2,18},{18,2},{3,19},{19,3},{4,20},{20... | collective-permute-start | bytes 884744 | tf_op jit(solution)/shard_map/ppermute | solution.py:269
  35.3 4.9 %collective-permute-start.7 = (bf16[288,512]{1,0:T(8,128)(2,1)S(1)}, bf16[288,512]{1,0:T(8,128)(2,1)S(1)}, u32[]{:S(2)}, u32[]{:S(2)}) collective-permute-start(bf16[288,512]{1,0:T(8,128)(2,1)S(1)} %collective-permute-done.6.refs_1_), channel_id=1, source_target_pairs={{0,16},{16,0},{1,17},{17,1},{2,18},{18,2},{3,19},{19,3},{4,20},{20... | collective-permute-start | bytes 884744 | tf_op jit(solution)/shard_map/ppermute | solution.py:269
  35.3 13.1 %collective-permute-start.4 = (bf16[288,512]{1,0:T(8,128)(2,1)S(1)}, bf16[288,512]{1,0:T(8,128)(2,1)S(1)}, u32[]{:S(2)}, u32[]{:S(2)}) collective-permute-start(bf16[288,512]{1,0:T(8,128)(2,1)S(1)} %collective-permute-done.3.x_ref.refs_3_), channel_id=1, source_target_pairs={{0,1},{1,2},{2,3},{3,4},{4,5},{5,6},{6,7},{7,0},{16,23},{17,16},{1... | collective-permute-start | bytes 884744 | tf_op jit(solution)/shard_map/ppermute | solution.py:274
  36.5 11.9 %collective-permute-start.5 = (bf16[144,512]{1,0:T(8,128)(2,1)}, bf16[144,512]{1,0:T(8,128)(2,1)S(1)}, u32[]{:S(2)}, u32[]{:S(2)}) collective-permute-start(bf16[144,512]{1,0:T(8,128)(2,1)} %halve.1), channel_id=1, source_target_pairs={{0,2},{1,3},{2,4},{3,5},{4,6},{5,7},{6,0},{7,1},{16,22},{17,23},{1... | collective-permute-start | bytes 442376 | tf_op jit(solution)/shard_map/ppermute | solution.py:274
  40.2 0.7 copy-start
  41.7 1.0 %copy-start.1 = (bf16[288,512]{1,0:T(8,128)(2,1)S(1)}, bf16[288,512]{1,0:T(8,128)(2,1)}, u32[]{:S(2)}) copy-start(bf16[288,512]{1,0:T(8,128)(2,1)} %copy-done) | copy-start | bytes 884740
  48.4 1.9 %collective-permute-start.9 = (bf16[288,512]{1,0:T(8,128)(2,1)S(1)}, bf16[288,512]{1,0:T(8,128)(2,1)S(1)}, u32[]{:S(2)}, u32[]{:S(2)}) collective-permute-start(bf16[288,512]{1,0:T(8,128)(2,1)S(1)} %collective-permute-done.4.refs_0_), channel_id=1, source_target_pairs={{0,16},{16,0},{1,17},{17,1},{2,18},{18,2},{3,19},{19,3},{4,20},{20... | collective-permute-start | bytes 884744 | tf_op jit(solution)/shard_map/ppermute | solution.py:269
  48.5 1.8 %collective-permute-start.10 = (bf16[144,512]{1,0:T(8,128)(2,1)S(1)}, bf16[144,512]{1,0:T(8,128)(2,1)S(1)}, u32[]{:S(2)}, u32[]{:S(2)}) collective-permute-start(bf16[144,512]{1,0:T(8,128)(2,1)S(1)} %collective-permute-done.5.refs_2_), channel_id=1, source_target_pairs={{0,16},{16,0},{1,17},{17,1},{2,18},{18,2},{3,19},{19,3},{4,20},{20... | collective-permute-start | bytes 442376 | tf_op jit(solution)/shard_map/ppermute | solution.py:269

commit v10 on v9

--- a/solution.py
+++ b/solution.py
@@ -275,7 +275,7 @@
 
     piece = pack(latents, key_rope)
     beside, mate = lax.ppermute(piece, ("xl", "xh"), near), to_core(piece)
-    mine = swap(piece)
+    mine = swap()
     pieces = [piece, beside, mate, to_core(beside)]
     pieces, mine = lax.optimization_barrier((pieces, mine))
     now = merge(pieces)
@@ -329,9 +329,8 @@
 def body(queries, latents, key_rope, key_up, value_up, pattern, stripe):
     cells = ("xl", "y")
     groups = ("xh", "z")
-    def swap(after):
+    def swap():
         send = queries.reshape(TOK, GRP, HEADS * QD).transpose(1, 0, 2)
-        send, _ = lax.optimization_barrier((send, after))
         return lax.all_to_all(send, groups, split_axis=0, concat_axis=0, tiled=True)
 
     def prepare(after):

time: 88.6 us -> 88.6 us (level)
  waiting for transfers between devices: 10.1 us -> 7.65 us
  starting transfers between devices: 26.4 us -> 28.7 us
    ppermute x4, starting transfers between devices: 7.49 us -> 9.71 us  [round_z(): return lax.ppermute(x, ('core', 'z'), up + down)]
    all_to_all x1, waiting for transfers between devices: 2.02 us -> 0.36 us  [swap(): return lax.all_to_all(send, groups, split_axis=0, concat_axis=0, tiled=True)]
    all_to_all x1, blocking collectives: 15.9 us -> 17 us  [body(): lax.all_to_all(combine(back.reshape(ROWS, EXT)), groups, split_axis=0, co...]
    ppermute x4, waiting for transfers between devices: 1.46 us -> 0.5 us  [round_z(): return lax.ppermute(x, ('core', 'z'), up + down)]
where the time goes in v10:
time: 88.6 us; the launch traced here: 88.2 us
  blocking collectives  32.1 us (36%)
  starting transfers between devices  28.7 us (32%)
  Pallas kernels  13.3 us (15%)
  waiting for transfers between devices  7.65 us (9%)
  local copies, waits for them, and re-layouts  5.13 us (6%)
  other arithmetic  1.17 us (1%)
    all_to_all x1, blocking collectives, body(): lax.all_to_all(combine(back.reshape(ROWS, EXT)), groups, split_axis=0, co...  17 us
    all_to_all x1, blocking collectives, body(): lax.all_to_all(part.reshape(CELLS, GRP * TOK, EXT), cells, split_axis=0,...  15.1 us
    all_to_all x1, starting transfers between devices, swap(): return lax.all_to_all(send, groups, split_axis=0, concat_axis=0, tiled=True)  11 us
    pallas_call x2, Pallas kernels, attend(): pl.pallas_call(functools.partial(attend_kernel, count, first), out_shape=...  10.5 us
    ppermute x4, starting transfers between devices, round_z(): return lax.ppermute(x, ('core', 'z'), up + down)  9.71 us
    all_to_all x1, starting transfers between devices, body(): q = lax.all_to_all(send, cells, split_axis=0, concat_axis=0, tiled=True)  4.47 us
    unnamed x15, local copies, waits for them, and re-layouts  3.89 us
    ppermute x1, waiting for transfers between devices, gather_keys(): beside, mate = (lax.ppermute(piece, ('xl', 'xh'), near), to_core(piece))  3.21 us
  transfers between devices with their start and end apart: 13, of which 6 were waited for; matrix products, arithmetic and copies ran while one was open for 3% of the time, Pallas kernels for 9%

profile of v10, /device:TPU:32, one launch (start us, length us, event | category | flops | bytes accessed | tf_op | source)
XLA Modules:
  0.0 88.2 jit_solution(8515972608938855136)
XLA Ops:
  0.0 11.0 %all-to-all-start = ((bf16[16,4,768]{2,1,0:T(4,128)(2,1)}), bf16[16,4,768]{2,1,0:T(4,128)(2,1)S(1)}, u32[]{:S(2)}, u32[]{:S(2)}) async-start(bf16[16,4,768]{2,1,0:T(4,128)(2,1)} %bitcast.16), calls=%async_computation | async-start | bytes 196608 | tf_op jit(solution)/shard_map/all_to_all | solution.py:334
  11.1 0.8 copy-done.2
  11.9 0.7 copy-done.3
  12.7 2.7 %collective-permute-start = (bf16[80,512]{1,0:T(8,128)(2,1)S(1)}, bf16[80,512]{1,0:T(8,128)(2,1)S(1)}, u32[]{:S(2)}, u32[]{:S(2)}) collective-permute-start(bf16[80,512]{1,0:T(8,128)(2,1)S(1)} %pack.1.refs_0_), channel_id=1, source_target_pairs={{0,136},{8,128},{128,8},{136,0},{1,137},{9,129},{129,9},{137,1},{2... | collective-permute-start | bytes 245768 | tf_op jit(solution)/shard_map/ppermute | solution.py:277
  15.4 3.2 %collective-permute-done.refs_1_ = bf16[80,512]{1,0:T(8,128)(2,1)S(1)} collective-permute-done((bf16[80,512]{1,0:T(8,128)(2,1)S(1)}, bf16[80,512]{1,0:T(8,128)(2,1)S(1)}, u32[]{:S(2)}, u32[]{:S(2)}) %collective-permute-start) | collective-permute-done | bytes 81952 | tf_op jit(solution)/shard_map/ppermute | solution.py:277
  18.6 1.3 %collective-permute-done.2.refs_3_ = bf16[80,512]{1,0:T(8,128)(2,1)S(1)} collective-permute-done((bf16[80,512]{1,0:T(8,128)(2,1)S(1)}, bf16[80,512]{1,0:T(8,128)(2,1)S(1)}, u32[]{:S(2)}, u32[]{:S(2)}) %collective-permute-start.2) | collective-permute-done | bytes 81952 | tf_op jit(solution)/shard_map/ppermute | solution.py:269
  20.3 2.1 %collective-permute-start.3 = (bf16[288,512]{1,0:T(8,128)(2,1)S(1)}, bf16[288,512]{1,0:T(8,128)(2,1)S(1)}, u32[]{:S(2)}, u32[]{:S(2)}) collective-permute-start(bf16[288,512]{1,0:T(8,128)(2,1)S(1)} %merge.1.refs_0_), channel_id=1, source_target_pairs={{0,2},{1,3},{2,4},{3,5},{4,6},{5,7},{6,0},{7,1},{16,22},{17,23},{1... | collective-permute-start | bytes 884744 | tf_op jit(solution)/shard_map/ppermute | solution.py:274
  22.4 2.4 %collective-permute-start.6 = (bf16[288,512]{1,0:T(8,128)(2,1)S(1)}, bf16[288,512]{1,0:T(8,128)(2,1)S(1)}, u32[]{:S(2)}, u32[]{:S(2)}) collective-permute-start(bf16[288,512]{1,0:T(8,128)(2,1)S(1)} %merge.1.refs_0_), channel_id=1, source_target_pairs={{0,1},{1,2},{2,3},{3,4},{4,5},{5,6},{6,7},{7,0},{16,23},{17,16},{1... | collective-permute-start | bytes 884744 | tf_op jit(solution)/shard_map/ppermute | solution.py:274
  24.8 0.9 %broadcast_in_dim.8 = bf16[8,64,768]{2,1,0:T(8,128)(2,1)} broadcast(bf16[64,768]{1,0:T(8,128)(2,1)S(1)} %broadcast_in_dim.7), dimensions={1,2} | broadcast | bytes 884736 | tf_op jit(solution)/shard_map/broadcast_in_dim | solution.py:345
  25.8 4.5 %all-to-all-start.1 = ((bf16[8,64,768]{2,1,0:T(8,128)(2,1)}), bf16[8,64,768]{2,1,0:T(8,128)(2,1)S(1)}, u32[]{:S(2)}, u32[]{:S(2)}) async-start(bf16[8,64,768]{2,1,0:T(8,128)(2,1)} %broadcast_in_dim.8), calls=%async_computation.1 | async-start | bytes 1572864 | tf_op jit(solution)/shard_map/all_to_all | solution.py:346
  30.3 1.5 %thresholds.1.refs_7_.refs_6_ = f32[8,2048]{1,0:T(8,128)S(1)} custom-call(s32[8,128]{1,0:T(8,128)S(1)} %copy-done.4, s32[128]{0:T(128)S(1)} %copy-done.5), custom_call_target="tpu_custom_call" | custom-call | flops 49999998976 | bytes 100000 | tf_op jit(solution)/shard_map/thresholds/pallas_call | solution.py:319
  32.1 1.2 %pad_maximum_fusion.refs_6_.refs_5_ = bf16[4,512,256]{2,1,0:T(8,128)(2,1)S(1)} fusion(bf16[4,512,128]{2,1,0:T(8,128)(2,1)} %param.11, bf16[4,512,128]{2,1,0:T(8,128)(2,1)S(1)} %bitcast.14), kind=kLoop, calls=%fused_computation | loop fusion | flops 2097152 | bytes 2097152 | tf_op jit(solution)/shard_map/concatenate | solution.py:340
  33.9 1.4 %collective-permute-start.4 = (bf16[288,512]{1,0:T(8,128)(2,1)S(1)}, bf16[288,512]{1,0:T(8,128)(2,1)S(1)}, u32[]{:S(2)}, u32[]{:S(2)}) collective-permute-start(bf16[288,512]{1,0:T(8,128)(2,1)S(1)} %collective-permute-done.3.x_ref.refs_3_), channel_id=1, source_target_pairs={{0,1},{1,2},{2,3},{3,4},{4,5},{5,6},{6,7},{7,0},{16,23},{17,16},{1... | collective-permute-start | bytes 884744 | tf_op jit(solution)/shard_map/ppermute | solution.py:274
  35.3 0.7 halve.1
  36.0 3.8 %collective-permute-start.5 = (bf16[144,512]{1,0:T(8,128)(2,1)}, bf16[144,512]{1,0:T(8,128)(2,1)S(1)}, u32[]{:S(2)}, u32[]{:S(2)}) collective-permute-start(bf16[144,512]{1,0:T(8,128)(2,1)} %halve.1), channel_id=1, source_target_pairs={{0,2},{1,3},{2,4},{3,5},{4,6},{5,7},{6,0},{7,1},{16,22},{17,23},{1... | collective-permute-start | bytes 442376 | tf_op jit(solution)/shard_map/ppermute | solution.py:274
  39.8 0.7 copy-done
  40.5 1.0 %all-to-all-done.1 = bf16[8,64,768]{2,1,0:T(8,128)(2,1)S(1)} async-done(((bf16[8,64,768]{2,1,0:T(8,128)(2,1)}), bf16[8,64,768]{2,1,0:T(8,128)(2,1)S(1)}, u32[]{:S(2)}, u32[]{:S(2)}) %all-to-all-start.1) | async-done | bytes 786464 | tf_op jit(solution)/shard_map/all_to_all | solution.py:346
  41.5 1.0 %copy-done.1 = bf16[288,512]{1,0:T(8,128)(2,1)S(1)} copy-done((bf16[288,512]{1,0:T(8,128)(2,1)S(1)}, bf16[288,512]{1,0:T(8,128)(2,1)}, u32[]{:S(2)}) %copy-start.1) | copy-done | bytes 294936
  42.5 5.6 %attend_early.1 = (f32[512,512]{1,0:T(8,128)S(1)}, f32[512,128]{1,0:T(8,128)S(1)}) custom-call(bf16[288,512]{1,0:T(8,128)(2,1)S(1)} %merge.1.refs_0_, bf16[288,512]{1,0:T(8,128)(2,1)S(1)} %collective-permute-done.6.refs_1_, bf16[288,512]{1,0:T(8,128)(2,1)S(1)} %copy-done.1, bf16[288,512]{1,0:T(8,128)(2,1)S(1)} %collective-permute-done.3.x_ref.refs_3_, ...), custom_call_target="tpu_custom_call" | custom-call | flops 5000000 | bytes 5000 | tf_op jit(solution)/shard_map/attend_early/pallas_call | solution.py:177
  48.7 1.3 %collective-permute-done.10.refs_3_ = bf16[144,512]{1,0:T(8,128)(2,1)S(1)} collective-permute-done((bf16[144,512]{1,0:T(8,128)(2,1)S(1)}, bf16[144,512]{1,0:T(8,128)(2,1)S(1)}, u32[]{:S(2)}, u32[]{:S(2)}) %collective-permute-start.10) | collective-permute-done | bytes 147488 | tf_op jit(solution)/shard_map/ppermute | solution.py:269
  50.0 4.9 %attend_late.1 = bf16[512,640]{1,0:T(8,128)(2,1)S(1)} custom-call(bf16[288,512]{1,0:T(8,128)(2,1)S(1)} %collective-permute-done.4.refs_0_, bf16[288,512]{1,0:T(8,128)(2,1)S(1)} %collective-permute-done.9.refs_1_, bf16[144,512]{1,0:T(8,128)(2,1)S(1)} %collective-permute-done.5.refs_2_, bf16[144,512]{1,0:T(8,128)(2,1)S(1)} %collective-permute-done.10.refs_3_, ...), custom_call_target="tpu_custom_call" | custom-call | flops 3000000 | bytes 3000 | tf_op jit(solution)/shard_map/attend_late/pallas_call | solution.py:177
  54.9 15.1 %all_to_all.20 = bf16[8,64,640]{2,1,0:T(8,128)(2,1)S(1)} all-to-all(bf16[8,64,640]{2,1,0:T(8,128)(2,1)S(1)} %bitcast.12), channel_id=1, replica_groups=mesh['xl'=2,'y'=4,'core'=2,'xh'=2,'z'=8] {'xl','y'}, dimensions={0} | all-to-all | bytes 1310720 | tf_op jit(solution)/shard_map/all_to_all | solution.py:353
  70.5 17.0 %all_to_all.21 = bf16[16,4,512]{2,1,0:T(4,128)(2,1)S(1)} all-to-all(bf16[16,4,512]{2,1,0:T(4,128)(2,1)S(1)} %combine.1), channel_id=1, replica_groups=mesh['xl'=2,'y'=4,'core'=2,'xh'=2,'z'=8] {'xh','z'}, dimensions={0} | all-to-all | bytes 131072 | tf_op jit(solution)/shard_map/all_to_all | solution.py:356
  87.5 0.6 copy.12
  (30 shorter events, 2.5 us)
Async XLA Ops:
  0.0 20.3 %all-to-all-start = ((bf16[16,4,768]{2,1,0:T(4,128)(2,1)}), bf16[16,4,768]{2,1,0:T(4,128)(2,1)S(1)}, u32[]{:S(2)}, u32[]{:S(2)}) async-start(bf16[16,4,768]{2,1,0:T(4,128)(2,1)} %bitcast.16), calls=%async_computation | async-start | bytes 196608 | tf_op jit(solution)/shard_map/all_to_all | solution.py:334
  11.0 0.8 copy-start.2
  11.9 0.7 copy-start.3
  12.7 5.9 %collective-permute-start = (bf16[80,512]{1,0:T(8,128)(2,1)S(1)}, bf16[80,512]{1,0:T(8,128)(2,1)S(1)}, u32[]{:S(2)}, u32[]{:S(2)}) collective-permute-start(bf16[80,512]{1,0:T(8,128)(2,1)S(1)} %pack.1.refs_0_), channel_id=1, source_target_pairs={{0,136},{8,128},{128,8},{136,0},{1,137},{9,129},{129,9},{137,1},{2... | collective-permute-start | bytes 245768 | tf_op jit(solution)/shard_map/ppermute | solution.py:277
  15.4 3.2 %collective-permute-start.1 = (bf16[80,512]{1,0:T(8,128)(2,1)S(1)}, bf16[80,512]{1,0:T(8,128)(2,1)S(1)}, u32[]{:S(2)}, u32[]{:S(2)}) collective-permute-start(bf16[80,512]{1,0:T(8,128)(2,1)S(1)} %pack.1.refs_0_), channel_id=1, source_target_pairs={{0,16},{16,0},{1,17},{17,1},{2,18},{18,2},{3,19},{19,3},{4,20},{20... | collective-permute-start | bytes 245768 | tf_op jit(solution)/shard_map/ppermute | solution.py:269
  18.6 1.3 %collective-permute-start.2 = (bf16[80,512]{1,0:T(8,128)(2,1)S(1)}, bf16[80,512]{1,0:T(8,128)(2,1)S(1)}, u32[]{:S(2)}, u32[]{:S(2)}) collective-permute-start(bf16[80,512]{1,0:T(8,128)(2,1)S(1)} %collective-permute-done.refs_1_), channel_id=1, source_target_pairs={{0,16},{16,0},{1,17},{17,1},{2,18},{18,2},{3,19},{19,3},{4,20},{20... | collective-permute-start | bytes 245768 | tf_op jit(solution)/shard_map/ppermute | solution.py:269
  20.3 13.0 %collective-permute-start.3 = (bf16[288,512]{1,0:T(8,128)(2,1)S(1)}, bf16[288,512]{1,0:T(8,128)(2,1)S(1)}, u32[]{:S(2)}, u32[]{:S(2)}) collective-permute-start(bf16[288,512]{1,0:T(8,128)(2,1)S(1)} %merge.1.refs_0_), channel_id=1, source_target_pairs={{0,2},{1,3},{2,4},{3,5},{4,6},{5,7},{6,0},{7,1},{16,22},{17,23},{1... | collective-permute-start | bytes 884744 | tf_op jit(solution)/shard_map/ppermute | solution.py:274
  22.4 11.5 %collective-permute-start.6 = (bf16[288,512]{1,0:T(8,128)(2,1)S(1)}, bf16[288,512]{1,0:T(8,128)(2,1)S(1)}, u32[]{:S(2)}, u32[]{:S(2)}) collective-permute-start(bf16[288,512]{1,0:T(8,128)(2,1)S(1)} %merge.1.refs_0_), channel_id=1, source_target_pairs={{0,1},{1,2},{2,3},{3,4},{4,5},{5,6},{6,7},{7,0},{16,23},{17,16},{1... | collective-permute-start | bytes 884744 | tf_op jit(solution)/shard_map/ppermute | solution.py:274
  24.8 5.4 %copy-start.4 = (s32[8,128]{1,0:T(8,128)S(1)}, s32[8,128]{1,0:T(8,128)}, u32[]{:S(2)}) copy-start(s32[8,128]{1,0:T(8,128)} %pattern_ref) | copy-start | bytes 12292
  24.8 5.4 %copy-start.5 = (s32[128]{0:T(128)S(1)}, s32[128]{0:T(128)}, u32[]{:S(2)}) copy-start(s32[128]{0:T(128)} %stripe_ref) | copy-start | bytes 1540
  25.8 15.8 %all-to-all-start.1 = ((bf16[8,64,768]{2,1,0:T(8,128)(2,1)}), bf16[8,64,768]{2,1,0:T(8,128)(2,1)S(1)}, u32[]{:S(2)}, u32[]{:S(2)}) async-start(bf16[8,64,768]{2,1,0:T(8,128)(2,1)} %broadcast_in_dim.8), calls=%async_computation.1 | async-start | bytes 1572864 | tf_op jit(solution)/shard_map/all_to_all | solution.py:346
  30.3 1.6 %copy-start.6 = (bf16[4,128,512]{2,1,0:T(8,128)(2,1)S(1)}, bf16[4,128,512]{2,1,0:T(8,128)(2,1)}, u32[]{:S(2)}) copy-start(bf16[4,128,512]{2,1,0:T(8,128)(2,1)} %param.10) | copy-start | bytes 1572868
  33.3 6.5 %collective-permute-start.8 = (bf16[288,512]{1,0:T(8,128)(2,1)S(1)}, bf16[288,512]{1,0:T(8,128)(2,1)S(1)}, u32[]{:S(2)}, u32[]{:S(2)}) collective-permute-start(bf16[288,512]{1,0:T(8,128)(2,1)S(1)} %collective-permute-done.3.x_ref.refs_3_), channel_id=1, source_target_pairs={{0,16},{16,0},{1,17},{17,1},{2,18},{18,2},{3,19},{19,3},{4,20},{20... | collective-permute-start | bytes 884744 | tf_op jit(solution)/shard_map/ppermute | solution.py:269
  33.9 5.9 %collective-permute-start.7 = (bf16[288,512]{1,0:T(8,128)(2,1)S(1)}, bf16[288,512]{1,0:T(8,128)(2,1)S(1)}, u32[]{:S(2)}, u32[]{:S(2)}) collective-permute-start(bf16[288,512]{1,0:T(8,128)(2,1)S(1)} %collective-permute-done.6.refs_1_), channel_id=1, source_target_pairs={{0,16},{16,0},{1,17},{17,1},{2,18},{18,2},{3,19},{19,3},{4,20},{20... | collective-permute-start | bytes 884744 | tf_op jit(solution)/shard_map/ppermute | solution.py:269
  33.9 14.3 %collective-permute-start.4 = (bf16[288,512]{1,0:T(8,128)(2,1)S(1)}, bf16[288,512]{1,0:T(8,128)(2,1)S(1)}, u32[]{:S(2)}, u32[]{:S(2)}) collective-permute-start(bf16[288,512]{1,0:T(8,128)(2,1)S(1)} %collective-permute-done.3.x_ref.refs_3_), channel_id=1, source_target_pairs={{0,1},{1,2},{2,3},{3,4},{4,5},{5,6},{6,7},{7,0},{16,23},{17,16},{1... | collective-permute-start | bytes 884744 | tf_op jit(solution)/shard_map/ppermute | solution.py:274
  36.0 12.1 %collective-permute-start.5 = (bf16[144,512]{1,0:T(8,128)(2,1)}, bf16[144,512]{1,0:T(8,128)(2,1)S(1)}, u32[]{:S(2)}, u32[]{:S(2)}) collective-permute-start(bf16[144,512]{1,0:T(8,128)(2,1)} %halve.1), channel_id=1, source_target_pairs={{0,2},{1,3},{2,4},{3,5},{4,6},{5,7},{6,0},{7,1},{16,22},{17,23},{1... | collective-permute-start | bytes 442376 | tf_op jit(solution)/shard_map/ppermute | solution.py:274
  39.8 0.7 copy-start
  41.5 1.0 %copy-start.1 = (bf16[288,512]{1,0:T(8,128)(2,1)S(1)}, bf16[288,512]{1,0:T(8,128)(2,1)}, u32[]{:S(2)}) copy-start(bf16[288,512]{1,0:T(8,128)(2,1)} %copy-done) | copy-start | bytes 884740
  48.2 1.9 %collective-permute-start.9 = (bf16[288,512]{1,0:T(8,128)(2,1)S(1)}, bf16[288,512]{1,0:T(8,128)(2,1)S(1)}, u32[]{:S(2)}, u32[]{:S(2)}) collective-permute-start(bf16[288,512]{1,0:T(8,128)(2,1)S(1)} %collective-permute-done.4.refs_0_), channel_id=1, source_target_pairs={{0,16},{16,0},{1,17},{17,1},{2,18},{18,2},{3,19},{19,3},{4,20},{20... | collective-permute-start | bytes 884744 | tf_op jit(solution)/shard_map/ppermute | solution.py:269
  48.3 1.8 %collective-permute-start.10 = (bf16[144,512]{1,0:T(8,128)(2,1)S(1)}, bf16[144,512]{1,0:T(8,128)(2,1)S(1)}, u32[]{:S(2)}, u32[]{:S(2)}) collective-permute-start(bf16[144,512]{1,0:T(8,128)(2,1)S(1)} %collective-permute-done.5.refs_2_), channel_id=1, source_target_pairs={{0,16},{16,0},{1,17},{17,1},{2,18},{18,2},{3,19},{19,3},{4,20},{20... | collective-permute-start | bytes 442376 | tf_op jit(solution)/shard_map/ppermute | solution.py:269
